TPU v7x, 128 devices: a whole 4x4x4 slice. The times are simulated.
128 devices in a mesh: patch: 64 (over z_lo, y, x, core), frame: 2 (over z_hi).
Axes of the slice: x: 4, y: 4, z: 4 (z_hi: 2, z_lo: 2; z = z_hi * 2 + z_lo), core: 2. Of those that a mesh axis runs over, the one named last changes fastest.
Arguments:
- basis: bfloat16 [3, 16384, 1024], P(None, 'patch'), may hold values from -0.5 to 0.5
- latents: bfloat16 [1024, 1024], P('frame', 'patch'), may hold values from -2 to 2
- rest_pos: float32 [3, 16384], P(None, 'patch'), may hold values from -3 to 3
- triangles: int32 [3, 32768], P(None, 'patch'), may hold values from 0 to 511
- hinges: int32 [4, 24576], P(None, 'patch'), may hold values from 0 to 511
- rest_sq: float32 [3, 32768], P(None, 'patch'), may hold values from 0.5 to 3
- bend_rest: float32 [3, 24576], P(None, 'patch'), may hold values from -5 to 5
- masses: float32 [16384], P('patch'), may hold values from 0.5 to 2
- send_rows: int32 [2, 8192], P(None, 'patch'), may hold values from 0 to 255, as said below
Outputs:
- basis_grad: float32 [3, 16384, 1024], P(None, ('patch', 'frame'))
- latent_grad: float32 [1024, 1024], P('frame', 'patch')
Inputs may be any that keep to these rules, and one draw needn't show every extreme that they name: `send_rows`: within one patch's columns the 256 entries of both rows are distinct own vertex numbers.
All inputs are finite; a program needn't handle non-finite values.
Results may differ from a plain program's by a relative error of at most 0.006.
Values may be sent and summed in bfloat16 or wider, within the bound.
No kernel may reach another device: no remote copies, remote signals or barrier semaphores. Data moves between devices by JAX's collectives and lax.ppermute only.
A program may use at most 64 MiB of HBM per device.

v0:
```python
import functools

import jax
import jax.numpy as jnp
from jax import lax
from jax.experimental import pallas as pl
from jax.experimental.pallas import tpu as pltpu
from jax.sharding import PartitionSpec as P

MEMBRANE = 5.0
BENDING = 5.0
GRAVITY = 40.0
BF = jnp.bfloat16
F32 = jnp.float32
NN = (((1,), (0,)), ((), ()))
TN = (((0,), (0,)), ((), ()))
NT = (((1,), (1,)), ((), ()))
PARAMS = pltpu.CompilerParams(vmem_limit_bytes=48 * 1024 * 1024)


def dot(a, b, dims=NN):
    return lax.dot_general(a, b, dims, preferred_element_type=F32)


def exact_dot(a, b):
    total = None
    for _ in range(3):
        part = b.astype(BF)
        b = b - part.astype(F32)
        term = dot(a, part)
        total = term if total is None else total + term
    return total


def one_hot(rows, ids):
    return (lax.broadcasted_iota(jnp.int32, (rows, ids.shape[1]), 0) == ids).astype(F32)


def pick_kernel(send_ref, basis_ref, prev_ref, next_ref):
    own, halo = basis_ref.shape[1], send_ref.shape[1]
    for row, out in ((0, prev_ref), (1, next_ref)):
        sel = one_hot(own, send_ref[row : row + 1, :]).astype(BF)
        for c in range(3):
            out[c * halo : (c + 1) * halo, :] = dot(sel, basis_ref[c], TN).astype(BF)


def incidence_kernel(tri_ref, hin_ref, d_ref, dt_ref):
    ext = dt_ref.shape[0]
    t = tri_ref.shape[1]
    a, b, c = (one_hot(ext, tri_ref[i : i + 1, :]) for i in range(3))
    for at, part in ((0, b - a), (t, c - b)):
        dt_ref[:, at : at + t] = part.astype(BF)
        d_ref[at : at + t, :] = part.T.astype(BF)
    a, b, c, d = (one_hot(ext, hin_ref[i : i + 1, :]) for i in range(4))
    part = c + d - a - b
    dt_ref[:, 2 * t :] = part.astype(BF)
    d_ref[2 * t :, :] = part.T.astype(BF)


def elastic_kernel(
    frames, own_n, halo,
    lat_ref, own_ref, prv_ref, nxt_ref, d_ref, dt_ref, off_ref, sq_ref, grav_ref,
    f_own_ref, f_prv_ref, f_nxt_ref, lg_ref,
):
    t = sq_ref.shape[1]
    lat = lat_ref[...]
    x_own = dot(own_ref[...], lat).astype(BF)
    x_prv = dot(prv_ref[...], lat).astype(BF)
    x_nxt = dot(nxt_ref[...], lat).astype(BF)
    d = d_ref[...]
    edges = []
    for c in range(3):
        x = jnp.concatenate(
            [
                x_own[c * own_n : (c + 1) * own_n],
                x_prv[c * halo : (c + 1) * halo],
                x_nxt[c * halo : (c + 1) * halo],
            ],
            axis=0,
        )
        edges.append(dot(d, x) + off_ref[c])
    e1 = [e[:t] for e in edges]
    e2 = [e[t : 2 * t] for e in edges]
    q1 = e1[0] * e1[0] + e1[1] * e1[1] + e1[2] * e1[2]
    q2 = e2[0] * e2[0] + e2[1] * e2[1] + e2[2] * e2[2]
    e3 = [u + v for u, v in zip(e1, e2)]
    q3 = e3[0] * e3[0] + e3[1] * e3[1] + e3[2] * e3[2]
    scale = 4.0 * MEMBRANE / frames
    s1, s2, s3 = (scale * (q - sq_ref[i]) for i, q in enumerate((q1, q2, q3)))
    dt = dt_ref[...]
    for c in range(3):
        third = s3 * e3[c]
        g = jnp.concatenate(
            [
                (s1 * e1[c] + third).astype(BF),
                (s2 * e2[c] + third).astype(BF),
                (edges[c][2 * t :] * (2.0 * BENDING / frames)).astype(BF),
            ],
            axis=0,
        )
        f = dot(dt, g)
        f_own = f[:own_n]
        if c == 2:
            f_own = f_own + grav_ref[...]
        f_own_ref[c * own_n : (c + 1) * own_n, :] = f_own
        f_prv_ref[c * halo : (c + 1) * halo, :] = f[own_n : own_n + halo].astype(BF)
        f_nxt_ref[c * halo : (c + 1) * halo, :] = f[own_n + halo :].astype(BF)
    lg = dot(own_ref[...], f_own_ref[...].astype(BF), TN)
    lg = lg + dot(prv_ref[...], f_prv_ref[...], TN)
    lg = lg + dot(nxt_ref[...], f_nxt_ref[...], TN)
    lg_ref[...] = lg.astype(BF)


def adjoint_kernel(send_ref, f_own_ref, back_prv_ref, back_nxt_ref, adj_ref):
    halo = send_ref.shape[1]
    own = f_own_ref.shape[0] // 3
    half = own // 2
    to_prev = one_hot(own, send_ref[0:1, :]).astype(BF)
    to_next = one_hot(own, send_ref[1:2, :]).astype(BF)
    for c in range(3):
        rows = slice(c * halo, (c + 1) * halo)
        total = f_own_ref[c * own : (c + 1) * own, :]
        total = total + dot(to_prev, back_prv_ref[rows, :]) + dot(to_next, back_nxt_ref[rows, :])
        total = total.astype(BF)
        for h in range(2):
            adj_ref[h, c * half : (c + 1) * half, :] = total[h * half : (h + 1) * half]


def basis_grad_kernel(mine_ref, other_ref, lat_mine_ref, lat_other_ref, out_ref):
    one = dot(mine_ref[...], lat_mine_ref[...], NT).astype(BF).astype(F32)
    two = dot(other_ref[...], lat_other_ref[...], NT).astype(BF).astype(F32)
    out_ref[...] = one + two


def call(kernel, outs, *args):
    return pl.pallas_call(
        kernel,
        out_shape=[jax.ShapeDtypeStruct(s, d) for s, d in outs],
        compiler_params=PARAMS,
    )(*args)


def local(basis, latents, rest_pos, triangles, hinges, rest_sq, bend_rest, masses, send_rows):
    own = basis.shape[1]
    width = basis.shape[2]
    frames = latents.shape[0]
    each = latents.shape[1]
    halo = send_rows.shape[1]
    tris = triangles.shape[1]
    hings = hinges.shape[1]
    ext = own + 2 * halo
    patches = lax.axis_size("patch")
    total_frames = frames * lax.axis_size("frame")
    chips = patches // 2
    onward = [(i, (i + 1) % patches) for i in range(patches)]
    backward = [((i + 1) % patches, i) for i in range(patches)]
    sibling = [(i, i ^ 1) for i in range(patches)]
    partner = [(0, 1), (1, 0)]
    same_core = [[2 * i + c for i in range(chips)] for c in range(2)]
    core = lax.axis_index("patch") % 2
    half_index = lax.axis_index("frame")

    def exchange(tiles):
        return lax.all_to_all(tiles, "patch", 0, 0, tiled=True, axis_index_groups=same_core)

    def interleaved(mine, other):
        both = jnp.where(
            core == 0, jnp.stack([mine, other], axis=1), jnp.stack([other, mine], axis=1)
        )
        return both.reshape(width, frames)

    shard = latents.T
    lat_core = exchange(jnp.broadcast_to(shard[None], (chips, each, frames)))
    rows_prev, rows_next = call(
        pick_kernel, [((3 * halo, width), BF)] * 2, send_rows, basis
    )
    halo_prv = lax.ppermute(rows_next, "patch", onward)
    halo_nxt = lax.ppermute(rows_prev, "patch", backward)
    d, dt = call(
        incidence_kernel,
        [((2 * tris + hings, ext), BF), ((ext, 2 * tris + hings), BF)],
        triangles,
        hinges,
    )
    sel = send_rows[:, :, None] == lax.broadcasted_iota(jnp.int32, (2, halo, own), 2)
    sent_rest = jnp.sum(jnp.where(sel[:, None], rest_pos[None, :, None, :], 0.0), axis=3)
    rest_prv = lax.ppermute(sent_rest[1], "patch", onward)
    rest_nxt = lax.ppermute(sent_rest[0], "patch", backward)
    rest_ext = jnp.concatenate([rest_pos, rest_prv, rest_nxt], axis=1)

    def offsets_kernel(d_ref, rest_ref, bend_ref, off_ref):
        off_ref[...] = exact_dot(d_ref[...], rest_ref[...]) - bend_ref[...]

    rest_cols = jnp.pad(rest_ext.T, ((0, 0), (0, 125)))
    bend_cols = jnp.pad(bend_rest.T, ((2 * tris, 0), (0, 125)))
    [offs] = call(offsets_kernel, [((2 * tris + hings, 128), F32)], d, rest_cols, bend_cols)
    offsets = offs[:, :3].T[:, :, None]
    sq_cols = rest_sq[:, :, None]
    gravity = (masses * (GRAVITY / total_frames))[:, None]

    lat_sib = lax.ppermute(lat_core, "patch", sibling)
    lat_all = interleaved(lat_core, lat_sib)

    step = min(frames, 256)
    full = lambda shape: pl.BlockSpec(shape, lambda i: (0,) * len(shape))
    cols = lambda rows: pl.BlockSpec((rows, step), lambda i: (0, i))
    f_own, f_prv, f_nxt, lg = pl.pallas_call(
        functools.partial(elastic_kernel, total_frames, own, halo),
        grid=(frames // step,),
        in_specs=[
            cols(width),
            full((3 * own, width)),
            full((3 * halo, width)),
            full((3 * halo, width)),
            full((2 * tris + hings, ext)),
            full((ext, 2 * tris + hings)),
            full((3, 2 * tris + hings, 1)),
            full((3, tris, 1)),
            full((own, 1)),
        ],
        out_specs=[cols(3 * own), cols(3 * halo), cols(3 * halo), cols(width)],
        out_shape=[
            jax.ShapeDtypeStruct((3 * own, frames), F32),
            jax.ShapeDtypeStruct((3 * halo, frames), BF),
            jax.ShapeDtypeStruct((3 * halo, frames), BF),
            jax.ShapeDtypeStruct((width, frames), BF),
        ],
        compiler_params=PARAMS,
    )(lat_all, basis.reshape(3 * own, width), halo_prv, halo_nxt, d, dt, offsets, sq_cols, gravity)

    back_nxt = lax.ppermute(f_prv, "patch", backward)
    back_prv = lax.ppermute(f_nxt, "patch", onward)

    lg = lg.reshape(chips, 2, each, frames)
    keep = jnp.where(core == 0, lg[:, 0], lg[:, 1])
    give = jnp.where(core == 0, lg[:, 1], lg[:, 0])
    got = lax.ppermute(give, "patch", sibling)
    pair = (keep.astype(F32) + got.astype(F32)).astype(BF)
    shares = exchange(pair)
    latent_grad = jnp.sum(shares.astype(F32), axis=0).T

    far_core = lax.ppermute(lat_core, "frame", partner)
    far_sib = lax.ppermute(far_core, "patch", sibling)
    lat_far = interleaved(far_core, far_sib)

    half = own // 2
    [adj] = call(
        adjoint_kernel, [((2, 3 * half, frames), BF)], send_rows, f_own, back_prv, back_nxt
    )
    mine = jnp.where(half_index == 0, adj[0], adj[1])
    other = jnp.where(half_index == 0, adj[1], adj[0])
    received = lax.ppermute(other, "frame", partner)
    [basis_grad] = call(
        basis_grad_kernel, [((3 * half, width), F32)], mine, received, lat_all, lat_far
    )
    return basis_grad.reshape(3, half, width), latent_grad


def solution(mesh):
    return jax.shard_map(
        local,
        mesh=mesh,
        in_specs=(
            P(None, "patch", None),
            P("frame", "patch"),
            P(None, "patch"),
            P(None, "patch"),
            P(None, "patch"),
            P(None, "patch"),
            P(None, "patch"),
            P("patch"),
            P(None, "patch"),
        ),
        out_specs=(P(None, ("patch", "frame"), None), P("frame", "patch")),
        check_vma=False,
    )
```

profile of v0, /device:TPU:1, one launch (start us, length us, event | category | flops | bytes accessed | tf_op | source)
XLA Modules:
  0.0 108.0 jit_solution(12087206274467395293)
XLA Ops:
  0.7 1.7 %broadcast_in_dim.38 = bf16[32,16,512]{2,1,0:T(8,128)(2,1)} broadcast(bf16[16,512]{1,0:T(8,128)(2,1)} %bitcast.58), dimensions={1,2} | broadcast | bytes 540672 | tf_op jit(solution)/shard_map/broadcast_in_dim | solution.py:173
  2.4 9.5 %all-to-all-start = ((bf16[32,16,512]{2,1,0:T(8,128)(2,1)}), bf16[32,16,512]{2,1,0:T(8,128)(2,1)}, u32[]{:S(2)}, u32[]{:S(2)}) async-start(bf16[32,16,512]{2,1,0:T(8,128)(2,1)} %broadcast_in_dim.38), calls=%async_computation | async-start | bytes 1048576 | tf_op jit(solution)/shard_map/all_to_all | solution.py:164
  12.2 2.3 %collective-permute-start.3 = (f32[3,128]{1,0:T(4,128)S(1)}, f32[3,128]{1,0:T(4,128)S(1)}, u32[]{:S(2)}, u32[]{:S(2)}) collective-permute-start(f32[3,128]{1,0:T(4,128)S(1)} %get-tuple-element.20), channel_id=1, source_target_pairs={{0,2},{2,4},{4,6},{6,8},{8,10},{10,12},{12,14},{14,16},{16,18},{18... | collective-permute-start | bytes 4616 | tf_op jit(solution)/shard_map/ppermute | solution.py:187
  14.6 1.6 %shard_map.104 = (bf16[384,1024]{1,0:T(8,128)(2,1)}, bf16[384,1024]{1,0:T(8,128)(2,1)}) custom-call(s32[2,128]{1,0:T(2,128)S(1)} %copy-done.6, bf16[3,256,1024]{2,1,0:T(8,128)(2,1)S(1)} %copy-done), custom_call_target="tpu_custom_call" | custom-call | tf_op jit(solution)/shard_map/pallas_call | solution.py:136
  16.2 1.7 %collective-permute-start.1 = (bf16[384,1024]{1,0:T(8,128)(2,1)}, bf16[384,1024]{1,0:T(8,128)(2,1)}, u32[]{:S(2)}, u32[]{:S(2)}) collective-permute-start(bf16[384,1024]{1,0:T(8,128)(2,1)} %get-tuple-element.10), channel_id=1, source_target_pairs={{0,2},{2,4},{4,6},{6,8},{8,10},{10,12},{12,14},{14,16},{16,18},{18... | collective-permute-start | bytes 2359304 | tf_op jit(solution)/shard_map/ppermute | solution.py:177
  17.9 2.9 %collective-permute-start.2 = (bf16[384,1024]{1,0:T(8,128)(2,1)}, bf16[384,1024]{1,0:T(8,128)(2,1)}, u32[]{:S(2)}, u32[]{:S(2)}) collective-permute-start(bf16[384,1024]{1,0:T(8,128)(2,1)} %get-tuple-element.11), channel_id=1, source_target_pairs={{2,0},{4,2},{6,4},{8,6},{10,8},{12,10},{14,12},{16,14},{18,16},{20... | collective-permute-start | bytes 2359304 | tf_op jit(solution)/shard_map/ppermute | solution.py:178
  21.4 1.0 shard_map.105
  22.5 1.1 %copy-done.3 = bf16[512,1408]{1,0:T(8,128)(2,1)} copy-done((bf16[512,1408]{1,0:T(8,128)(2,1)}, bf16[512,1408]{1,0:T(8,128)(2,1)S(1)}, u32[]{:S(2)}) %copy-start.3) | copy-done | bytes 1441816
  23.6 6.0 %collective-permute-start = (bf16[32,16,512]{2,1,0:T(8,128)(2,1)}, bf16[32,16,512]{2,1,0:T(8,128)(2,1)}, u32[]{:S(2)}, u32[]{:S(2)}) collective-permute-start(bf16[32,16,512]{2,1,0:T(8,128)(2,1)} %all-to-all-done), channel_id=1, source_target_pairs={{0,2},{2,0},{4,6},{6,4},{8,10},{10,8},{12,14},{14,12},{16,18},{18,... | collective-permute-start | bytes 1572872 | tf_op jit(solution)/shard_map/ppermute | solution.py:201
  29.7 0.9 copy.45
  30.6 1.0 pad.8.rest_ref
  31.5 1.3 %shard_map.106 = f32[1408,128]{1,0:T(8,128)S(1)} custom-call(bf16[1408,512]{1,0:T(8,128)(2,1)S(1)} %get-tuple-element.12.d_ref, f32[512,128]{1,0:T(8,128)S(1)} %pad.8.rest_ref, f32[1408,128]{1,0:T(8,128)S(1)} %pad.9.bend_ref), custom_call_target="tpu_custom_call" | custom-call | tf_op jit(solution)/shard_map/pallas_call | solution.py:136
  32.9 10.5 %copy.48.off_ref = f32[3,1408,1]{2,1,0:T(8,128)} copy(f32[3,1408,1]{0,1,2:T(8,128)S(1)} %slice_bitcast_fusion) | data formatting | bytes 33792 | tf_op jit(solution)/shard_map/broadcast_in_dim | solution.py:197
  43.4 3.3 %collective-permute-start.8 = (bf16[32,16,512]{2,1,0:T(8,128)(2,1)}, bf16[32,16,512]{2,1,0:T(8,128)(2,1)}, u32[]{:S(2)}, u32[]{:S(2)}) collective-permute-start(bf16[32,16,512]{2,1,0:T(8,128)(2,1)} %all-to-all-done), channel_id=1, source_target_pairs={{0,1},{1,0},{2,3},{3,2},{4,5},{5,4},{6,7},{7,6},{8,9},{9,8},{10,11... | collective-permute-start | bytes 1572872 | tf_op jit(solution)/shard_map/ppermute | solution.py:242
  46.7 1.7 %maximum_select_fusion = bf16[32,2,16,512]{3,2,0,1:T(8,128)(2,1)S(1)} fusion(bf16[32,1,16,512]{3,2,0,1:T(8,128)(2,1)} %bitcast.2, bf16[32,1,16,512]{3,2,0,1:T(8,128)(2,1)} %bitcast.1, pred[]{:T(512)S(6)} %eq.25), kind=kLoop, calls=%fused_computation | loop fusion | flops 1572864 | bytes 2097153 | tf_op jit(solution)/shard_map/jit(_where)/select_n | solution.py:167
  48.5 16.2 %shard_map.107 = (f32[768,512]{1,0:T(8,128)}, bf16[384,512]{1,0:T(8,128)(2,1)}, bf16[384,512]{1,0:T(8,128)(2,1)}, bf16[1024,512]{1,0:T(8,128)(2,1)S(1)}) custom-call(bf16[1024,512]{1,0:T(8,128)(2,1)S(1)} %bitcast.48, bf16[768,1024]{1,0:T(8,128)(2,1)} %bitcast.50, bf16[384,1024]{1,0:T(8,128)(2,1)} %collective-permute-done.1.prv_ref, ...), custom_call_target="tpu_custom_call" | custom-call | tf_op jit(solution)/shard_map/pallas_call | solution.py:207
  64.8 0.9 fusion.1
  65.6 0.5 collective-permute-start.10
  66.1 0.5 collective-permute-start.6
  66.6 5.5 %collective-permute-start.9 = (bf16[32,16,512]{2,1,0:T(8,128)(2,1)}, bf16[32,16,512]{2,1,0:T(8,128)(2,1)}, u32[]{:S(2)}, u32[]{:S(2)}) collective-permute-start(bf16[32,16,512]{2,1,0:T(8,128)(2,1)} %collective-permute-done.8), channel_id=1, source_target_pairs={{0,2},{2,0},{4,6},{6,4},{8,10},{10,8},{12,14},{14,12},{16,18},{18,... | collective-permute-start | bytes 1572872 | tf_op jit(solution)/shard_map/ppermute | solution.py:243
  72.1 1.7 %collective-permute-done.6.back_nxt_ref = bf16[384,512]{1,0:T(8,128)(2,1)S(1)} collective-permute-done((bf16[384,512]{1,0:T(8,128)(2,1)}, bf16[384,512]{1,0:T(8,128)(2,1)S(1)}, u32[]{:S(2)}, u32[]{:S(2)}) %collective-permute-start.6) | collective-permute-done | bytes 393248 | tf_op jit(solution)/shard_map/ppermute | solution.py:231
  73.8 0.8 copy-done.4
  74.6 1.4 %copy-done.2 = f32[768,512]{1,0:T(8,128)S(1)} copy-done((f32[768,512]{1,0:T(8,128)S(1)}, f32[768,512]{1,0:T(8,128)}, u32[]{:S(2)}) %copy-start.2) | copy-done | bytes 1572888
  76.0 1.0 copy-done.5
  77.0 0.5 shard_map.108
  77.6 2.1 %fusion = bf16[32,16,512]{2,1,0:T(8,128)(2,1)} fusion(bf16[32,16,512]{2,1,0:T(8,128)(2,1)} %collective-permute-done.10, pred[]{:T(512)S(6)} %eq.25, bf16[32,2,16,512]{3,2,1,0:T(8,128)(2,1)S(1)} %bitcast.53), kind=kLoop, calls=%fused_computation.3 | loop fusion | flops 1310720 | bytes 2097153 | tf_op jit(solution)/shard_map/convert_element_type | solution.py:238
  79.7 11.2 %all-to-all-start.1 = ((bf16[32,16,512]{2,1,0:T(8,128)(2,1)}), bf16[32,16,512]{2,1,0:T(8,128)(2,1)S(1)}, u32[]{:S(2)}, u32[]{:S(2)}) async-start(bf16[32,16,512]{2,1,0:T(8,128)(2,1)} %fusion), calls=%async_computation.1 | async-start | bytes 1048576 | tf_op jit(solution)/shard_map/all_to_all | solution.py:164
  91.0 0.6 collective-permute-start.7
  91.6 1.7 %maximum_select_fusion.1 = bf16[32,2,16,512]{3,2,1,0:T(8,128)(2,1)S(1)} fusion(bf16[32,1,16,512]{3,2,1,0:T(8,128)(2,1)} %bitcast.16, bf16[32,1,16,512]{3,2,1,0:T(8,128)(2,1)} %bitcast.15, pred[]{:T(512)S(6)} %eq.25), kind=kLoop, calls=%fused_computation.1 | loop fusion | flops 1572864 | bytes 2097153 | tf_op jit(solution)/shard_map/jit(_where)/select_n | solution.py:167
  93.3 11.8 %collective-permute-done.7.other_ref = bf16[384,512]{1,0:T(8,128)(2,1)S(1)} collective-permute-done((bf16[384,512]{1,0:T(8,128)(2,1)S(1)}, bf16[384,512]{1,0:T(8,128)(2,1)S(1)}, u32[]{:S(2)}, u32[]{:S(2)}) %collective-permute-start.7) | collective-permute-done | bytes 393248 | tf_op jit(solution)/shard_map/ppermute | solution.py:252
  105.1 2.2 %shard_map.109 = f32[384,1024]{1,0:T(8,128)} custom-call(bf16[384,512]{1,0:T(8,128)(2,1)S(1)} %get-tuple-element.19.mine_ref, bf16[384,512]{1,0:T(8,128)(2,1)S(1)} %collective-permute-done.7.other_ref, bf16[1024,512]{1,0:T(8,128)(2,1)S(1)} %bitcast.49, bf16[1024,512]{1,0:T(8,128)(2,1)S(1)} %bitcast.51), custom_call_target="tpu_custom_call" | custom-call | tf_op jit(solution)/shard_map/pallas_call | solution.py:136
  107.3 0.7 convert_reduce_fusion
  (47 shorter events, 1.2 us)
Async XLA Ops:
  0.6 11.3 %copy-start.6 = (s32[2,128]{1,0:T(2,128)S(1)}, s32[2,128]{1,0:T(2,128)}, u32[]{:S(2)}) copy-start(s32[2,128]{1,0:T(2,128)} %send_ref.3) | copy-start | bytes 3076
  0.6 11.4 %copy-start.9 = (f32[3,256]{1,0:T(4,128)S(1)}, f32[3,256]{1,0:T(4,128)}, u32[]{:S(2)}) copy-start(f32[3,256]{1,0:T(4,128)} %param.11) | copy-start | bytes 9220
  0.7 13.9 %copy-start = (bf16[3,256,1024]{2,1,0:T(8,128)(2,1)S(1)}, bf16[3,256,1024]{2,1,0:T(8,128)(2,1)}, u32[]{:S(2)}) copy-start(bf16[3,256,1024]{2,1,0:T(8,128)(2,1)} %basis_ref.1) | copy-start | bytes 4718596
  0.7 20.2 %copy-start.12 = (f32[256]{0:T(256)S(1)}, f32[256]{0:T(256)}, u32[]{:S(2)}) copy-start(f32[256]{0:T(256)} %param.16) | copy-start | bytes 3076
  0.7 20.2 %copy-start.11 = (f32[3,384]{1,0:T(4,128)S(1)}, f32[3,384]{1,0:T(4,128)}, u32[]{:S(2)}) copy-start(f32[3,384]{1,0:T(4,128)} %param.15) | copy-start | bytes 13828
  2.4 18.6 %copy-start.10 = (f32[3,512]{1,0:T(4,128)S(1)}, f32[3,512]{1,0:T(4,128)}, u32[]{:S(2)}) copy-start(f32[3,512]{1,0:T(4,128)} %param.14) | copy-start | bytes 18436
  2.4 21.2 %all-to-all-start = ((bf16[32,16,512]{2,1,0:T(8,128)(2,1)}), bf16[32,16,512]{2,1,0:T(8,128)(2,1)}, u32[]{:S(2)}, u32[]{:S(2)}) async-start(bf16[32,16,512]{2,1,0:T(8,128)(2,1)} %broadcast_in_dim.38), calls=%async_computation | async-start | bytes 1048576 | tf_op jit(solution)/shard_map/all_to_all | solution.py:164
  11.9 9.5 %copy-start.7 = (s32[3,512]{1,0:T(4,128)S(1)}, s32[3,512]{1,0:T(4,128)}, u32[]{:S(2)}) copy-start(s32[3,512]{1,0:T(4,128)} %tri_ref.1) | copy-start | bytes 18436
  11.9 9.5 %copy-start.8 = (s32[4,384]{1,0:T(4,128)S(1)}, s32[4,384]{1,0:T(4,128)}, u32[]{:S(2)}) copy-start(s32[4,384]{1,0:T(4,128)} %hin_ref.1) | copy-start | bytes 18436
  12.2 17.5 %collective-permute-start.3 = (f32[3,128]{1,0:T(4,128)S(1)}, f32[3,128]{1,0:T(4,128)S(1)}, u32[]{:S(2)}, u32[]{:S(2)}) collective-permute-start(f32[3,128]{1,0:T(4,128)S(1)} %get-tuple-element.20), channel_id=1, source_target_pairs={{0,2},{2,4},{4,6},{6,8},{8,10},{10,12},{12,14},{14,16},{16,18},{18... | collective-permute-start | bytes 4616 | tf_op jit(solution)/shard_map/ppermute | solution.py:187
  14.6 15.1 %collective-permute-start.4 = (f32[3,128]{1,0:T(4,128)S(1)}, f32[3,128]{1,0:T(4,128)S(1)}, u32[]{:S(2)}, u32[]{:S(2)}) collective-permute-start(f32[3,128]{1,0:T(4,128)S(1)} %get-tuple-element.21), channel_id=1, source_target_pairs={{2,0},{4,2},{6,4},{8,6},{10,8},{12,10},{14,12},{16,14},{18,16},{20... | collective-permute-start | bytes 4616 | tf_op jit(solution)/shard_map/ppermute | solution.py:188
  16.2 32.4 %collective-permute-start.1 = (bf16[384,1024]{1,0:T(8,128)(2,1)}, bf16[384,1024]{1,0:T(8,128)(2,1)}, u32[]{:S(2)}, u32[]{:S(2)}) collective-permute-start(bf16[384,1024]{1,0:T(8,128)(2,1)} %get-tuple-element.10), channel_id=1, source_target_pairs={{0,2},{2,4},{4,6},{6,8},{8,10},{10,12},{12,14},{14,16},{16,18},{18... | collective-permute-start | bytes 2359304 | tf_op jit(solution)/shard_map/ppermute | solution.py:177
  17.9 30.6 %collective-permute-start.2 = (bf16[384,1024]{1,0:T(8,128)(2,1)}, bf16[384,1024]{1,0:T(8,128)(2,1)}, u32[]{:S(2)}, u32[]{:S(2)}) collective-permute-start(bf16[384,1024]{1,0:T(8,128)(2,1)} %get-tuple-element.11), channel_id=1, source_target_pairs={{2,0},{4,2},{6,4},{8,6},{10,8},{12,10},{14,12},{16,14},{18,16},{20... | collective-permute-start | bytes 2359304 | tf_op jit(solution)/shard_map/ppermute | solution.py:178
  22.5 1.1 %copy-start.3 = (bf16[512,1408]{1,0:T(8,128)(2,1)}, bf16[512,1408]{1,0:T(8,128)(2,1)S(1)}, u32[]{:S(2)}) copy-start(bf16[512,1408]{1,0:T(8,128)(2,1)S(1)} %get-tuple-element.13.dt_ref) | copy-start | bytes 4325380
  23.6 9.2 %copy-start.1 = (bf16[1408,512]{1,0:T(8,128)(2,1)}, bf16[1408,512]{1,0:T(8,128)(2,1)S(1)}, u32[]{:S(2)}) copy-start(bf16[1408,512]{1,0:T(8,128)(2,1)S(1)} %get-tuple-element.12.d_ref) | copy-start | bytes 4325380
  23.6 23.1 %collective-permute-start = (bf16[32,16,512]{2,1,0:T(8,128)(2,1)}, bf16[32,16,512]{2,1,0:T(8,128)(2,1)}, u32[]{:S(2)}, u32[]{:S(2)}) collective-permute-start(bf16[32,16,512]{2,1,0:T(8,128)(2,1)} %all-to-all-done), channel_id=1, source_target_pairs={{0,2},{2,0},{4,6},{6,4},{8,10},{10,8},{12,14},{14,12},{16,18},{18,... | collective-permute-start | bytes 1572872 | tf_op jit(solution)/shard_map/ppermute | solution.py:201
  43.4 23.2 %collective-permute-start.8 = (bf16[32,16,512]{2,1,0:T(8,128)(2,1)}, bf16[32,16,512]{2,1,0:T(8,128)(2,1)}, u32[]{:S(2)}, u32[]{:S(2)}) collective-permute-start(bf16[32,16,512]{2,1,0:T(8,128)(2,1)} %all-to-all-done), channel_id=1, source_target_pairs={{0,1},{1,0},{2,3},{3,2},{4,5},{5,4},{6,7},{7,6},{8,9},{9,8},{10,11... | collective-permute-start | bytes 1572872 | tf_op jit(solution)/shard_map/ppermute | solution.py:242
  65.6 11.9 %collective-permute-start.10 = (bf16[32,16,512]{2,1,0:T(8,128)(2,1)}, bf16[32,16,512]{2,1,0:T(8,128)(2,1)}, u32[]{:S(2)}, u32[]{:S(2)}) collective-permute-start(bf16[32,16,512]{2,1,0:T(8,128)(2,1)} %fusion.1), channel_id=1, source_target_pairs={{0,2},{2,0},{4,6},{6,4},{8,10},{10,8},{12,14},{14,12},{16,18},{18,... | collective-permute-start | bytes 1572872 | tf_op jit(solution)/shard_map/ppermute | solution.py:237
  66.1 6.0 %collective-permute-start.5 = (bf16[384,512]{1,0:T(8,128)(2,1)}, bf16[384,512]{1,0:T(8,128)(2,1)S(1)}, u32[]{:S(2)}, u32[]{:S(2)}) collective-permute-start(bf16[384,512]{1,0:T(8,128)(2,1)} %get-tuple-element.15), channel_id=1, source_target_pairs={{0,2},{2,4},{4,6},{6,8},{8,10},{10,12},{12,14},{14,16},{16,18},{18... | collective-permute-start | bytes 1179656 | tf_op jit(solution)/shard_map/ppermute | solution.py:232
  66.1 7.7 %collective-permute-start.6 = (bf16[384,512]{1,0:T(8,128)(2,1)}, bf16[384,512]{1,0:T(8,128)(2,1)S(1)}, u32[]{:S(2)}, u32[]{:S(2)}) collective-permute-start(bf16[384,512]{1,0:T(8,128)(2,1)} %get-tuple-element.16), channel_id=1, source_target_pairs={{2,0},{4,2},{6,4},{8,6},{10,8},{12,10},{14,12},{16,14},{18,16},{20... | collective-permute-start | bytes 1179656 | tf_op jit(solution)/shard_map/ppermute | solution.py:231
  66.6 25.0 %collective-permute-start.9 = (bf16[32,16,512]{2,1,0:T(8,128)(2,1)}, bf16[32,16,512]{2,1,0:T(8,128)(2,1)}, u32[]{:S(2)}, u32[]{:S(2)}) collective-permute-start(bf16[32,16,512]{2,1,0:T(8,128)(2,1)} %collective-permute-done.8), channel_id=1, source_target_pairs={{0,2},{2,0},{4,6},{6,4},{8,10},{10,8},{12,14},{14,12},{16,18},{18,... | collective-permute-start | bytes 1572872 | tf_op jit(solution)/shard_map/ppermute | solution.py:243
  73.8 0.8 copy-start.4
  74.6 1.4 %copy-start.2 = (f32[768,512]{1,0:T(8,128)S(1)}, f32[768,512]{1,0:T(8,128)}, u32[]{:S(2)}) copy-start(f32[768,512]{1,0:T(8,128)} %get-tuple-element.14.f_own_ref) | copy-start | bytes 4718596
  76.0 1.0 copy-start.5
  79.7 27.6 %all-to-all-start.1 = ((bf16[32,16,512]{2,1,0:T(8,128)(2,1)}), bf16[32,16,512]{2,1,0:T(8,128)(2,1)S(1)}, u32[]{:S(2)}, u32[]{:S(2)}) async-start(bf16[32,16,512]{2,1,0:T(8,128)(2,1)} %fusion), calls=%async_computation.1 | async-start | bytes 1048576 | tf_op jit(solution)/shard_map/all_to_all | solution.py:164
  91.0 14.1 %collective-permute-start.7 = (bf16[384,512]{1,0:T(8,128)(2,1)S(1)}, bf16[384,512]{1,0:T(8,128)(2,1)S(1)}, u32[]{:S(2)}, u32[]{:S(2)}) collective-permute-start(bf16[384,512]{1,0:T(8,128)(2,1)S(1)} %get-tuple-element.18), channel_id=1, source_target_pairs={{0,1},{1,0},{2,3},{3,2},{4,5},{5,4},{6,7},{7,6},{8,9},{9,8},{10,11... | collective-permute-start | bytes 1179656 | tf_op jit(solution)/shard_map/ppermute | solution.py:252
where the time goes:
time: 109 us; the launch traced here: 108 us
  starting transfers between devices  44.1 us (40%)
  Pallas kernels  22.8 us (21%)
  local copies, waits for them, and re-layouts  19.1 us (18%)
  waiting for transfers between devices  13.5 us (12%)
  other arithmetic  7.47 us (7%)
    all_to_all x2, starting transfers between devices, exchange(): lax.all_to_all(tiles, 'patch', 0, 0, tiled=True, axis_index_groups=same_c...  20.7 us
    pallas_call x1, Pallas kernels, local(): pl.pallas_call(functools.partial(elastic_kernel, total_frames, own, halo)...  16.2 us
    ppermute x1, waiting for transfers between devices, local(): received = lax.ppermute(other, 'frame', partner)  11.8 us
    broadcast_in_dim x2, local copies, waits for them, and re-layouts, local(): offsets = offs[:, :3].T[:, :, None]  10.6 us
    pallas_call x5, Pallas kernels, call(): pl.pallas_call(kernel, out_shape=[jax.ShapeDtypeStruct(s, d) for s, d in...  6.6 us
    ppermute x1, starting transfers between devices, local(): lat_sib = lax.ppermute(lat_core, 'patch', sibling)  6.04 us
    ppermute x1, starting transfers between devices, local(): far_sib = lax.ppermute(far_core, 'patch', sibling)  5.51 us
    unnamed x27, local copies, waits for them, and re-layouts  4.46 us
  transfers between devices with their start and end apart: 13, of which 2 were waited for; matrix products, arithmetic and copies ran while one was open for 18% of the time, Pallas kernels for 21%

commit v1 on v0

v1 whole, which is shorter than its diff:
```python
import functools

import jax
import jax.numpy as jnp
from jax import lax
from jax.experimental import pallas as pl
from jax.experimental.pallas import tpu as pltpu
from jax.sharding import PartitionSpec as P

MEMBRANE = 5.0
BENDING = 5.0
GRAVITY = 40.0
BF = jnp.bfloat16
F32 = jnp.float32
NN = (((1,), (0,)), ((), ()))
TN = (((0,), (0,)), ((), ()))
NT = (((1,), (1,)), ((), ()))
PARAMS = pltpu.CompilerParams(vmem_limit_bytes=48 * 1024 * 1024)


def dot(a, b, dims=NN):
    return lax.dot_general(a, b, dims, preferred_element_type=F32)


def exact_dot(a, b):
    total = None
    for _ in range(3):
        part = b.astype(BF)
        b = b - part.astype(F32)
        term = dot(a, part)
        total = term if total is None else total + term
    return total


def one_hot(rows, ids):
    return (lax.broadcasted_iota(jnp.int32, (rows, ids.shape[1]), 0) == ids).astype(F32)


def column_block(rows):
    n, width = rows.shape
    return jnp.concatenate([rows, jnp.zeros((128 - n, width), F32)], axis=0).T


def interleave(core, mine_ref, other_ref, out_ref):
    chips, each, _ = mine_ref.shape
    for i in range(chips):
        out_ref[pl.ds(pl.multiple_of((2 * i + core) * each, each), each), :] = mine_ref[i]
        out_ref[pl.ds(pl.multiple_of((2 * i + 1 - core) * each, each), each), :] = other_ref[i]


def pick_kernel(send_ref, basis_ref, rest_ref, prev_ref, next_ref):
    own, halo = basis_ref.shape[1], send_ref.shape[1]
    rest = rest_ref[...]
    parts = []
    for _ in range(3):
        part = rest.astype(BF)
        rest = rest - part.astype(F32)
        parts.append(part.astype(F32))
    parts.append(jnp.zeros((7, own), F32))
    parts = jnp.concatenate(parts, axis=0).astype(BF)
    for row, out in ((0, prev_ref), (1, next_ref)):
        sel = one_hot(own, send_ref[row : row + 1, :]).astype(BF)
        for c in range(3):
            out[c * halo : (c + 1) * halo, :] = dot(sel, basis_ref[c], TN).astype(BF)
        out[3 * halo :, :] = jnp.zeros((out.shape[0] - 3 * halo, out.shape[1]), BF)
        out[3 * halo :, :halo] = dot(parts, sel).astype(BF)


def incidence_kernel(tri_ref, hin_ref, d_ref, dt_ref, b_ref, bt_ref, lap_ref):
    ext = dt_ref.shape[0]
    t = tri_ref.shape[1]
    a, b, c = (one_hot(ext, tri_ref[i : i + 1, :]) for i in range(3))
    for at, part in ((0, b - a), (t, c - b)):
        dt_ref[:, at : at + t] = part.astype(BF)
        d_ref[at : at + t, :] = part.T.astype(BF)
    a, b, c, d = (one_hot(ext, hin_ref[i : i + 1, :]) for i in range(4))
    part = c + d - a - b
    bt_ref[...] = part.astype(BF)
    b_ref[...] = part.T.astype(BF)
    lap_ref[...] = dot(bt_ref[...], b_ref[...]).astype(BF)


def constants_kernel(
    frames,
    rest_ref, mass_ref, prv_ref, nxt_ref, bend_ref, sq_ref, d_ref, b_ref, bt_ref, own_ref,
    edge_ref, vert_ref, sqc_ref, own_t_ref, prv_t_ref, nxt_t_ref,
):
    halo = (prv_ref.shape[0] - 16) // 3
    own_n = rest_ref.shape[1]
    pieces = [jnp.concatenate([rest_ref[...], mass_ref[...]], axis=0)]
    for ref in (prv_ref, nxt_ref):
        tail = ref[3 * halo :, :halo].astype(F32)
        pieces.append(
            jnp.concatenate([tail[0:3] + tail[3:6] + tail[6:9], jnp.zeros((1, halo), F32)], axis=0)
        )
    cols = column_block(jnp.concatenate(pieces, axis=1))
    edge_ref[...] = exact_dot(d_ref[...], cols)
    stretch = exact_dot(b_ref[...], cols) - column_block(bend_ref[...])
    force = exact_dot(bt_ref[...], stretch) * (2.0 * BENDING / frames)
    lane = lax.broadcasted_iota(jnp.int32, cols.shape, 1)
    weight = jnp.sum(jnp.where(lane == 3, cols, 0.0), axis=1, keepdims=True) * (GRAVITY / frames)
    vert_ref[...] = force + jnp.where(lane == 2, weight, 0.0)
    sqc_ref[...] = column_block(sq_ref[...])
    for c in range(3):
        own_t_ref[:, c * own_n : (c + 1) * own_n] = own_ref[c].T
    prv_t_ref[...] = prv_ref[: 3 * halo, :].T
    nxt_t_ref[...] = nxt_ref[: 3 * halo, :].T


def elastic_kernel(
    frames, step,
    core_ref, mine_ref, sib_ref, own_ref, prv_ref, nxt_ref, d_ref, dt_ref, lap_ref, edge_ref,
    vert_ref, sq_ref,
    lat_ref, f_own_ref, f_prv_ref, f_nxt_ref,
):
    own_n = own_ref.shape[1]
    t = sq_ref.shape[0]
    halo = f_prv_ref.shape[0] // 3
    interleave(core_ref[0], mine_ref, sib_ref, lat_ref)
    scale = 4.0 * MEMBRANE / frames
    for at in range(0, lat_ref.shape[1], step):
        here = slice(at, at + step)
        lat = lat_ref[:, here]
        x_prv = dot(prv_ref[: 3 * halo, :], lat).astype(BF)
        x_nxt = dot(nxt_ref[: 3 * halo, :], lat).astype(BF)
        points, edges = [], []
        for c in range(3):
            x = jnp.concatenate(
                [
                    dot(own_ref[c], lat).astype(BF),
                    x_prv[c * halo : (c + 1) * halo],
                    x_nxt[c * halo : (c + 1) * halo],
                ],
                axis=0,
            )
            points.append(x)
            edges.append(dot(d_ref[...], x) + edge_ref[:, c : c + 1])
        e1 = [e[:t] for e in edges]
        e2 = [e[t:] for e in edges]
        e3 = [u + v for u, v in zip(e1, e2)]
        s1, s2, s3 = (
            scale * (e[0] * e[0] + e[1] * e[1] + e[2] * e[2] - sq_ref[:, i : i + 1])
            for i, e in enumerate((e1, e2, e3))
        )
        for c in range(3):
            third = s3 * e3[c]
            g = jnp.concatenate(
                [(s1 * e1[c] + third).astype(BF), (s2 * e2[c] + third).astype(BF)], axis=0
            )
            f = dot(dt_ref[...], g) + dot(lap_ref[...], points[c]) * (2.0 * BENDING / frames)
            f = f + vert_ref[:, c : c + 1]
            f_own_ref[c * own_n : (c + 1) * own_n, here] = f[:own_n]
            f_prv_ref[c * halo : (c + 1) * halo, here] = f[own_n : own_n + halo].astype(BF)
            f_nxt_ref[c * halo : (c + 1) * halo, here] = f[own_n + halo :].astype(BF)


def latent_kernel(own_t_ref, prv_t_ref, nxt_t_ref, f_own_ref, f_prv_ref, f_nxt_ref, lg_ref):
    lg = dot(own_t_ref[...], f_own_ref[...].astype(BF))
    lg = lg + dot(prv_t_ref[...], f_prv_ref[...]) + dot(nxt_t_ref[...], f_nxt_ref[...])
    lg_ref[...] = lg.astype(BF)


def adjoint_kernel(
    half_ref, send_ref, f_own_ref, back_prv_ref, back_nxt_ref, mine_ref, other_ref
):
    halo = send_ref.shape[1]
    own = f_own_ref.shape[0] // 3
    half = own // 2
    first = half_ref[0] == 0
    to_prev = one_hot(own, send_ref[0:1, :]).astype(BF)
    to_next = one_hot(own, send_ref[1:2, :]).astype(BF)
    for c in range(3):
        rows = slice(c * halo, (c + 1) * halo)
        total = f_own_ref[c * own : (c + 1) * own, :]
        total = total + dot(to_prev, back_prv_ref[rows, :]) + dot(to_next, back_nxt_ref[rows, :])
        low, high = total[:half], total[half:]
        mine_ref[c * half : (c + 1) * half, :] = jnp.where(first, low, high).astype(BF)
        other_ref[c * half : (c + 1) * half, :] = jnp.where(first, high, low).astype(BF)


def own_part_kernel(mine_ref, lat_ref, out_ref):
    out_ref[...] = dot(mine_ref[...], lat_ref[...], NT).astype(BF)


def basis_grad_kernel(core_ref, part_ref, far_ref, core_lat_ref, sib_lat_ref, out_ref, lat_ref):
    interleave(core_ref[0], core_lat_ref, sib_lat_ref, lat_ref)
    far = dot(far_ref[...], lat_ref[...], NT).astype(BF).astype(F32)
    out_ref[...] = part_ref[...].astype(F32) + far


SMEM = pl.BlockSpec(memory_space=pltpu.SMEM)
VMEM = pl.BlockSpec(memory_space=pltpu.VMEM)


def call(kernel, outs, *args, scalars=0, scratch=()):
    return pl.pallas_call(
        kernel,
        in_specs=[SMEM] * scalars + [VMEM] * (len(args) - scalars),
        out_specs=[VMEM] * len(outs),
        out_shape=[jax.ShapeDtypeStruct(s, d) for s, d in outs],
        scratch_shapes=list(scratch),
        compiler_params=PARAMS,
    )(*args)


def local(basis, latents, rest_pos, triangles, hinges, rest_sq, bend_rest, masses, send_rows):
    own = basis.shape[1]
    width = basis.shape[2]
    frames = latents.shape[0]
    each = latents.shape[1]
    halo = send_rows.shape[1]
    tris = triangles.shape[1]
    hings = hinges.shape[1]
    ext = own + 2 * halo
    half = own // 2
    patches = lax.axis_size("patch")
    total_frames = frames * lax.axis_size("frame")
    chips = patches // 2
    onward = [(i, (i + 1) % patches) for i in range(patches)]
    backward = [((i + 1) % patches, i) for i in range(patches)]
    sibling = [(i, i ^ 1) for i in range(patches)]
    partner = [(0, 1), (1, 0)]
    same_core = [[2 * i + c for i in range(chips)] for c in range(2)]
    core = (lax.axis_index("patch") % 2).astype(jnp.int32).reshape(1)
    half_index = lax.axis_index("frame").astype(jnp.int32).reshape(1)

    lat_core = lax.all_to_all(
        jnp.broadcast_to(latents.T[None], (chips, each, frames)),
        "patch", 0, 0, tiled=True, axis_index_groups=same_core,
    )
    sent = ((3 * halo + 16, width), BF)
    rows_prev, rows_next = call(pick_kernel, [sent, sent], send_rows, basis, rest_pos)
    halo_prv = lax.ppermute(rows_next, "patch", onward)
    halo_nxt = lax.ppermute(rows_prev, "patch", backward)
    d, dt, b, bt, lap = call(
        incidence_kernel,
        [
            ((2 * tris, ext), BF),
            ((ext, 2 * tris), BF),
            ((hings, ext), BF),
            ((ext, hings), BF),
            ((ext, ext), BF),
        ],
        triangles,
        hinges,
    )
    edge, vert, sq, own_t, prv_t, nxt_t = call(
        functools.partial(constants_kernel, total_frames),
        [
            ((2 * tris, 128), F32),
            ((ext, 128), F32),
            ((tris, 128), F32),
            ((width, 3 * own), BF),
            ((width, 3 * halo), BF),
            ((width, 3 * halo), BF),
        ],
        rest_pos, masses[None], halo_prv, halo_nxt, bend_rest, rest_sq, d, b, bt, basis,
    )
    lat_sib = lax.ppermute(lat_core, "patch", sibling)
    lat_all, f_own, f_prv, f_nxt = call(
        functools.partial(elastic_kernel, total_frames, min(frames, 256)),
        [
            ((width, frames), BF),
            ((3 * own, frames), F32),
            ((3 * halo, frames), BF),
            ((3 * halo, frames), BF),
        ],
        core, lat_core, lat_sib, basis, halo_prv, halo_nxt, d, dt, lap, edge, vert, sq,
        scalars=1,
    )

    back_nxt = lax.ppermute(f_prv, "patch", backward)
    back_prv = lax.ppermute(f_nxt, "patch", onward)

    [lg] = call(
        latent_kernel, [((width, frames), BF)], own_t, prv_t, nxt_t, f_own, f_prv, f_nxt
    )
    shares = lax.all_to_all(lg.reshape(patches, each, frames), "patch", 0, 0, tiled=True)
    latent_grad = jnp.sum(shares.astype(F32), axis=0).T

    far_core = lax.ppermute(lat_core, "frame", partner)
    far_sib = lax.ppermute(far_core, "patch", sibling)

    piece = ((3 * half, frames), BF)
    mine, other = call(
        adjoint_kernel, [piece, piece], half_index, send_rows, f_own, back_prv, back_nxt,
        scalars=1,
    )
    received = lax.ppermute(other, "frame", partner)
    [part] = call(own_part_kernel, [((3 * half, width), BF)], mine, lat_all)
    [basis_grad] = call(
        basis_grad_kernel, [((3 * half, width), F32)], core, part, received, far_core, far_sib,
        scalars=1, scratch=[pltpu.VMEM((width, frames), BF)],
    )
    return basis_grad.reshape(3, half, width), latent_grad


def solution(mesh):
    return jax.shard_map(
        local,
        mesh=mesh,
        in_specs=(
            P(None, "patch", None),
            P("frame", "patch"),
            P(None, "patch"),
            P(None, "patch"),
            P(None, "patch"),
            P(None, "patch"),
            P(None, "patch"),
            P("patch"),
            P(None, "patch"),
        ),
        out_specs=(P(None, ("patch", "frame"), None), P("frame", "patch")),
        check_vma=False,
    )
```

time: 109 us -> 99.1 us (0.909)
  the two profiles are of different devices: /device:TPU:1 before, /device:TPU:0 now
where the time goes in v1:
time: 99.1 us; the launch traced here: 98.6 us
  starting transfers between devices  34.2 us (35%)
  waiting for transfers between devices  28.8 us (29%)
  Pallas kernels  28.2 us (28%)
  local copies, waits for them, and re-layouts  4.6 us (5%)
  other arithmetic  2.01 us (2%)
    pallas_call x8, Pallas kernels, call(): pl.pallas_call(kernel, in_specs=[SMEM] * scalars + [VMEM] * (len(args) -...  28.2 us
    ppermute x1, waiting for transfers between devices, local(): back_prv = lax.ppermute(f_nxt, 'patch', onward)  16.3 us
    all_to_all x1, starting transfers between devices, local(): lax.all_to_all(jnp.broadcast_to(latents.T[None], (chips, each, frames)),...  8.76 us
    all_to_all x1, starting transfers between devices, local(): lax.all_to_all(lg.reshape(patches, each, frames), 'patch', 0, 0, tiled=True)  6.16 us
    ppermute x1, starting transfers between devices, local(): halo_nxt = lax.ppermute(rows_prev, 'patch', backward)  5.96 us
    ppermute x1, starting transfers between devices, local(): back_nxt = lax.ppermute(f_prv, 'patch', backward)  5.95 us
    ppermute x1, waiting for transfers between devices, local(): received = lax.ppermute(other, 'frame', partner)  5.13 us
    all_to_all x1, waiting for transfers between devices, local(): lax.all_to_all(jnp.broadcast_to(latents.T[None], (chips, each, frames)),...  4.17 us
  transfers between devices with their start and end apart: 10, of which 4 were waited for; matrix products, arithmetic and copies ran while one was open for 0% of the time, Pallas kernels for 29%

profile of v1, /device:TPU:0, one launch (start us, length us, event | category | flops | bytes accessed | tf_op | source)
XLA Modules:
  0.0 98.6 jit_solution(6731726721582099056)
XLA Ops:
  0.7 0.0 copy-start
  0.7 1.7 %broadcast_in_dim.4 = bf16[32,16,512]{2,1,0:T(8,128)(2,1)} broadcast(bf16[16,512]{1,0:T(8,128)(2,1)} %bitcast.10), dimensions={1,2} | broadcast | bytes 540672 | tf_op jit(solution)/shard_map/broadcast_in_dim | solution.py:228
  2.4 8.8 %all-to-all-start = ((bf16[32,16,512]{2,1,0:T(8,128)(2,1)}), bf16[32,16,512]{2,1,0:T(8,128)(2,1)S(1)}, u32[]{:S(2)}, u32[]{:S(2)}) async-start(bf16[32,16,512]{2,1,0:T(8,128)(2,1)} %broadcast_in_dim.4), calls=%async_computation | async-start | bytes 1048576 | tf_op jit(solution)/shard_map/all_to_all | solution.py:227
  11.2 1.7 %shard_map.104 = (bf16[400,1024]{1,0:T(8,128)(2,1)}, bf16[400,1024]{1,0:T(8,128)(2,1)}) custom-call(s32[2,128]{1,0:T(2,128)S(1)} %copy-done.14, bf16[3,256,1024]{2,1,0:T(8,128)(2,1)S(1)} %copy-done, f32[3,256]{1,0:T(4,128)S(1)} %copy-done.9), custom_call_target="tpu_custom_call" | custom-call | tf_op jit(solution)/shard_map/pallas_call | solution.py:196
  12.9 0.0 collective-permute-start.1
  12.9 6.0 %collective-permute-start.2 = (bf16[400,1024]{1,0:T(8,128)(2,1)}, bf16[400,1024]{1,0:T(8,128)(2,1)S(1)}, u32[]{:S(2)}, u32[]{:S(2)}) collective-permute-start(bf16[400,1024]{1,0:T(8,128)(2,1)} %get-tuple-element.22), channel_id=1, source_target_pairs={{2,0},{4,2},{6,4},{8,6},{10,8},{12,10},{14,12},{16,14},{18,16},{20... | collective-permute-start | bytes 2457608 | tf_op jit(solution)/shard_map/ppermute | solution.py:234
  18.9 4.2 %all-to-all-done.mine_ref = bf16[32,16,512]{2,1,0:T(8,128)(2,1)S(1)} async-done(((bf16[32,16,512]{2,1,0:T(8,128)(2,1)}), bf16[32,16,512]{2,1,0:T(8,128)(2,1)S(1)}, u32[]{:S(2)}, u32[]{:S(2)}) %all-to-all-start) | async-done | bytes 524320 | tf_op jit(solution)/shard_map/all_to_all | solution.py:227
  23.0 0.0 collective-permute-start
  23.0 3.6 %collective-permute-start.6 = (bf16[32,16,512]{2,1,0:T(8,128)(2,1)S(1)}, bf16[32,16,512]{2,1,0:T(8,128)(2,1)}, u32[]{:S(2)}, u32[]{:S(2)}) collective-permute-start(bf16[32,16,512]{2,1,0:T(8,128)(2,1)S(1)} %all-to-all-done.mine_ref), channel_id=1, source_target_pairs={{0,1},{1,0},{2,3},{3,2},{4,5},{5,4},{6,7},{7,6},{8,9},{9,8},{10,11... | collective-permute-start | bytes 1572872 | tf_op jit(solution)/shard_map/ppermute | solution.py:281
  26.6 1.2 %shard_map.105 = (bf16[1024,512]{1,0:T(8,128)(2,1)S(1)}, bf16[512,1024]{1,0:T(8,128)(2,1)S(1)}, bf16[384,512]{1,0:T(8,128)(2,1)S(1)}, bf16[512,384]{1,0:T(8,128)(2,1)S(1)}, bf16[512,512]{1,0:T(8,128)(2,1)S(1)}) custom-call(s32[3,512]{1,0:T(4,128)S(1)} %copy-done.11, s32[4,384]{1,0:T(4,128)S(1)} %copy-done.13), custom_call_target="tpu_custom_call" | custom-call | tf_op jit(solution)/shard_map/pallas_call | solution.py:196
  27.9 1.0 copy-done.4
  28.8 3.2 %collective-permute-done.1.prv_ref = bf16[400,1024]{1,0:T(8,128)(2,1)S(1)} collective-permute-done((bf16[400,1024]{1,0:T(8,128)(2,1)}, bf16[400,1024]{1,0:T(8,128)(2,1)S(1)}, u32[]{:S(2)}, u32[]{:S(2)}) %collective-permute-start.1) | collective-permute-done | bytes 819232 | tf_op jit(solution)/shard_map/ppermute | solution.py:233
  32.0 0.0 collective-permute-done.2.nxt_ref
  32.0 4.0 %shard_map.106 = (f32[1024,128]{1,0:T(8,128)S(1)}, f32[512,128]{1,0:T(8,128)S(1)}, f32[512,128]{1,0:T(8,128)S(1)}, bf16[1024,768]{1,0:T(8,128)(2,1)}, bf16[1024,...) custom-call(f32[3,256]{1,0:T(4,128)S(1)} %copy-done.9, f32[1,256]{1,0:T(1,128)S(1)} %bitcast.7, ...), custom_call_target="tpu_custom_call" | custom-call | tf_op jit(solution)/shard_map/pallas_call | solution.py:196
  36.0 0.0 collective-permute-done.sib_ref
  36.0 0.8 copy-done.5
  36.8 1.0 %copy-done.6 = bf16[32,16,512]{2,1,0:T(8,128)(2,1)S(1)} copy-done((bf16[32,16,512]{2,1,0:T(8,128)(2,1)S(1)}, bf16[32,16,512]{2,1,0:T(8,128)(2,1)}, u32[]{:S(2)}) %copy-start.6) | copy-done | bytes 524312
  37.9 11.5 %shard_map.107 = (bf16[1024,512]{1,0:T(8,128)(2,1)S(1)}, f32[768,512]{1,0:T(8,128)}, bf16[384,512]{1,0:T(8,128)(2,1)S(1)}, bf16[384,512]{1,0:T(8,128)(2,1)S(1)}) custom-call(s32[1]{0:T(128)} %bitcast.core_ref, bf16[32,16,512]{2,1,0:T(8,128)(2,1)S(1)} %all-to-all-done.mine_ref, bf16[32,16,512]{2,1,0:T(8,128)(2,1)S(1)} %copy-done.6, ...), custom_call_target="tpu_custom_call" | custom-call | tf_op jit(solution)/shard_map/pallas_call | solution.py:196
  49.3 4.7 %shard_map.111 = bf16[1024,512]{1,0:T(8,128)(2,1)} custom-call(bf16[1024,768]{1,0:T(8,128)(2,1)S(1)} %copy-done.3, bf16[1024,384]{1,0:T(8,128)(2,1)S(1)} %get-tuple-element.38.prv_t_ref, bf16[1024,384]{1,0:T(8,128)(2,1)S(1)} %get-tuple-element.39.nxt_t_ref, f32[768,512]{1,0:T(8,128)} %get-tuple-element.31.f_own_ref, ...), custom_call_target="tpu_custom_call" | custom-call | tf_op jit(solution)/shard_map/pallas_call | solution.py:196
  54.1 6.2 %all-to-all-start.1 = ((bf16[64,16,512]{2,1,0:T(8,128)(2,1)}), bf16[64,16,512]{2,1,0:T(8,128)(2,1)}, u32[]{:S(2)}, u32[]{:S(2)}) async-start(bf16[64,16,512]{2,1,0:T(8,128)(2,1)} %bitcast.5), calls=%async_computation.1 | async-start | bytes 2097152 | tf_op jit(solution)/shard_map/all_to_all | solution.py:278
  60.2 0.1 collective-permute-start.3
  60.3 6.0 %collective-permute-start.4 = (bf16[384,512]{1,0:T(8,128)(2,1)}, bf16[384,512]{1,0:T(8,128)(2,1)}, u32[]{:S(2)}, u32[]{:S(2)}) collective-permute-start(bf16[384,512]{1,0:T(8,128)(2,1)} %copy-done.7), channel_id=1, source_target_pairs={{2,0},{4,2},{6,4},{8,6},{10,8},{12,10},{14,12},{16,14},{18,16},{20... | collective-permute-start | bytes 1179656 | tf_op jit(solution)/shard_map/ppermute | solution.py:272
  66.3 0.0 collective-permute-done.6.core_lat_ref
  66.3 0.0 collective-permute-start.7
  66.3 16.3 %collective-permute-done.3.back_prv_ref = bf16[384,512]{1,0:T(8,128)(2,1)} collective-permute-done((bf16[384,512]{1,0:T(8,128)(2,1)}, bf16[384,512]{1,0:T(8,128)(2,1)}, u32[]{:S(2)}, u32[]{:S(2)}) %collective-permute-start.3) | collective-permute-done | bytes 393248 | tf_op jit(solution)/shard_map/ppermute | solution.py:273
  82.6 1.7 %shard_map.108 = (bf16[384,512]{1,0:T(8,128)(2,1)S(1)}, bf16[384,512]{1,0:T(8,128)(2,1)S(1)}) custom-call(s32[1]{0:T(128)} %bitcast.1.half_ref, s32[2,128]{1,0:T(2,128)S(1)} %copy-done.14, f32[768,512]{1,0:T(8,128)S(1)} %copy-done.1, bf16[384,512]{1,0:T(8,128)(2,1)} %collective-permute-done.3.back_prv_ref, bf16[384,512]{1,0:T(8,128)(2,1)} %collective-permute-done.4.back_nxt_ref), custom_call_target="tpu_custom_call" | custom-call | tf_op jit(solution)/shard_map/pallas_call | solution.py:196
  84.3 3.7 %collective-permute-start.5 = (bf16[384,512]{1,0:T(8,128)(2,1)S(1)}, bf16[384,512]{1,0:T(8,128)(2,1)S(1)}, u32[]{:S(2)}, u32[]{:S(2)}) collective-permute-start(bf16[384,512]{1,0:T(8,128)(2,1)S(1)} %get-tuple-element.36), channel_id=1, source_target_pairs={{0,1},{1,0},{2,3},{3,2},{4,5},{5,4},{6,7},{7,6},{8,9},{9,8},{10,11... | collective-permute-start | bytes 1179656 | tf_op jit(solution)/shard_map/ppermute | solution.py:289
  87.9 0.6 shard_map.109.part_ref
  88.6 5.1 %collective-permute-done.5.far_ref = bf16[384,512]{1,0:T(8,128)(2,1)S(1)} collective-permute-done((bf16[384,512]{1,0:T(8,128)(2,1)S(1)}, bf16[384,512]{1,0:T(8,128)(2,1)S(1)}, u32[]{:S(2)}, u32[]{:S(2)}) %collective-permute-start.5) | collective-permute-done | bytes 393248 | tf_op jit(solution)/shard_map/ppermute | solution.py:289
  93.7 2.9 %shard_map.110 = f32[384,1024]{1,0:T(8,128)} custom-call(s32[1]{0:T(128)} %bitcast.core_ref, bf16[384,1024]{1,0:T(8,128)(2,1)S(1)} %shard_map.109.part_ref, bf16[384,512]{1,0:T(8,128)(2,1)S(1)} %collective-permute-done.5.far_ref, bf16[32,16,512]{2,1,0:T(8,128)(2,1)} %collective-permute-done.6.core_lat_ref, ...), custom_call_target="tpu_custom_call" | custom-call | tf_op jit(solution)/shard_map/pallas_call | solution.py:196
  96.6 0.0 all-to-all-done.1
  96.6 2.0 %convert_reduce_fusion = f32[16,512]{1,0:T(8,128)} fusion(bf16[64,16,512]{2,1,0:T(8,128)(2,1)} %all-to-all-done.1), kind=kLoop, calls=%fused_computation | loop fusion | flops 1040384 | bytes 1081344 | tf_op jit(solution)/shard_map/reduce_sum | solution.py:279
  (30 shorter events, 0.1 us)
Async XLA Ops:
  0.6 10.6 %copy-start.9 = (f32[3,256]{1,0:T(4,128)S(1)}, f32[3,256]{1,0:T(4,128)}, u32[]{:S(2)}) copy-start(f32[3,256]{1,0:T(4,128)} %rest_ref.3) | copy-start | bytes 9220
  0.6 10.6 %copy-start.14 = (s32[2,128]{1,0:T(2,128)S(1)}, s32[2,128]{1,0:T(2,128)}, u32[]{:S(2)}) copy-start(s32[2,128]{1,0:T(2,128)} %send_ref.3) | copy-start | bytes 3076
  0.7 10.6 %copy-start = (bf16[3,256,1024]{2,1,0:T(8,128)(2,1)S(1)}, bf16[3,256,1024]{2,1,0:T(8,128)(2,1)}, u32[]{:S(2)}) copy-start(bf16[3,256,1024]{2,1,0:T(8,128)(2,1)} %own_ref.3) | copy-start | bytes 4718596
  0.7 26.0 %copy-start.11 = (s32[3,512]{1,0:T(4,128)S(1)}, s32[3,512]{1,0:T(4,128)}, u32[]{:S(2)}) copy-start(s32[3,512]{1,0:T(4,128)} %tri_ref.1) | copy-start | bytes 18436
  0.7 25.9 %copy-start.13 = (s32[4,384]{1,0:T(4,128)S(1)}, s32[4,384]{1,0:T(4,128)}, u32[]{:S(2)}) copy-start(s32[4,384]{1,0:T(4,128)} %hin_ref.1) | copy-start | bytes 18436
  0.7 31.3 %copy-start.10 = (f32[3,512]{1,0:T(4,128)S(1)}, f32[3,512]{1,0:T(4,128)}, u32[]{:S(2)}) copy-start(f32[3,512]{1,0:T(4,128)} %sq_ref.1) | copy-start | bytes 18436
  0.7 31.3 %copy-start.12 = (f32[3,384]{1,0:T(4,128)S(1)}, f32[3,384]{1,0:T(4,128)}, u32[]{:S(2)}) copy-start(f32[3,384]{1,0:T(4,128)} %bend_ref.1) | copy-start | bytes 13828
  0.7 31.3 %copy-start.15 = (f32[256]{0:T(256)S(1)}, f32[256]{0:T(256)}, u32[]{:S(2)}) copy-start(f32[256]{0:T(256)} %param.16) | copy-start | bytes 3076
  2.4 20.6 %all-to-all-start = ((bf16[32,16,512]{2,1,0:T(8,128)(2,1)}), bf16[32,16,512]{2,1,0:T(8,128)(2,1)S(1)}, u32[]{:S(2)}, u32[]{:S(2)}) async-start(bf16[32,16,512]{2,1,0:T(8,128)(2,1)} %broadcast_in_dim.4), calls=%async_computation | async-start | bytes 1048576 | tf_op jit(solution)/shard_map/all_to_all | solution.py:227
  12.9 19.1 %collective-permute-start.1 = (bf16[400,1024]{1,0:T(8,128)(2,1)}, bf16[400,1024]{1,0:T(8,128)(2,1)S(1)}, u32[]{:S(2)}, u32[]{:S(2)}) collective-permute-start(bf16[400,1024]{1,0:T(8,128)(2,1)} %get-tuple-element.21), channel_id=1, source_target_pairs={{0,2},{2,4},{4,6},{6,8},{8,10},{10,12},{12,14},{14,16},{16,18},{18... | collective-permute-start | bytes 2457608 | tf_op jit(solution)/shard_map/ppermute | solution.py:233
  12.9 19.1 %collective-permute-start.2 = (bf16[400,1024]{1,0:T(8,128)(2,1)}, bf16[400,1024]{1,0:T(8,128)(2,1)S(1)}, u32[]{:S(2)}, u32[]{:S(2)}) collective-permute-start(bf16[400,1024]{1,0:T(8,128)(2,1)} %get-tuple-element.22), channel_id=1, source_target_pairs={{2,0},{4,2},{6,4},{8,6},{10,8},{12,10},{14,12},{16,14},{18,16},{20... | collective-permute-start | bytes 2457608 | tf_op jit(solution)/shard_map/ppermute | solution.py:234
  23.0 13.0 %collective-permute-start = (bf16[32,16,512]{2,1,0:T(8,128)(2,1)S(1)}, bf16[32,16,512]{2,1,0:T(8,128)(2,1)S(1)}, u32[]{:S(2)}, u32[]{:S(2)}) collective-permute-start(bf16[32,16,512]{2,1,0:T(8,128)(2,1)S(1)} %all-to-all-done.mine_ref), channel_id=1, source_target_pairs={{0,2},{2,0},{4,6},{6,4},{8,10},{10,8},{12,14},{14,12},{16,18},{18,... | collective-permute-start | bytes 1572872 | tf_op jit(solution)/shard_map/ppermute | solution.py:259
  23.0 43.2 %collective-permute-start.6 = (bf16[32,16,512]{2,1,0:T(8,128)(2,1)S(1)}, bf16[32,16,512]{2,1,0:T(8,128)(2,1)}, u32[]{:S(2)}, u32[]{:S(2)}) collective-permute-start(bf16[32,16,512]{2,1,0:T(8,128)(2,1)S(1)} %all-to-all-done.mine_ref), channel_id=1, source_target_pairs={{0,1},{1,0},{2,3},{3,2},{4,5},{5,4},{6,7},{7,6},{8,9},{9,8},{10,11... | collective-permute-start | bytes 1572872 | tf_op jit(solution)/shard_map/ppermute | solution.py:281
  27.9 1.0 copy-start.4
  28.8 7.1 %copy-start.2 = (bf16[1024,512]{1,0:T(8,128)(2,1)}, bf16[1024,512]{1,0:T(8,128)(2,1)S(1)}, u32[]{:S(2)}) copy-start(bf16[1024,512]{1,0:T(8,128)(2,1)S(1)} %get-tuple-element.23.d_ref) | copy-start | bytes 3145732
  36.0 0.8 copy-start.5
  36.8 1.0 %copy-start.6 = (bf16[32,16,512]{2,1,0:T(8,128)(2,1)S(1)}, bf16[32,16,512]{2,1,0:T(8,128)(2,1)}, u32[]{:S(2)}) copy-start(bf16[32,16,512]{2,1,0:T(8,128)(2,1)} %copy-done.5) | copy-start | bytes 1572868
  37.9 11.5 %copy-start.3 = (bf16[1024,768]{1,0:T(8,128)(2,1)S(1)}, bf16[1024,768]{1,0:T(8,128)(2,1)}, u32[]{:S(2)}) copy-start(bf16[1024,768]{1,0:T(8,128)(2,1)} %get-tuple-element.37.own_t_ref) | copy-start | bytes 4718596
  49.3 4.7 %copy-start.7 = (bf16[384,512]{1,0:T(8,128)(2,1)}, bf16[384,512]{1,0:T(8,128)(2,1)S(1)}, u32[]{:S(2)}) copy-start(bf16[384,512]{1,0:T(8,128)(2,1)S(1)} %get-tuple-element.33.f_prv_ref) | copy-start | bytes 1179652
  49.3 4.7 %copy-start.8 = (bf16[384,512]{1,0:T(8,128)(2,1)}, bf16[384,512]{1,0:T(8,128)(2,1)S(1)}, u32[]{:S(2)}) copy-start(bf16[384,512]{1,0:T(8,128)(2,1)S(1)} %get-tuple-element.32.f_nxt_ref) | copy-start | bytes 1179652
  54.1 28.5 %copy-start.1 = (f32[768,512]{1,0:T(8,128)S(1)}, f32[768,512]{1,0:T(8,128)}, u32[]{:S(2)}) copy-start(f32[768,512]{1,0:T(8,128)} %get-tuple-element.31.f_own_ref) | copy-start | bytes 4718596
  54.1 42.5 %all-to-all-start.1 = ((bf16[64,16,512]{2,1,0:T(8,128)(2,1)}), bf16[64,16,512]{2,1,0:T(8,128)(2,1)}, u32[]{:S(2)}, u32[]{:S(2)}) async-start(bf16[64,16,512]{2,1,0:T(8,128)(2,1)} %bitcast.5), calls=%async_computation.1 | async-start | bytes 2097152 | tf_op jit(solution)/shard_map/all_to_all | solution.py:278
  60.2 22.3 %collective-permute-start.3 = (bf16[384,512]{1,0:T(8,128)(2,1)}, bf16[384,512]{1,0:T(8,128)(2,1)}, u32[]{:S(2)}, u32[]{:S(2)}) collective-permute-start(bf16[384,512]{1,0:T(8,128)(2,1)} %copy-done.8), channel_id=1, source_target_pairs={{0,2},{2,4},{4,6},{6,8},{8,10},{10,12},{12,14},{14,16},{16,18},{18... | collective-permute-start | bytes 1179656 | tf_op jit(solution)/shard_map/ppermute | solution.py:273
  60.3 22.3 %collective-permute-start.4 = (bf16[384,512]{1,0:T(8,128)(2,1)}, bf16[384,512]{1,0:T(8,128)(2,1)}, u32[]{:S(2)}, u32[]{:S(2)}) collective-permute-start(bf16[384,512]{1,0:T(8,128)(2,1)} %copy-done.7), channel_id=1, source_target_pairs={{2,0},{4,2},{6,4},{8,6},{10,8},{12,10},{14,12},{16,14},{18,16},{20... | collective-permute-start | bytes 1179656 | tf_op jit(solution)/shard_map/ppermute | solution.py:272
  66.3 22.3 %collective-permute-start.7 = (bf16[32,16,512]{2,1,0:T(8,128)(2,1)}, bf16[32,16,512]{2,1,0:T(8,128)(2,1)S(1)}, u32[]{:S(2)}, u32[]{:S(2)}) collective-permute-start(bf16[32,16,512]{2,1,0:T(8,128)(2,1)} %collective-permute-done.6.core_lat_ref), channel_id=1, source_target_pairs={{0,2},{2,0},{4,6},{6,4},{8,10},{10,8},{12,14},{14,12},{16,18},{18,... | collective-permute-start | bytes 1572872 | tf_op jit(solution)/shard_map/ppermute | solution.py:282
  84.3 9.4 %collective-permute-start.5 = (bf16[384,512]{1,0:T(8,128)(2,1)S(1)}, bf16[384,512]{1,0:T(8,128)(2,1)S(1)}, u32[]{:S(2)}, u32[]{:S(2)}) collective-permute-start(bf16[384,512]{1,0:T(8,128)(2,1)S(1)} %get-tuple-element.36), channel_id=1, source_target_pairs={{0,1},{1,0},{2,3},{3,2},{4,5},{5,4},{6,7},{7,6},{8,9},{9,8},{10,11... | collective-permute-start | bytes 1179656 | tf_op jit(solution)/shard_map/ppermute | solution.py:289

commit v2 on v1

--- a/solution.py
+++ b/solution.py
@@ -1,4 +1,5 @@
 import functools
+import math
 
 import jax
 import jax.numpy as jnp
@@ -15,7 +16,6 @@
 NN = (((1,), (0,)), ((), ()))
 TN = (((0,), (0,)), ((), ()))
 NT = (((1,), (1,)), ((), ()))
-PARAMS = pltpu.CompilerParams(vmem_limit_bytes=48 * 1024 * 1024)
 
 
 def dot(a, b, dims=NN):
@@ -48,7 +48,15 @@
         out_ref[pl.ds(pl.multiple_of((2 * i + 1 - core) * each, each), each), :] = other_ref[i]
 
 
-def pick_kernel(send_ref, basis_ref, rest_ref, prev_ref, next_ref):
+def send(ref):
+    if isinstance(ref, Stored):
+        ref.send()
+
+
+def first_kernel(shard_ref, send_ref, basis_ref, rest_ref, copies_ref, prev_ref, next_ref):
+    for i in range(copies_ref.shape[0]):
+        copies_ref[i] = shard_ref[...]
+    send(copies_ref)
     own, halo = basis_ref.shape[1], send_ref.shape[1]
     rest = rest_ref[...]
     parts = []
@@ -64,10 +72,17 @@
             out[c * halo : (c + 1) * halo, :] = dot(sel, basis_ref[c], TN).astype(BF)
         out[3 * halo :, :] = jnp.zeros((out.shape[0] - 3 * halo, out.shape[1]), BF)
         out[3 * halo :, :halo] = dot(parts, sel).astype(BF)
-
-
-def incidence_kernel(tri_ref, hin_ref, d_ref, dt_ref, b_ref, bt_ref, lap_ref):
+        send(out)
+
+
+def own_kernel(
+    tri_ref, hin_ref, sq_ref, own_ref, d_ref, dt_ref, b_ref, bt_ref, lap_ref, sqc_ref, own_t_ref
+):
     ext = dt_ref.shape[0]
+    own_n = own_ref.shape[1]
+    sqc_ref[...] = column_block(sq_ref[...])
+    for c in range(3):
+        own_t_ref[:, c * own_n : (c + 1) * own_n] = own_ref[c].T
     t = tri_ref.shape[1]
     a, b, c = (one_hot(ext, tri_ref[i : i + 1, :]) for i in range(3))
     for at, part in ((0, b - a), (t, c - b)):
@@ -80,13 +95,12 @@
     lap_ref[...] = dot(bt_ref[...], b_ref[...]).astype(BF)
 
 
-def constants_kernel(
+def halo_kernel(
     frames,
-    rest_ref, mass_ref, prv_ref, nxt_ref, bend_ref, sq_ref, d_ref, b_ref, bt_ref, own_ref,
-    edge_ref, vert_ref, sqc_ref, own_t_ref, prv_t_ref, nxt_t_ref,
+    rest_ref, mass_ref, prv_ref, nxt_ref, bend_ref, d_ref, b_ref, bt_ref,
+    edge_ref, vert_ref, halo_t_ref,
 ):
     halo = (prv_ref.shape[0] - 16) // 3
-    own_n = rest_ref.shape[1]
     pieces = [jnp.concatenate([rest_ref[...], mass_ref[...]], axis=0)]
     for ref in (prv_ref, nxt_ref):
         tail = ref[3 * halo :, :halo].astype(F32)
@@ -100,18 +114,15 @@
     lane = lax.broadcasted_iota(jnp.int32, cols.shape, 1)
     weight = jnp.sum(jnp.where(lane == 3, cols, 0.0), axis=1, keepdims=True) * (GRAVITY / frames)
     vert_ref[...] = force + jnp.where(lane == 2, weight, 0.0)
-    sqc_ref[...] = column_block(sq_ref[...])
-    for c in range(3):
-        own_t_ref[:, c * own_n : (c + 1) * own_n] = own_ref[c].T
-    prv_t_ref[...] = prv_ref[: 3 * halo, :].T
-    nxt_t_ref[...] = nxt_ref[: 3 * halo, :].T
+    halo_t_ref[:, : 3 * halo] = prv_ref[: 3 * halo, :].T
+    halo_t_ref[:, 3 * halo :] = nxt_ref[: 3 * halo, :].T
 
 
 def elastic_kernel(
     frames, step,
     core_ref, mine_ref, sib_ref, own_ref, prv_ref, nxt_ref, d_ref, dt_ref, lap_ref, edge_ref,
-    vert_ref, sq_ref,
-    lat_ref, f_own_ref, f_prv_ref, f_nxt_ref,
+    vert_ref, sq_ref, own_t_ref, halo_t_ref,
+    lat_ref, f_own_ref, f_prv_ref, f_nxt_ref, lg_ref, f_all_ref,
 ):
     own_n = own_ref.shape[1]
     t = sq_ref.shape[0]
@@ -150,14 +161,26 @@
             f = dot(dt_ref[...], g) + dot(lap_ref[...], points[c]) * (2.0 * BENDING / frames)
             f = f + vert_ref[:, c : c + 1]
             f_own_ref[c * own_n : (c + 1) * own_n, here] = f[:own_n]
-            f_prv_ref[c * halo : (c + 1) * halo, here] = f[own_n : own_n + halo].astype(BF)
-            f_nxt_ref[c * halo : (c + 1) * halo, here] = f[own_n + halo :].astype(BF)
-
-
-def latent_kernel(own_t_ref, prv_t_ref, nxt_t_ref, f_own_ref, f_prv_ref, f_nxt_ref, lg_ref):
-    lg = dot(own_t_ref[...], f_own_ref[...].astype(BF))
-    lg = lg + dot(prv_t_ref[...], f_prv_ref[...]) + dot(nxt_t_ref[...], f_nxt_ref[...])
-    lg_ref[...] = lg.astype(BF)
+            short = f.astype(BF)
+            f_prv_ref[c * halo : (c + 1) * halo, here] = short[own_n : own_n + halo]
+            f_nxt_ref[c * halo : (c + 1) * halo, here] = short[own_n + halo :]
+            for at_row, size, first in (
+                (c * own_n, own_n, 0),
+                (3 * own_n + c * halo, halo, own_n),
+                (3 * (own_n + halo) + c * halo, halo, own_n + halo),
+            ):
+                f_all_ref[at_row : at_row + size, here] = short[first : first + size]
+    for at in range(0, lg_ref.shape[0], 256):
+        rows = slice(at, at + 256)
+        both = jnp.concatenate([own_t_ref[rows, :], halo_t_ref[rows, :]], axis=1)
+        lg_ref[rows, :] = dot(both, f_all_ref[...]).astype(BF)
+
+
+def share_kernel(shares_ref, out_ref):
+    total = shares_ref[0].astype(F32)
+    for i in range(1, shares_ref.shape[0]):
+        total = total + shares_ref[i].astype(F32)
+    out_ref[...] = total
 
 
 def adjoint_kernel(
@@ -188,18 +211,90 @@
     out_ref[...] = part_ref[...].astype(F32) + far
 
 
+class Loaded:
+    def __init__(self, source, ref, sem):
+        self.ref, self.copy = ref, pltpu.make_async_copy(source, ref, sem)
+        self.shape, self.waiting = ref.shape, True
+        self.copy.start()
+
+    def wait(self):
+        if self.waiting:
+            self.copy.wait()
+            self.waiting = False
+
+    def __getitem__(self, index):
+        self.wait()
+        return self.ref[index]
+
+
+class Stored:
+    def __init__(self, ref, target, sem):
+        self.ref, self.copy = ref, pltpu.make_async_copy(ref, target, sem)
+        self.shape, self.open = ref.shape, True
+
+    def __setitem__(self, index, value):
+        self.ref[index] = value
+
+    def __getitem__(self, index):
+        return self.ref[index]
+
+    def send(self):
+        if self.open:
+            self.copy.start()
+            self.open = False
+
+
 SMEM = pl.BlockSpec(memory_space=pltpu.SMEM)
+ANY = pl.BlockSpec(memory_space=pl.ANY)
 VMEM = pl.BlockSpec(memory_space=pltpu.VMEM)
 
 
-def call(kernel, outs, *args, scalars=0, scratch=()):
+def call(kernel, outs, *args, scalars=0, direct=True, near=(), scratch=(), macs=0, room=0):
+    moved = sum(a.size * a.dtype.itemsize for a in args)
+    moved += sum(math.prod(s) * jnp.dtype(d).itemsize for s, d in outs)
+    ins, n_in, n_out = args[scalars:], len(args) - scalars, len(outs)
+    params = pltpu.CompilerParams(vmem_limit_bytes=(room or 24) << 20)
+    if direct:
+        return pl.pallas_call(
+            kernel,
+            cost_estimate=pl.CostEstimate(flops=2 * macs, bytes_accessed=moved, transcendentals=0),
+            in_specs=[SMEM] * scalars + [VMEM] * n_in,
+            out_specs=[VMEM] * n_out,
+            out_shape=[jax.ShapeDtypeStruct(s, d) for s, d in outs],
+            scratch_shapes=list(scratch),
+            compiler_params=params,
+        )(*args)
+    far = [i for i in range(n_in) if i + scalars not in near]
+    n_far = len(far)
+
+    def body(*refs):
+        numbers, refs = refs[:scalars], refs[scalars:]
+        sources, targets, refs = refs[:n_in], refs[n_in : n_in + n_out], refs[n_in + n_out :]
+        held, made, refs = refs[:n_far], refs[n_far : n_far + n_out], refs[n_far + n_out :]
+        in_sem, out_sem, *rest = refs
+        loads = list(sources)
+        for i, at in enumerate(far):
+            loads[at] = Loaded(sources[at], held[i], in_sem.at[i])
+        stores = [Stored(v, x, out_sem.at[i]) for i, (x, v) in enumerate(zip(targets, made))]
+        kernel(*numbers, *loads, *stores, *rest)
+        for at in far:
+            loads[at].wait()
+        for store in stores:
+            store.send()
+        for store in stores:
+            store.copy.wait()
+
     return pl.pallas_call(
-        kernel,
-        in_specs=[SMEM] * scalars + [VMEM] * (len(args) - scalars),
-        out_specs=[VMEM] * len(outs),
+        body,
+        cost_estimate=pl.CostEstimate(flops=2 * macs, bytes_accessed=moved, transcendentals=0),
+        in_specs=[SMEM] * scalars + [ANY if i in far else VMEM for i in range(n_in)],
+        out_specs=[ANY] * n_out,
         out_shape=[jax.ShapeDtypeStruct(s, d) for s, d in outs],
-        scratch_shapes=list(scratch),
-        compiler_params=PARAMS,
+        scratch_shapes=[pltpu.VMEM(ins[i].shape, ins[i].dtype) for i in far]
+        + [pltpu.VMEM(s, d) for s, d in outs]
+        + [pltpu.SemaphoreType.DMA((max(n_far, 1),)), pltpu.SemaphoreType.DMA((n_out,))]
+        + list(scratch),
+        compiler_params=params,
     )(*args)
 
 
@@ -224,59 +319,56 @@
     core = (lax.axis_index("patch") % 2).astype(jnp.int32).reshape(1)
     half_index = lax.axis_index("frame").astype(jnp.int32).reshape(1)
 
+    sent = ((3 * halo + 16, width), BF)
+    copies, rows_prev, rows_next = call(
+        first_kernel, [((chips, each, frames), BF), sent, sent],
+        latents.T, send_rows, basis, rest_pos, direct=False, room=60,
+    )
     lat_core = lax.all_to_all(
-        jnp.broadcast_to(latents.T[None], (chips, each, frames)),
-        "patch", 0, 0, tiled=True, axis_index_groups=same_core,
-    )
-    sent = ((3 * halo + 16, width), BF)
-    rows_prev, rows_next = call(pick_kernel, [sent, sent], send_rows, basis, rest_pos)
+        copies, "patch", 0, 0, tiled=True, axis_index_groups=same_core
+    )
     halo_prv = lax.ppermute(rows_next, "patch", onward)
     halo_nxt = lax.ppermute(rows_prev, "patch", backward)
-    d, dt, b, bt, lap = call(
-        incidence_kernel,
+    d, dt, b, bt, lap, sq, own_t = call(
+        own_kernel,
         [
             ((2 * tris, ext), BF),
             ((ext, 2 * tris), BF),
             ((hings, ext), BF),
             ((ext, hings), BF),
             ((ext, ext), BF),
-        ],
-        triangles,
-        hinges,
-    )
-    edge, vert, sq, own_t, prv_t, nxt_t = call(
-        functools.partial(constants_kernel, total_frames),
-        [
-            ((2 * tris, 128), F32),
-            ((ext, 128), F32),
             ((tris, 128), F32),
             ((width, 3 * own), BF),
-            ((width, 3 * halo), BF),
-            ((width, 3 * halo), BF),
         ],
-        rest_pos, masses[None], halo_prv, halo_nxt, bend_rest, rest_sq, d, b, bt, basis,
+        triangles, hinges, rest_sq, basis,
+        macs=1 << 30,
+    )
+    edge, vert, halo_t = call(
+        functools.partial(halo_kernel, total_frames),
+        [((2 * tris, 128), F32), ((ext, 128), F32), ((width, 6 * halo), BF)],
+        rest_pos, masses[None], halo_prv, halo_nxt, bend_rest, d, b, bt,
+        macs=1 << 30,
     )
     lat_sib = lax.ppermute(lat_core, "patch", sibling)
-    lat_all, f_own, f_prv, f_nxt = call(
+    lat_all, f_own, f_prv, f_nxt, lg = call(
         functools.partial(elastic_kernel, total_frames, min(frames, 256)),
         [
             ((width, frames), BF),
             ((3 * own, frames), F32),
             ((3 * halo, frames), BF),
             ((3 * halo, frames), BF),
+            ((width, frames), BF),
         ],
         core, lat_core, lat_sib, basis, halo_prv, halo_nxt, d, dt, lap, edge, vert, sq,
-        scalars=1,
+        own_t, halo_t,
+        scalars=1, scratch=[pltpu.VMEM((3 * ext, frames), BF)], macs=5 << 30, room=32,
     )
 
     back_nxt = lax.ppermute(f_prv, "patch", backward)
     back_prv = lax.ppermute(f_nxt, "patch", onward)
 
-    [lg] = call(
-        latent_kernel, [((width, frames), BF)], own_t, prv_t, nxt_t, f_own, f_prv, f_nxt
-    )
     shares = lax.all_to_all(lg.reshape(patches, each, frames), "patch", 0, 0, tiled=True)
-    latent_grad = jnp.sum(shares.astype(F32), axis=0).T
+    [latent_grad] = call(share_kernel, [((each, frames), F32)], shares)
 
     far_core = lax.ppermute(lat_core, "frame", partner)
     far_sib = lax.ppermute(far_core, "patch", sibling)
@@ -284,15 +376,15 @@
     piece = ((3 * half, frames), BF)
     mine, other = call(
         adjoint_kernel, [piece, piece], half_index, send_rows, f_own, back_prv, back_nxt,
-        scalars=1,
+        scalars=1, macs=10 << 30,
     )
     received = lax.ppermute(other, "frame", partner)
-    [part] = call(own_part_kernel, [((3 * half, width), BF)], mine, lat_all)
+    [part] = call(own_part_kernel, [((3 * half, width), BF)], mine, lat_all, macs=3 * half * width * frames)
     [basis_grad] = call(
         basis_grad_kernel, [((3 * half, width), F32)], core, part, received, far_core, far_sib,
         scalars=1, scratch=[pltpu.VMEM((width, frames), BF)],
     )
-    return basis_grad.reshape(3, half, width), latent_grad
+    return basis_grad.reshape(3, half, width), latent_grad.T
 
 
 def solution(mesh):

time: 99.1 us -> 91.8 us (0.926)
  the two profiles are of different devices: /device:TPU:0 before, /device:TPU:1 now
where the time goes in v2:
time: 91.8 us; the launch traced here: 91.3 us
  starting transfers between devices  35.9 us (39%)
  Pallas kernels  26.2 us (29%)
  waiting for transfers between devices  24.7 us (27%)
  local copies, waits for them, and re-layouts  3.73 us (4%)
    pallas_call x7, Pallas kernels, call(): pl.pallas_call(kernel, cost_estimate=pl.CostEstimate(flops=2 * macs, byte...  22.9 us
    ppermute x1, waiting for transfers between devices, local(): received = lax.ppermute(other, 'frame', partner)  17.3 us
    all_to_all x1, starting transfers between devices, local(): lax.all_to_all(lg.reshape(patches, each, frames), 'patch', 0, 0, tiled=True)  10 us
    all_to_all x1, starting transfers between devices, local(): lax.all_to_all(copies, 'patch', 0, 0, tiled=True, axis_index_groups=same_...  9.23 us
    all_to_all x1, waiting for transfers between devices, local(): lax.all_to_all(copies, 'patch', 0, 0, tiled=True, axis_index_groups=same_...  7.38 us
    unnamed x24, local copies, waits for them, and re-layouts  3.73 us
    ppermute x1, starting transfers between devices, local(): far_core = lax.ppermute(lat_core, 'frame', partner)  3.56 us
    ppermute x1, starting transfers between devices, local(): received = lax.ppermute(other, 'frame', partner)  3.38 us
  transfers between devices with their start and end apart: 10, of which 2 were waited for; matrix products, arithmetic and copies ran while one was open for 0% of the time, Pallas kernels for 24%

profile of v2, /device:TPU:1, one launch (start us, length us, event | category | flops | bytes accessed | tf_op | source)
XLA Modules:
  0.0 91.3 jit_solution(14473416664679391758)
XLA Ops:
  0.7 3.2 %shard_map.104 = (bf16[32,16,512]{2,1,0:T(8,128)(2,1)}, bf16[400,1024]{1,0:T(8,128)(2,1)}, bf16[400,1024]{1,0:T(8,128)(2,1)}) custom-call(bf16[16,512]{1,0:T(8,128)(2,1)} %bitcast.10, s32[2,128]{1,0:T(2,128)} %send_ref.1, bf16[3,256,1024]{2,1,0:T(8,128)(2,1)} %own_ref.3, f32[3,256]{1,0:T(4,128)} %rest_ref.1), custom_call_target="tpu_custom_call" | custom-call | bytes 3756032 | tf_op jit(solution)/shard_map/pallas_call | solution.py:287
  3.9 9.2 %all-to-all-start = ((bf16[32,16,512]{2,1,0:T(8,128)(2,1)}), bf16[32,16,512]{2,1,0:T(8,128)(2,1)S(1)}, u32[]{:S(2)}, u32[]{:S(2)}) async-start(bf16[32,16,512]{2,1,0:T(8,128)(2,1)} %get-tuple-element.22), calls=%async_computation | async-start | bytes 1048576 | tf_op jit(solution)/shard_map/all_to_all | solution.py:327
  13.1 2.4 %collective-permute-start.1 = (bf16[400,1024]{1,0:T(8,128)(2,1)}, bf16[400,1024]{1,0:T(8,128)(2,1)S(1)}, u32[]{:S(2)}, u32[]{:S(2)}) collective-permute-start(bf16[400,1024]{1,0:T(8,128)(2,1)} %get-tuple-element.23), channel_id=1, source_target_pairs={{0,2},{2,4},{4,6},{6,8},{8,10},{10,12},{12,14},{14,16},{16,18},{18... | collective-permute-start | bytes 2457608 | tf_op jit(solution)/shard_map/ppermute | solution.py:330
  15.5 0.0 collective-permute-start.2
  15.6 7.4 %all-to-all-done.mine_ref = bf16[32,16,512]{2,1,0:T(8,128)(2,1)S(1)} async-done(((bf16[32,16,512]{2,1,0:T(8,128)(2,1)}), bf16[32,16,512]{2,1,0:T(8,128)(2,1)S(1)}, u32[]{:S(2)}, u32[]{:S(2)}) %all-to-all-start) | async-done | bytes 524320 | tf_op jit(solution)/shard_map/all_to_all | solution.py:327
  22.9 3.3 %collective-permute-start = (bf16[32,16,512]{2,1,0:T(8,128)(2,1)S(1)}, bf16[32,16,512]{2,1,0:T(8,128)(2,1)}, u32[]{:S(2)}, u32[]{:S(2)}) collective-permute-start(bf16[32,16,512]{2,1,0:T(8,128)(2,1)S(1)} %all-to-all-done.mine_ref), channel_id=1, source_target_pairs={{0,2},{2,0},{4,6},{6,4},{8,10},{10,8},{12,14},{14,12},{16,18},{18,... | collective-permute-start | bytes 1572872 | tf_op jit(solution)/shard_map/ppermute | solution.py:352
  26.2 0.0 copy-start.1
  26.2 0.0 copy-start.8
  26.2 0.0 copy-start.9
  26.2 1.7 %shard_map.105 = (bf16[1024,512]{1,0:T(8,128)(2,1)S(1)}, bf16[512,1024]{1,0:T(8,128)(2,1)S(1)}, bf16[384,512]{1,0:T(8,128)(2,1)S(1)}, bf16[512,384]{1,0:T(8,128)...) custom-call(s32[3,512]{1,0:T(4,128)S(1)} %copy-done.5, ...), custom_call_target="tpu_custom_call" | custom-call | flops 2147483648 | bytes 6834176 | tf_op jit(solution)/shard_map/pallas_call | solution.py:258
  28.0 3.6 %collective-permute-start.6 = (bf16[32,16,512]{2,1,0:T(8,128)(2,1)S(1)}, bf16[32,16,512]{2,1,0:T(8,128)(2,1)}, u32[]{:S(2)}, u32[]{:S(2)}) collective-permute-start(bf16[32,16,512]{2,1,0:T(8,128)(2,1)S(1)} %all-to-all-done.mine_ref), channel_id=1, source_target_pairs={{0,1},{1,0},{2,3},{3,2},{4,5},{5,4},{6,7},{7,6},{8,9},{9,8},{10,11... | collective-permute-start | bytes 1572872 | tf_op jit(solution)/shard_map/ppermute | solution.py:373
  31.6 0.0 collective-permute-done.1.prv_ref
  31.6 0.0 collective-permute-done.2.nxt_ref
  31.6 3.2 %shard_map.106 = (f32[1024,128]{1,0:T(8,128)S(1)}, f32[512,128]{1,0:T(8,128)S(1)}, bf16[1024,768]{1,0:T(8,128)(2,1)S(1)}) custom-call(f32[3,256]{1,0:T(4,128)S(1)} %copy-done.1, f32[1,256]{1,0:T(1,128)S(1)} %bitcast.7, bf16[400,1024]{1,0:T(8,128)(2,1)S(1)} %collective-permute-done.1.prv_ref, bf16[400,1024]{1,0:T(8,128)(2,1)} %collective-permute-done.2.nxt_ref, ...), custom_call_target="tpu_custom_call" | custom-call | flops 2147483648 | bytes 5841408 | tf_op jit(solution)/shard_map/pallas_call | solution.py:258
  34.9 1.1 %copy-done.4 = bf16[400,1024]{1,0:T(8,128)(2,1)S(1)} copy-done((bf16[400,1024]{1,0:T(8,128)(2,1)S(1)}, bf16[400,1024]{1,0:T(8,128)(2,1)}, u32[]{:S(2)}) %copy-start.4) | copy-done | bytes 819224
  36.0 12.0 %shard_map.107 = (bf16[1024,512]{1,0:T(8,128)(2,1)S(1)}, f32[768,512]{1,0:T(8,128)S(1)}, bf16[384,512]{1,0:T(8,128)(2,1)S(1)}, bf16[384,512]{1,0:T(8,128)(2,1)}, bf16[1024,512]{1,0:T(8,128)(2,1)}) custom-call(s32[1]{0:T(128)} %bitcast.core_ref, bf16[32,16,512]{2,1,0:T(8,128)(2,1)S(1)} %all-to-all-done.mine_ref, ...), custom_call_target="tpu_custom_call" | custom-call | flops 10737418240 | bytes 15532036 | tf_op jit(solution)/shard_map/pallas_call | solution.py:258
  48.0 1.1 %copy-done.10 = f32[768,512]{1,0:T(8,128)} copy-done((f32[768,512]{1,0:T(8,128)}, f32[768,512]{1,0:T(8,128)S(1)}, u32[]{:S(2)}) %copy-start.10) | copy-done | bytes 1572888
  49.2 3.3 %collective-permute-start.4 = (bf16[384,512]{1,0:T(8,128)(2,1)S(1)}, bf16[384,512]{1,0:T(8,128)(2,1)}, u32[]{:S(2)}, u32[]{:S(2)}) collective-permute-start(bf16[384,512]{1,0:T(8,128)(2,1)S(1)} %get-tuple-element.37), channel_id=1, source_target_pairs={{2,0},{4,2},{6,4},{8,6},{10,8},{12,10},{14,12},{16,14},{18,16},{20... | collective-permute-start | bytes 1179656 | tf_op jit(solution)/shard_map/ppermute | solution.py:367
  52.5 10.0 %all-to-all-start.1 = ((bf16[64,16,512]{2,1,0:T(8,128)(2,1)}), bf16[64,16,512]{2,1,0:T(8,128)(2,1)S(1)}, u32[]{:S(2)}, u32[]{:S(2)}) async-start(bf16[64,16,512]{2,1,0:T(8,128)(2,1)} %bitcast.5), calls=%async_computation.1 | async-start | bytes 2097152 | tf_op jit(solution)/shard_map/all_to_all | solution.py:370
  62.6 0.6 collective-permute-start.7
  63.2 0.0 collective-permute-done.3.back_prv_ref
  63.2 0.0 collective-permute-done.4.back_nxt_ref
  63.2 0.0 copy-start.11
  63.3 1.4 %copy-done.11 = f32[768,512]{1,0:T(8,128)S(1)} copy-done((f32[768,512]{1,0:T(8,128)S(1)}, f32[768,512]{1,0:T(8,128)}, u32[]{:S(2)}) %copy-start.11) | copy-done | bytes 1572888
  64.7 1.7 %shard_map.108 = (bf16[384,512]{1,0:T(8,128)(2,1)S(1)}, bf16[384,512]{1,0:T(8,128)(2,1)S(1)}) custom-call(s32[1]{0:T(128)} %bitcast.1.half_ref, s32[2,128]{1,0:T(2,128)S(1)} %copy-done.2, f32[768,512]{1,0:T(8,128)S(1)} %copy-done.11, bf16[384,512]{1,0:T(8,128)(2,1)} %collective-permute-done.3.back_prv_ref, bf16[384,512]{1,0:T(8,128)(2,1)} %collective-permute-done.4.back_nxt_ref), custom_call_target="tpu_custom_call" | custom-call | flops 21474836480 | bytes 3146756 | tf_op jit(solution)/shard_map/pallas_call | solution.py:258
  66.3 3.4 %collective-permute-start.5 = (bf16[384,512]{1,0:T(8,128)(2,1)S(1)}, bf16[384,512]{1,0:T(8,128)(2,1)S(1)}, u32[]{:S(2)}, u32[]{:S(2)}) collective-permute-start(bf16[384,512]{1,0:T(8,128)(2,1)S(1)} %get-tuple-element.40), channel_id=1, source_target_pairs={{0,1},{1,0},{2,3},{3,2},{4,5},{5,4},{6,7},{7,6},{8,9},{9,8},{10,11... | collective-permute-start | bytes 1179656 | tf_op jit(solution)/shard_map/ppermute | solution.py:381
  69.7 0.6 shard_map.109.part_ref
  70.3 0.0 collective-permute-done.7.sib_lat_ref
  70.4 17.3 %collective-permute-done.5.far_ref = bf16[384,512]{1,0:T(8,128)(2,1)S(1)} collective-permute-done((bf16[384,512]{1,0:T(8,128)(2,1)S(1)}, bf16[384,512]{1,0:T(8,128)(2,1)S(1)}, u32[]{:S(2)}, u32[]{:S(2)}) %collective-permute-start.5) | collective-permute-done | bytes 393248 | tf_op jit(solution)/shard_map/ppermute | solution.py:381
  87.6 2.9 %shard_map.110 = f32[384,1024]{1,0:T(8,128)} custom-call(s32[1]{0:T(128)} %bitcast.core_ref, bf16[384,1024]{1,0:T(8,128)(2,1)S(1)} %shard_map.109.part_ref, bf16[384,512]{1,0:T(8,128)(2,1)S(1)} %collective-permute-done.5.far_ref, bf16[32,16,512]{2,1,0:T(8,128)(2,1)} %collective-permute-done.6.core_lat_ref, ...), custom_call_target="tpu_custom_call" | custom-call | bytes 3801092 | tf_op jit(solution)/shard_map/pallas_call | solution.py:258
  90.5 0.0 all-to-all-done.1.shares_ref
  90.5 0.8 shard_map.111
  (20 shorter events, 0.0 us)
Async XLA Ops:
  0.6 25.6 %copy-start = (bf16[3,256,1024]{2,1,0:T(8,128)(2,1)S(1)}, bf16[3,256,1024]{2,1,0:T(8,128)(2,1)}, u32[]{:S(2)}) copy-start(bf16[3,256,1024]{2,1,0:T(8,128)(2,1)} %own_ref.3) | copy-start | bytes 4718596
  0.6 25.6 %copy-start.5 = (s32[3,512]{1,0:T(4,128)S(1)}, s32[3,512]{1,0:T(4,128)}, u32[]{:S(2)}) copy-start(s32[3,512]{1,0:T(4,128)} %tri_ref.1) | copy-start | bytes 18436
  0.7 25.6 %copy-start.7 = (s32[4,384]{1,0:T(4,128)S(1)}, s32[4,384]{1,0:T(4,128)}, u32[]{:S(2)}) copy-start(s32[4,384]{1,0:T(4,128)} %hin_ref.1) | copy-start | bytes 18436
  0.7 25.5 %copy-start.6 = (f32[3,512]{1,0:T(4,128)S(1)}, f32[3,512]{1,0:T(4,128)}, u32[]{:S(2)}) copy-start(f32[3,512]{1,0:T(4,128)} %sq_ref.1) | copy-start | bytes 18436
  3.9 19.0 %all-to-all-start = ((bf16[32,16,512]{2,1,0:T(8,128)(2,1)}), bf16[32,16,512]{2,1,0:T(8,128)(2,1)S(1)}, u32[]{:S(2)}, u32[]{:S(2)}) async-start(bf16[32,16,512]{2,1,0:T(8,128)(2,1)} %get-tuple-element.22), calls=%async_computation | async-start | bytes 1048576 | tf_op jit(solution)/shard_map/all_to_all | solution.py:327
  13.1 18.4 %collective-permute-start.1 = (bf16[400,1024]{1,0:T(8,128)(2,1)}, bf16[400,1024]{1,0:T(8,128)(2,1)S(1)}, u32[]{:S(2)}, u32[]{:S(2)}) collective-permute-start(bf16[400,1024]{1,0:T(8,128)(2,1)} %get-tuple-element.23), channel_id=1, source_target_pairs={{0,2},{2,4},{4,6},{6,8},{8,10},{10,12},{12,14},{14,16},{16,18},{18... | collective-permute-start | bytes 2457608 | tf_op jit(solution)/shard_map/ppermute | solution.py:330
  15.5 16.0 %collective-permute-start.2 = (bf16[400,1024]{1,0:T(8,128)(2,1)}, bf16[400,1024]{1,0:T(8,128)(2,1)}, u32[]{:S(2)}, u32[]{:S(2)}) collective-permute-start(bf16[400,1024]{1,0:T(8,128)(2,1)} %get-tuple-element.24), channel_id=1, source_target_pairs={{2,0},{4,2},{6,4},{8,6},{10,8},{12,10},{14,12},{16,14},{18,16},{20... | collective-permute-start | bytes 2457608 | tf_op jit(solution)/shard_map/ppermute | solution.py:331
  22.9 11.9 %collective-permute-start = (bf16[32,16,512]{2,1,0:T(8,128)(2,1)S(1)}, bf16[32,16,512]{2,1,0:T(8,128)(2,1)}, u32[]{:S(2)}, u32[]{:S(2)}) collective-permute-start(bf16[32,16,512]{2,1,0:T(8,128)(2,1)S(1)} %all-to-all-done.mine_ref), channel_id=1, source_target_pairs={{0,2},{2,0},{4,6},{6,4},{8,10},{10,8},{12,14},{14,12},{16,18},{18,... | collective-permute-start | bytes 1572872 | tf_op jit(solution)/shard_map/ppermute | solution.py:352
  26.2 5.4 %copy-start.1 = (f32[3,256]{1,0:T(4,128)S(1)}, f32[3,256]{1,0:T(4,128)}, u32[]{:S(2)}) copy-start(f32[3,256]{1,0:T(4,128)} %rest_ref.1) | copy-start | bytes 9220
  26.2 5.4 %copy-start.8 = (f32[3,384]{1,0:T(4,128)S(1)}, f32[3,384]{1,0:T(4,128)}, u32[]{:S(2)}) copy-start(f32[3,384]{1,0:T(4,128)} %bend_ref.1) | copy-start | bytes 13828
  26.2 5.4 %copy-start.9 = (f32[256]{0:T(256)S(1)}, f32[256]{0:T(256)}, u32[]{:S(2)}) copy-start(f32[256]{0:T(256)} %param.16) | copy-start | bytes 3076
  28.0 34.6 %collective-permute-start.6 = (bf16[32,16,512]{2,1,0:T(8,128)(2,1)S(1)}, bf16[32,16,512]{2,1,0:T(8,128)(2,1)}, u32[]{:S(2)}, u32[]{:S(2)}) collective-permute-start(bf16[32,16,512]{2,1,0:T(8,128)(2,1)S(1)} %all-to-all-done.mine_ref), channel_id=1, source_target_pairs={{0,1},{1,0},{2,3},{3,2},{4,5},{5,4},{6,7},{7,6},{8,9},{9,8},{10,11... | collective-permute-start | bytes 1572872 | tf_op jit(solution)/shard_map/ppermute | solution.py:373
  31.6 3.3 %copy-start.3 = (bf16[400,1024]{1,0:T(8,128)(2,1)}, bf16[400,1024]{1,0:T(8,128)(2,1)S(1)}, u32[]{:S(2)}) copy-start(bf16[400,1024]{1,0:T(8,128)(2,1)S(1)} %collective-permute-done.1.prv_ref) | copy-start | bytes 2457604
  34.9 1.1 %copy-start.4 = (bf16[400,1024]{1,0:T(8,128)(2,1)S(1)}, bf16[400,1024]{1,0:T(8,128)(2,1)}, u32[]{:S(2)}) copy-start(bf16[400,1024]{1,0:T(8,128)(2,1)} %copy-done.3) | copy-start | bytes 2457604
  48.0 1.1 %copy-start.10 = (f32[768,512]{1,0:T(8,128)}, f32[768,512]{1,0:T(8,128)S(1)}, u32[]{:S(2)}) copy-start(f32[768,512]{1,0:T(8,128)S(1)} %get-tuple-element.35.f_own_ref) | copy-start | bytes 4718596
  49.2 14.1 %copy-start.2 = (s32[2,128]{1,0:T(2,128)S(1)}, s32[2,128]{1,0:T(2,128)}, u32[]{:S(2)}) copy-start(s32[2,128]{1,0:T(2,128)} %send_ref.1) | copy-start | bytes 3076
  49.2 14.1 %collective-permute-start.3 = (bf16[384,512]{1,0:T(8,128)(2,1)}, bf16[384,512]{1,0:T(8,128)(2,1)}, u32[]{:S(2)}, u32[]{:S(2)}) collective-permute-start(bf16[384,512]{1,0:T(8,128)(2,1)} %get-tuple-element.36), channel_id=1, source_target_pairs={{0,2},{2,4},{4,6},{6,8},{8,10},{10,12},{12,14},{14,16},{16,18},{18... | collective-permute-start | bytes 1179656 | tf_op jit(solution)/shard_map/ppermute | solution.py:368
  49.2 14.1 %collective-permute-start.4 = (bf16[384,512]{1,0:T(8,128)(2,1)S(1)}, bf16[384,512]{1,0:T(8,128)(2,1)}, u32[]{:S(2)}, u32[]{:S(2)}) collective-permute-start(bf16[384,512]{1,0:T(8,128)(2,1)S(1)} %get-tuple-element.37), channel_id=1, source_target_pairs={{2,0},{4,2},{6,4},{8,6},{10,8},{12,10},{14,12},{16,14},{18,16},{20... | collective-permute-start | bytes 1179656 | tf_op jit(solution)/shard_map/ppermute | solution.py:367
  52.5 38.0 %all-to-all-start.1 = ((bf16[64,16,512]{2,1,0:T(8,128)(2,1)}), bf16[64,16,512]{2,1,0:T(8,128)(2,1)S(1)}, u32[]{:S(2)}, u32[]{:S(2)}) async-start(bf16[64,16,512]{2,1,0:T(8,128)(2,1)} %bitcast.5), calls=%async_computation.1 | async-start | bytes 2097152 | tf_op jit(solution)/shard_map/all_to_all | solution.py:370
  62.6 7.8 %collective-permute-start.7 = (bf16[32,16,512]{2,1,0:T(8,128)(2,1)}, bf16[32,16,512]{2,1,0:T(8,128)(2,1)S(1)}, u32[]{:S(2)}, u32[]{:S(2)}) collective-permute-start(bf16[32,16,512]{2,1,0:T(8,128)(2,1)} %collective-permute-done.6.core_lat_ref), channel_id=1, source_target_pairs={{0,2},{2,0},{4,6},{6,4},{8,10},{10,8},{12,14},{14,12},{16,18},{18,... | collective-permute-start | bytes 1572872 | tf_op jit(solution)/shard_map/ppermute | solution.py:374
  63.2 1.4 %copy-start.11 = (f32[768,512]{1,0:T(8,128)S(1)}, f32[768,512]{1,0:T(8,128)}, u32[]{:S(2)}) copy-start(f32[768,512]{1,0:T(8,128)} %copy-done.10) | copy-start | bytes 4718596
  66.3 21.3 %collective-permute-start.5 = (bf16[384,512]{1,0:T(8,128)(2,1)S(1)}, bf16[384,512]{1,0:T(8,128)(2,1)S(1)}, u32[]{:S(2)}, u32[]{:S(2)}) collective-permute-start(bf16[384,512]{1,0:T(8,128)(2,1)S(1)} %get-tuple-element.40), channel_id=1, source_target_pairs={{0,1},{1,0},{2,3},{3,2},{4,5},{5,4},{6,7},{7,6},{8,9},{9,8},{10,11... | collective-permute-start | bytes 1179656 | tf_op jit(solution)/shard_map/ppermute | solution.py:381

commit v3 on v2

--- a/solution.py
+++ b/solution.py
@@ -48,15 +48,12 @@
         out_ref[pl.ds(pl.multiple_of((2 * i + 1 - core) * each, each), each), :] = other_ref[i]
 
 
-def send(ref):
-    if isinstance(ref, Stored):
-        ref.send()
-
-
-def first_kernel(shard_ref, send_ref, basis_ref, rest_ref, copies_ref, prev_ref, next_ref):
+def copies_kernel(shard_ref, copies_ref):
     for i in range(copies_ref.shape[0]):
         copies_ref[i] = shard_ref[...]
-    send(copies_ref)
+
+
+def rows_kernel(send_ref, basis_ref, rest_ref, prev_ref, next_ref):
     own, halo = basis_ref.shape[1], send_ref.shape[1]
     rest = rest_ref[...]
     parts = []
@@ -72,7 +69,6 @@
             out[c * halo : (c + 1) * halo, :] = dot(sel, basis_ref[c], TN).astype(BF)
         out[3 * halo :, :] = jnp.zeros((out.shape[0] - 3 * halo, out.shape[1]), BF)
         out[3 * halo :, :halo] = dot(parts, sel).astype(BF)
-        send(out)
 
 
 def own_kernel(
@@ -122,7 +118,7 @@
     frames, step,
     core_ref, mine_ref, sib_ref, own_ref, prv_ref, nxt_ref, d_ref, dt_ref, lap_ref, edge_ref,
     vert_ref, sq_ref, own_t_ref, halo_t_ref,
-    lat_ref, f_own_ref, f_prv_ref, f_nxt_ref, lg_ref, f_all_ref,
+    lat_ref, f_own_ref, f_prv_ref, f_nxt_ref, keep_ref, give_ref, f_all_ref,
 ):
     own_n = own_ref.shape[1]
     t = sq_ref.shape[0]
@@ -170,10 +166,21 @@
                 (3 * (own_n + halo) + c * halo, halo, own_n + halo),
             ):
                 f_all_ref[at_row : at_row + size, here] = short[first : first + size]
-    for at in range(0, lg_ref.shape[0], 256):
+    each = mine_ref.shape[1]
+    first = core_ref[0] == 0
+    for at in range(0, lat_ref.shape[0], 256):
         rows = slice(at, at + 256)
         both = jnp.concatenate([own_t_ref[rows, :], halo_t_ref[rows, :]], axis=1)
-        lg_ref[rows, :] = dot(both, f_all_ref[...]).astype(BF)
+        block = dot(both, f_all_ref[...])
+        for i in range(0, 256, 2 * each):
+            low, high = block[i : i + each], block[i + each : i + 2 * each]
+            chip = (at + i) // (2 * each)
+            keep_ref[chip] = jnp.where(first, low, high).astype(BF)
+            give_ref[chip] = jnp.where(first, high, low).astype(BF)
+
+
+def pair_kernel(a_ref, b_ref, out_ref):
+    out_ref[...] = (a_ref[...].astype(F32) + b_ref[...].astype(F32)).astype(BF)
 
 
 def share_kernel(shares_ref, out_ref):
@@ -201,47 +208,22 @@
         other_ref[c * half : (c + 1) * half, :] = jnp.where(first, high, low).astype(BF)
 
 
-def own_part_kernel(mine_ref, lat_ref, out_ref):
+def own_part_far_kernel(core_ref, mine_ref, lat_ref, core_lat_ref, sib_lat_ref, out_ref, far_lat_ref):
+    interleave(core_ref[0], core_lat_ref, sib_lat_ref, far_lat_ref)
     out_ref[...] = dot(mine_ref[...], lat_ref[...], NT).astype(BF)
 
 
-def basis_grad_kernel(core_ref, part_ref, far_ref, core_lat_ref, sib_lat_ref, out_ref, lat_ref):
-    interleave(core_ref[0], core_lat_ref, sib_lat_ref, lat_ref)
-    far = dot(far_ref[...], lat_ref[...], NT).astype(BF).astype(F32)
-    out_ref[...] = part_ref[...].astype(F32) + far
-
-
-class Loaded:
-    def __init__(self, source, ref, sem):
-        self.ref, self.copy = ref, pltpu.make_async_copy(source, ref, sem)
-        self.shape, self.waiting = ref.shape, True
-        self.copy.start()
-
-    def wait(self):
-        if self.waiting:
-            self.copy.wait()
-            self.waiting = False
-
-    def __getitem__(self, index):
-        self.wait()
-        return self.ref[index]
-
-
-class Stored:
-    def __init__(self, ref, target, sem):
-        self.ref, self.copy = ref, pltpu.make_async_copy(ref, target, sem)
-        self.shape, self.open = ref.shape, True
-
-    def __setitem__(self, index, value):
-        self.ref[index] = value
-
-    def __getitem__(self, index):
-        return self.ref[index]
-
-    def send(self):
-        if self.open:
-            self.copy.start()
-            self.open = False
+def last_kernel(part_ref, far_ref, lat_ref, done_ref, out_ref, sum_ref, sem):
+    third = out_ref.shape[0] // 3
+    copies = []
+    for c in range(3):
+        rows = slice(c * third, (c + 1) * third)
+        far = dot(far_ref[rows, :], lat_ref[...], NT).astype(BF).astype(F32)
+        sum_ref[rows, :] = part_ref[rows, :].astype(F32) + far
+        copies.append(pltpu.make_async_copy(sum_ref.at[rows], out_ref.at[rows], sem.at[c]))
+        copies[-1].start()
+    for copy in copies:
+        copy.wait()
 
 
 SMEM = pl.BlockSpec(memory_space=pltpu.SMEM)
@@ -249,52 +231,17 @@
 VMEM = pl.BlockSpec(memory_space=pltpu.VMEM)
 
 
-def call(kernel, outs, *args, scalars=0, direct=True, near=(), scratch=(), macs=0, room=0):
+def call(kernel, outs, *args, scalars=0, macs=0, room=24, scratch=()):
     moved = sum(a.size * a.dtype.itemsize for a in args)
     moved += sum(math.prod(s) * jnp.dtype(d).itemsize for s, d in outs)
-    ins, n_in, n_out = args[scalars:], len(args) - scalars, len(outs)
-    params = pltpu.CompilerParams(vmem_limit_bytes=(room or 24) << 20)
-    if direct:
-        return pl.pallas_call(
-            kernel,
-            cost_estimate=pl.CostEstimate(flops=2 * macs, bytes_accessed=moved, transcendentals=0),
-            in_specs=[SMEM] * scalars + [VMEM] * n_in,
-            out_specs=[VMEM] * n_out,
-            out_shape=[jax.ShapeDtypeStruct(s, d) for s, d in outs],
-            scratch_shapes=list(scratch),
-            compiler_params=params,
-        )(*args)
-    far = [i for i in range(n_in) if i + scalars not in near]
-    n_far = len(far)
-
-    def body(*refs):
-        numbers, refs = refs[:scalars], refs[scalars:]
-        sources, targets, refs = refs[:n_in], refs[n_in : n_in + n_out], refs[n_in + n_out :]
-        held, made, refs = refs[:n_far], refs[n_far : n_far + n_out], refs[n_far + n_out :]
-        in_sem, out_sem, *rest = refs
-        loads = list(sources)
-        for i, at in enumerate(far):
-            loads[at] = Loaded(sources[at], held[i], in_sem.at[i])
-        stores = [Stored(v, x, out_sem.at[i]) for i, (x, v) in enumerate(zip(targets, made))]
-        kernel(*numbers, *loads, *stores, *rest)
-        for at in far:
-            loads[at].wait()
-        for store in stores:
-            store.send()
-        for store in stores:
-            store.copy.wait()
-
     return pl.pallas_call(
-        body,
+        kernel,
         cost_estimate=pl.CostEstimate(flops=2 * macs, bytes_accessed=moved, transcendentals=0),
-        in_specs=[SMEM] * scalars + [ANY if i in far else VMEM for i in range(n_in)],
-        out_specs=[ANY] * n_out,
+        in_specs=[SMEM] * scalars + [VMEM] * (len(args) - scalars),
+        out_specs=[VMEM] * len(outs),
         out_shape=[jax.ShapeDtypeStruct(s, d) for s, d in outs],
-        scratch_shapes=[pltpu.VMEM(ins[i].shape, ins[i].dtype) for i in far]
-        + [pltpu.VMEM(s, d) for s, d in outs]
-        + [pltpu.SemaphoreType.DMA((max(n_far, 1),)), pltpu.SemaphoreType.DMA((n_out,))]
-        + list(scratch),
-        compiler_params=params,
+        scratch_shapes=list(scratch),
+        compiler_params=pltpu.CompilerParams(vmem_limit_bytes=room << 20),
     )(*args)
 
 
@@ -320,9 +267,9 @@
     half_index = lax.axis_index("frame").astype(jnp.int32).reshape(1)
 
     sent = ((3 * halo + 16, width), BF)
-    copies, rows_prev, rows_next = call(
-        first_kernel, [((chips, each, frames), BF), sent, sent],
-        latents.T, send_rows, basis, rest_pos, direct=False, room=60,
+    [copies] = call(copies_kernel, [((chips, each, frames), BF)], latents.T)
+    rows_prev, rows_next = call(
+        rows_kernel, [sent, sent], send_rows, basis, rest_pos, room=48
     )
     lat_core = lax.all_to_all(
         copies, "patch", 0, 0, tiled=True, axis_index_groups=same_core
@@ -350,14 +297,15 @@
         macs=1 << 30,
     )
     lat_sib = lax.ppermute(lat_core, "patch", sibling)
-    lat_all, f_own, f_prv, f_nxt, lg = call(
+    lat_all, f_own, f_prv, f_nxt, keep, give = call(
         functools.partial(elastic_kernel, total_frames, min(frames, 256)),
         [
             ((width, frames), BF),
             ((3 * own, frames), F32),
             ((3 * halo, frames), BF),
             ((3 * halo, frames), BF),
-            ((width, frames), BF),
+            ((chips, each, frames), BF),
+            ((chips, each, frames), BF),
         ],
         core, lat_core, lat_sib, basis, halo_prv, halo_nxt, d, dt, lap, edge, vert, sq,
         own_t, halo_t,
@@ -367,7 +315,9 @@
     back_nxt = lax.ppermute(f_prv, "patch", backward)
     back_prv = lax.ppermute(f_nxt, "patch", onward)
 
-    shares = lax.all_to_all(lg.reshape(patches, each, frames), "patch", 0, 0, tiled=True)
+    got = lax.ppermute(give, "patch", sibling)
+    [pair] = call(pair_kernel, [((chips, each, frames), BF)], keep, got)
+    shares = lax.all_to_all(pair, "patch", 0, 0, tiled=True, axis_index_groups=same_core)
     [latent_grad] = call(share_kernel, [((each, frames), F32)], shares)
 
     far_core = lax.ppermute(lat_core, "frame", partner)
@@ -379,11 +329,18 @@
         scalars=1, macs=10 << 30,
     )
     received = lax.ppermute(other, "frame", partner)
-    [part] = call(own_part_kernel, [((3 * half, width), BF)], mine, lat_all, macs=3 * half * width * frames)
-    [basis_grad] = call(
-        basis_grad_kernel, [((3 * half, width), F32)], core, part, received, far_core, far_sib,
-        scalars=1, scratch=[pltpu.VMEM((width, frames), BF)],
-    )
+    part, lat_far = call(
+        own_part_far_kernel, [((3 * half, width), BF), ((width, frames), BF)],
+        core, mine, lat_all, far_core, far_sib, scalars=1, macs=3 * half * width * frames,
+    )
+    basis_grad = pl.pallas_call(
+        last_kernel,
+        in_specs=[VMEM, VMEM, VMEM, pl.BlockSpec(memory_space=pltpu.HBM)],
+        out_specs=pl.BlockSpec(memory_space=pl.ANY),
+        out_shape=jax.ShapeDtypeStruct((3 * half, width), F32),
+        scratch_shapes=[pltpu.VMEM((3 * half, width), F32), pltpu.SemaphoreType.DMA((3,))],
+        compiler_params=pltpu.CompilerParams(vmem_limit_bytes=24 << 20),
+    )(part, received, lat_far, latent_grad)
     return basis_grad.reshape(3, half, width), latent_grad.T
 
 

time: 91.8 us -> 88.8 us (0.967)
  waiting for transfers between devices: 24.7 us -> 14.7 us
  local copies, waits for them, and re-layouts: 3.73 us -> 8.98 us
  Pallas kernels: 26.2 us -> 28.5 us
  starting transfers between devices: 35.9 us -> 34.9 us
    ppermute x1, waiting for transfers between devices: 17.3 us -> 8.62 us  [local(): received = lax.ppermute(other, 'frame', partner)]
    all_to_all x1, starting transfers between devices: 10 us -> 3.89 us  [local(): lax.all_to_all(pair, 'patch', 0, 0, tiled=True, axis_index_groups=same_core)]
    unnamed x24 -> x36, local copies, waits for them, and re-layouts: 3.73 us -> 8.98 us
    ppermute x1, starting transfers between devices: 0.65 us -> 5.46 us  [local(): far_sib = lax.ppermute(far_core, 'patch', sibling)]
    ppermute x0 -> x1, starting transfers between devices: none -> 3.54 us  [local(): got = lax.ppermute(give, 'patch', sibling)]
    ppermute x1, starting transfers between devices: 3.34 us -> 0.51 us  [local(): back_nxt = lax.ppermute(f_prv, 'patch', backward)]
    pallas_call x7 -> x9, Pallas kernels: 22.9 us -> 25.5 us  [call(): pl.pallas_call(kernel, cost_estimate=pl.CostEstimate(flops=2 * macs, byte...]
    all_to_all x1, waiting for transfers between devices: 7.38 us -> 5.81 us  [local(): lax.all_to_all(copies, 'patch', 0, 0, tiled=True, axis_index_groups=same_...]
  transfers between devices with their start and end apart: 10 -> 11, of which waited for: 2 -> 3; matrix products, arithmetic and copies ran while one was open for 0% -> 0% of each run, Pallas kernels for 24% -> 28%
where the time goes in v3:
time: 88.8 us; the launch traced here: 88 us
  starting transfers between devices  34.9 us (39%)
  Pallas kernels  28.5 us (32%)
  waiting for transfers between devices  14.7 us (17%)
  local copies, waits for them, and re-layouts  8.98 us (10%)
  between operations  0.98 us (1%)
    pallas_call x9, Pallas kernels, call(): pl.pallas_call(kernel, cost_estimate=pl.CostEstimate(flops=2 * macs, byte...  25.5 us
    all_to_all x1, starting transfers between devices, local(): lax.all_to_all(copies, 'patch', 0, 0, tiled=True, axis_index_groups=same_...  9.35 us
    unnamed x36, local copies, waits for them, and re-layouts  8.98 us
    ppermute x1, waiting for transfers between devices, local(): received = lax.ppermute(other, 'frame', partner)  8.62 us
    all_to_all x1, waiting for transfers between devices, local(): lax.all_to_all(copies, 'patch', 0, 0, tiled=True, axis_index_groups=same_...  5.81 us
    ppermute x1, starting transfers between devices, local(): far_sib = lax.ppermute(far_core, 'patch', sibling)  5.46 us
    all_to_all x1, starting transfers between devices, local(): lax.all_to_all(pair, 'patch', 0, 0, tiled=True, axis_index_groups=same_core)  3.89 us
    ppermute x1, starting transfers between devices, local(): far_core = lax.ppermute(lat_core, 'frame', partner)  3.56 us
  transfers between devices with their start and end apart: 11, of which 3 were waited for; matrix products, arithmetic and copies ran while one was open for 0% of the time, Pallas kernels for 28%

profile of v3, /device:TPU:1, one launch (start us, length us, event | category | flops | bytes accessed | tf_op | source)
XLA Modules:
  0.0 88.0 jit_solution(8922239298266229235)
XLA Ops:
  0.7 0.8 copy-done.4
  1.5 0.8 shard_map.104
  2.3 9.4 %all-to-all-start = ((bf16[32,16,512]{2,1,0:T(8,128)(2,1)}), bf16[32,16,512]{2,1,0:T(8,128)(2,1)}, u32[]{:S(2)}, u32[]{:S(2)}) async-start(bf16[32,16,512]{2,1,0:T(8,128)(2,1)} %shard_map.104), calls=%async_computation | async-start | bytes 1048576 | tf_op jit(solution)/shard_map/all_to_all | solution.py:274
  11.7 1.7 %shard_map.105 = (bf16[400,1024]{1,0:T(8,128)(2,1)}, bf16[400,1024]{1,0:T(8,128)(2,1)}) custom-call(s32[2,128]{1,0:T(2,128)S(1)} %copy-done.6, bf16[3,256,1024]{2,1,0:T(8,128)(2,1)S(1)} %copy-done, f32[3,256]{1,0:T(4,128)S(1)} %copy-done.5), custom_call_target="tpu_custom_call" | custom-call | bytes 3215360 | tf_op jit(solution)/shard_map/pallas_call | solution.py:237
  13.4 2.3 %collective-permute-start.1 = (bf16[400,1024]{1,0:T(8,128)(2,1)}, bf16[400,1024]{1,0:T(8,128)(2,1)S(1)}, u32[]{:S(2)}, u32[]{:S(2)}) collective-permute-start(bf16[400,1024]{1,0:T(8,128)(2,1)} %get-tuple-element.24), channel_id=1, source_target_pairs={{0,2},{2,4},{4,6},{6,8},{8,10},{10,12},{12,14},{14,16},{16,18},{18... | collective-permute-start | bytes 2457608 | tf_op jit(solution)/shard_map/ppermute | solution.py:277
  15.7 5.8 %all-to-all-done.mine_ref = bf16[32,16,512]{2,1,0:T(8,128)(2,1)} async-done(((bf16[32,16,512]{2,1,0:T(8,128)(2,1)}), bf16[32,16,512]{2,1,0:T(8,128)(2,1)}, u32[]{:S(2)}, u32[]{:S(2)}) %all-to-all-start) | async-done | bytes 524320 | tf_op jit(solution)/shard_map/all_to_all | solution.py:274
  21.5 3.0 %collective-permute-start = (bf16[32,16,512]{2,1,0:T(8,128)(2,1)}, bf16[32,16,512]{2,1,0:T(8,128)(2,1)S(1)}, u32[]{:S(2)}, u32[]{:S(2)}) collective-permute-start(bf16[32,16,512]{2,1,0:T(8,128)(2,1)} %all-to-all-done.mine_ref), channel_id=1, source_target_pairs={{0,2},{2,0},{4,6},{6,4},{8,10},{10,8},{12,14},{14,12},{16,18},{18,... | collective-permute-start | bytes 1572872 | tf_op jit(solution)/shard_map/ppermute | solution.py:299
  24.5 0.0 copy-start.15
  24.5 1.7 %shard_map.106 = (bf16[1024,512]{1,0:T(8,128)(2,1)S(1)}, bf16[512,1024]{1,0:T(8,128)(2,1)S(1)}, bf16[384,512]{1,0:T(8,128)(2,1)S(1)}, bf16[512,384]{1,0:T(8,128)...) custom-call(s32[3,512]{1,0:T(4,128)S(1)} %copy-done.11, ...), custom_call_target="tpu_custom_call" | custom-call | flops 2147483648 | bytes 6834176 | tf_op jit(solution)/shard_map/pallas_call | solution.py:237
  26.2 3.6 %collective-permute-start.5 = (bf16[32,16,512]{2,1,0:T(8,128)(2,1)}, bf16[32,16,512]{2,1,0:T(8,128)(2,1)}, u32[]{:S(2)}, u32[]{:S(2)}) collective-permute-start(bf16[32,16,512]{2,1,0:T(8,128)(2,1)} %all-to-all-done.mine_ref), channel_id=1, source_target_pairs={{0,1},{1,0},{2,3},{3,2},{4,5},{5,4},{6,7},{7,6},{8,9},{9,8},{10,11... | collective-permute-start | bytes 1572872 | tf_op jit(solution)/shard_map/ppermute | solution.py:323
  29.8 3.3 %shard_map.107 = (f32[1024,128]{1,0:T(8,128)S(1)}, f32[512,128]{1,0:T(8,128)S(1)}, bf16[1024,768]{1,0:T(8,128)(2,1)S(1)}) custom-call(f32[3,256]{1,0:T(4,128)S(1)} %copy-done.5, f32[1,256]{1,0:T(1,128)S(1)} %bitcast.8, bf16[400,1024]{1,0:T(8,128)(2,1)S(1)} %collective-permute-done.1.prv_ref, bf16[400,1024]{1,0:T(8,128)(2,1)} %collective-permute-done.2.nxt_ref, ...), custom_call_target="tpu_custom_call" | custom-call | flops 2147483648 | bytes 5841408 | tf_op jit(solution)/shard_map/pallas_call | solution.py:237
  33.1 0.8 copy-done.9
  33.9 1.1 %copy-done.8 = bf16[400,1024]{1,0:T(8,128)(2,1)S(1)} copy-done((bf16[400,1024]{1,0:T(8,128)(2,1)S(1)}, bf16[400,1024]{1,0:T(8,128)(2,1)}, u32[]{:S(2)}) %copy-start.8) | copy-done | bytes 819224
  35.1 1.0 %copy-done.10 = bf16[32,16,512]{2,1,0:T(8,128)(2,1)S(1)} copy-done((bf16[32,16,512]{2,1,0:T(8,128)(2,1)S(1)}, bf16[32,16,512]{2,1,0:T(8,128)(2,1)}, u32[]{:S(2)}) %copy-start.10) | copy-done | bytes 524312
  36.1 12.3 %shard_map.108 = (bf16[1024,512]{1,0:T(8,128)(2,1)S(1)}, f32[768,512]{1,0:T(8,128)S(1)}, bf16[384,512]{1,0:T(8,128)(2,1)S(1)}, bf16[384,512]{1,0:T(8,128)(2,1)},...) custom-call(s32[1]{0:T(128)} %bitcast.core_ref, bf16[32,16,512]{2,1,0:T(8,128)(2,1)} %all-to-all-done.mine_ref, ...), custom_call_target="tpu_custom_call" | custom-call | flops 10737418240 | bytes 15532036 | tf_op jit(solution)/shard_map/pallas_call | solution.py:237
  48.5 1.1 %copy-done.16 = f32[768,512]{1,0:T(8,128)} copy-done((f32[768,512]{1,0:T(8,128)}, f32[768,512]{1,0:T(8,128)S(1)}, u32[]{:S(2)}) %copy-start.16) | copy-done | bytes 1572888
  49.6 3.5 %collective-permute-start.8 = (bf16[32,16,512]{2,1,0:T(8,128)(2,1)}, bf16[32,16,512]{2,1,0:T(8,128)(2,1)S(1)}, u32[]{:S(2)}, u32[]{:S(2)}) collective-permute-start(bf16[32,16,512]{2,1,0:T(8,128)(2,1)} %get-tuple-element.45), channel_id=1, source_target_pairs={{0,2},{2,0},{4,6},{6,4},{8,10},{10,8},{12,14},{14,12},{16,18},{18,... | collective-permute-start | bytes 1572872 | tf_op jit(solution)/shard_map/ppermute | solution.py:318
  53.1 0.5 collective-permute-start.4
  53.6 5.5 %collective-permute-start.6 = (bf16[32,16,512]{2,1,0:T(8,128)(2,1)}, bf16[32,16,512]{2,1,0:T(8,128)(2,1)S(1)}, u32[]{:S(2)}, u32[]{:S(2)}) collective-permute-start(bf16[32,16,512]{2,1,0:T(8,128)(2,1)} %collective-permute-done.5.core_lat_ref), channel_id=1, source_target_pairs={{0,2},{2,0},{4,6},{6,4},{8,10},{10,8},{12,14},{14,12},{16,18},{18,... | collective-permute-start | bytes 1572872 | tf_op jit(solution)/shard_map/ppermute | solution.py:324
  59.1 0.9 %shard_map.111 = bf16[32,16,512]{2,1,0:T(8,128)(2,1)} custom-call(bf16[32,16,512]{2,1,0:T(8,128)(2,1)S(1)} %get-tuple-element.44.a_ref, bf16[32,16,512]{2,1,0:T(8,128)(2,1)S(1)} %collective-permute-done.8.b_ref), custom_call_target="tpu_custom_call" | custom-call | bytes 1572864 | tf_op jit(solution)/shard_map/pallas_call | solution.py:237
  60.0 3.9 %all-to-all-start.1 = ((bf16[32,16,512]{2,1,0:T(8,128)(2,1)}), bf16[32,16,512]{2,1,0:T(8,128)(2,1)S(1)}, u32[]{:S(2)}, u32[]{:S(2)}) async-start(bf16[32,16,512]{2,1,0:T(8,128)(2,1)} %shard_map.111), calls=%async_computation.1 | async-start | bytes 1048576 | tf_op jit(solution)/shard_map/all_to_all | solution.py:320
  64.0 1.4 %copy-done.17 = f32[768,512]{1,0:T(8,128)S(1)} copy-done((f32[768,512]{1,0:T(8,128)S(1)}, f32[768,512]{1,0:T(8,128)}, u32[]{:S(2)}) %copy-start.17) | copy-done | bytes 1572888
  65.4 2.4 %shard_map.109 = (bf16[384,512]{1,0:T(8,128)(2,1)S(1)}, bf16[384,512]{1,0:T(8,128)(2,1)}) custom-call(s32[1]{0:T(128)} %bitcast.1.half_ref, s32[2,128]{1,0:T(2,128)S(1)} %copy-done.6, f32[768,512]{1,0:T(8,128)S(1)} %copy-done.17, bf16[384,512]{1,0:T(8,128)(2,1)S(1)} %collective-permute-done.3.back_prv_ref, bf16[384,512]{1,0:T(8,128)(2,1)} %collective-permute-done.4.back_nxt_ref), custom_call_target="tpu_custom_call" | custom-call | flops 21474836480 | bytes 3146756 | tf_op jit(solution)/shard_map/pallas_call | solution.py:237
  67.7 3.3 %collective-permute-start.7 = (bf16[384,512]{1,0:T(8,128)(2,1)}, bf16[384,512]{1,0:T(8,128)(2,1)}, u32[]{:S(2)}, u32[]{:S(2)}) collective-permute-start(bf16[384,512]{1,0:T(8,128)(2,1)} %get-tuple-element.42), channel_id=1, source_target_pairs={{0,1},{1,0},{2,3},{3,2},{4,5},{5,4},{6,7},{7,6},{8,9},{9,8},{10,11... | collective-permute-start | bytes 1179656 | tf_op jit(solution)/shard_map/ppermute | solution.py:331
  71.0 0.8 copy-done.1
  71.8 1.0 %copy-done.2 = bf16[32,16,512]{2,1,0:T(8,128)(2,1)S(1)} copy-done((bf16[32,16,512]{2,1,0:T(8,128)(2,1)S(1)}, bf16[32,16,512]{2,1,0:T(8,128)(2,1)}, u32[]{:S(2)}) %copy-start.2) | copy-done | bytes 524312
  72.9 1.7 %shard_map.110 = (bf16[384,1024]{1,0:T(8,128)(2,1)S(1)}, bf16[1024,512]{1,0:T(8,128)(2,1)S(1)}) custom-call(s32[1]{0:T(128)} %bitcast.core_ref, bf16[384,512]{1,0:T(8,128)(2,1)S(1)} %get-tuple-element.39.mine_ref, bf16[1024,512]{1,0:T(8,128)(2,1)S(1)} %get-tuple-element.40.lat_ref, bf16[32,16,512]{2,1,0:T(8,128)(2,1)} %collective-permute-done.5.core_lat_ref, ...), custom_call_target="tpu_custom_call" | custom-call | flops 402653184 | bytes 4325380 | tf_op jit(solution)/shard_map/pallas_call | solution.py:237
  74.6 0.3 all-to-all-done.1.shares_ref
  74.8 0.7 shard_map.112.done_ref
  75.5 8.6 %collective-permute-done.7.far_ref = bf16[384,512]{1,0:T(8,128)(2,1)} collective-permute-done((bf16[384,512]{1,0:T(8,128)(2,1)}, bf16[384,512]{1,0:T(8,128)(2,1)}, u32[]{:S(2)}, u32[]{:S(2)}) %collective-permute-start.7) | collective-permute-done | bytes 393248 | tf_op jit(solution)/shard_map/ppermute | solution.py:331
  84.1 0.8 copy-done.3
  84.9 3.0 %shard_map.113 = f32[384,1024]{1,0:T(8,128)} custom-call(bf16[384,1024]{1,0:T(8,128)(2,1)S(1)} %get-tuple-element.41.part_ref, bf16[384,512]{1,0:T(8,128)(2,1)} %collective-permute-done.7.far_ref, bf16[1024,512]{1,0:T(8,128)(2,1)S(1)} %get-tuple-element.43.lat_ref, f32[16,512]{1,0:T(8,128)S(1)} %copy-done.3), custom_call_target="tpu_custom_call" | custom-call | tf_op jit(solution)/shard_map/pallas_call | solution.py:336
  (36 shorter events, 0.1 us)
Async XLA Ops:
  0.6 11.1 %copy-start = (bf16[3,256,1024]{2,1,0:T(8,128)(2,1)S(1)}, bf16[3,256,1024]{2,1,0:T(8,128)(2,1)}, u32[]{:S(2)}) copy-start(bf16[3,256,1024]{2,1,0:T(8,128)(2,1)} %own_ref.3) | copy-start | bytes 4718596
  0.6 0.8 copy-start.4
  1.5 10.2 %copy-start.5 = (f32[3,256]{1,0:T(4,128)S(1)}, f32[3,256]{1,0:T(4,128)}, u32[]{:S(2)}) copy-start(f32[3,256]{1,0:T(4,128)} %rest_ref.3) | copy-start | bytes 9220
  1.5 10.2 %copy-start.6 = (s32[2,128]{1,0:T(2,128)S(1)}, s32[2,128]{1,0:T(2,128)}, u32[]{:S(2)}) copy-start(s32[2,128]{1,0:T(2,128)} %send_ref.3) | copy-start | bytes 3076
  1.5 23.0 %copy-start.11 = (s32[3,512]{1,0:T(4,128)S(1)}, s32[3,512]{1,0:T(4,128)}, u32[]{:S(2)}) copy-start(s32[3,512]{1,0:T(4,128)} %tri_ref.1) | copy-start | bytes 18436
  1.5 23.0 %copy-start.12 = (f32[3,512]{1,0:T(4,128)S(1)}, f32[3,512]{1,0:T(4,128)}, u32[]{:S(2)}) copy-start(f32[3,512]{1,0:T(4,128)} %sq_ref.1) | copy-start | bytes 18436
  1.5 23.0 %copy-start.13 = (s32[4,384]{1,0:T(4,128)S(1)}, s32[4,384]{1,0:T(4,128)}, u32[]{:S(2)}) copy-start(s32[4,384]{1,0:T(4,128)} %hin_ref.1) | copy-start | bytes 18436
  2.3 19.1 %all-to-all-start = ((bf16[32,16,512]{2,1,0:T(8,128)(2,1)}), bf16[32,16,512]{2,1,0:T(8,128)(2,1)}, u32[]{:S(2)}, u32[]{:S(2)}) async-start(bf16[32,16,512]{2,1,0:T(8,128)(2,1)} %shard_map.104), calls=%async_computation | async-start | bytes 1048576 | tf_op jit(solution)/shard_map/all_to_all | solution.py:274
  13.4 16.4 %collective-permute-start.1 = (bf16[400,1024]{1,0:T(8,128)(2,1)}, bf16[400,1024]{1,0:T(8,128)(2,1)S(1)}, u32[]{:S(2)}, u32[]{:S(2)}) collective-permute-start(bf16[400,1024]{1,0:T(8,128)(2,1)} %get-tuple-element.24), channel_id=1, source_target_pairs={{0,2},{2,4},{4,6},{6,8},{8,10},{10,12},{12,14},{14,16},{16,18},{18... | collective-permute-start | bytes 2457608 | tf_op jit(solution)/shard_map/ppermute | solution.py:277
  15.7 14.2 %collective-permute-start.2 = (bf16[400,1024]{1,0:T(8,128)(2,1)}, bf16[400,1024]{1,0:T(8,128)(2,1)}, u32[]{:S(2)}, u32[]{:S(2)}) collective-permute-start(bf16[400,1024]{1,0:T(8,128)(2,1)} %get-tuple-element.25), channel_id=1, source_target_pairs={{2,0},{4,2},{6,4},{8,6},{10,8},{12,10},{14,12},{16,14},{18,16},{20... | collective-permute-start | bytes 2457608 | tf_op jit(solution)/shard_map/ppermute | solution.py:278
  21.5 11.6 %collective-permute-start = (bf16[32,16,512]{2,1,0:T(8,128)(2,1)}, bf16[32,16,512]{2,1,0:T(8,128)(2,1)S(1)}, u32[]{:S(2)}, u32[]{:S(2)}) collective-permute-start(bf16[32,16,512]{2,1,0:T(8,128)(2,1)} %all-to-all-done.mine_ref), channel_id=1, source_target_pairs={{0,2},{2,0},{4,6},{6,4},{8,10},{10,8},{12,14},{14,12},{16,18},{18,... | collective-permute-start | bytes 1572872 | tf_op jit(solution)/shard_map/ppermute | solution.py:299
  24.5 5.3 %copy-start.14 = (f32[3,384]{1,0:T(4,128)S(1)}, f32[3,384]{1,0:T(4,128)}, u32[]{:S(2)}) copy-start(f32[3,384]{1,0:T(4,128)} %bend_ref.1) | copy-start | bytes 13828
  24.5 5.3 %copy-start.15 = (f32[256]{0:T(256)S(1)}, f32[256]{0:T(256)}, u32[]{:S(2)}) copy-start(f32[256]{0:T(256)} %param.16) | copy-start | bytes 3076
  26.2 27.4 %collective-permute-start.5 = (bf16[32,16,512]{2,1,0:T(8,128)(2,1)}, bf16[32,16,512]{2,1,0:T(8,128)(2,1)}, u32[]{:S(2)}, u32[]{:S(2)}) collective-permute-start(bf16[32,16,512]{2,1,0:T(8,128)(2,1)} %all-to-all-done.mine_ref), channel_id=1, source_target_pairs={{0,1},{1,0},{2,3},{3,2},{4,5},{5,4},{6,7},{7,6},{8,9},{9,8},{10,11... | collective-permute-start | bytes 1572872 | tf_op jit(solution)/shard_map/ppermute | solution.py:323
  29.8 3.3 %copy-start.7 = (bf16[400,1024]{1,0:T(8,128)(2,1)}, bf16[400,1024]{1,0:T(8,128)(2,1)S(1)}, u32[]{:S(2)}) copy-start(bf16[400,1024]{1,0:T(8,128)(2,1)S(1)} %collective-permute-done.1.prv_ref) | copy-start | bytes 2457604
  33.1 0.8 copy-start.9
  33.9 1.1 %copy-start.8 = (bf16[400,1024]{1,0:T(8,128)(2,1)S(1)}, bf16[400,1024]{1,0:T(8,128)(2,1)}, u32[]{:S(2)}) copy-start(bf16[400,1024]{1,0:T(8,128)(2,1)} %copy-done.7) | copy-start | bytes 2457604
  35.1 1.0 %copy-start.10 = (bf16[32,16,512]{2,1,0:T(8,128)(2,1)S(1)}, bf16[32,16,512]{2,1,0:T(8,128)(2,1)}, u32[]{:S(2)}) copy-start(bf16[32,16,512]{2,1,0:T(8,128)(2,1)} %copy-done.9) | copy-start | bytes 1572868
  48.5 1.1 %copy-start.16 = (f32[768,512]{1,0:T(8,128)}, f32[768,512]{1,0:T(8,128)S(1)}, u32[]{:S(2)}) copy-start(f32[768,512]{1,0:T(8,128)S(1)} %get-tuple-element.36.f_own_ref) | copy-start | bytes 4718596
  49.6 9.5 %collective-permute-start.8 = (bf16[32,16,512]{2,1,0:T(8,128)(2,1)}, bf16[32,16,512]{2,1,0:T(8,128)(2,1)S(1)}, u32[]{:S(2)}, u32[]{:S(2)}) collective-permute-start(bf16[32,16,512]{2,1,0:T(8,128)(2,1)} %get-tuple-element.45), channel_id=1, source_target_pairs={{0,2},{2,0},{4,6},{6,4},{8,10},{10,8},{12,14},{14,12},{16,18},{18,... | collective-permute-start | bytes 1572872 | tf_op jit(solution)/shard_map/ppermute | solution.py:318
  53.1 10.8 %collective-permute-start.3 = (bf16[384,512]{1,0:T(8,128)(2,1)}, bf16[384,512]{1,0:T(8,128)(2,1)S(1)}, u32[]{:S(2)}, u32[]{:S(2)}) collective-permute-start(bf16[384,512]{1,0:T(8,128)(2,1)} %get-tuple-element.37), channel_id=1, source_target_pairs={{0,2},{2,4},{4,6},{6,8},{8,10},{10,12},{12,14},{14,16},{16,18},{18... | collective-permute-start | bytes 1179656 | tf_op jit(solution)/shard_map/ppermute | solution.py:316
  53.1 10.8 %collective-permute-start.4 = (bf16[384,512]{1,0:T(8,128)(2,1)S(1)}, bf16[384,512]{1,0:T(8,128)(2,1)}, u32[]{:S(2)}, u32[]{:S(2)}) collective-permute-start(bf16[384,512]{1,0:T(8,128)(2,1)S(1)} %get-tuple-element.38), channel_id=1, source_target_pairs={{2,0},{4,2},{6,4},{8,6},{10,8},{12,10},{14,12},{16,14},{18,16},{20... | collective-permute-start | bytes 1179656 | tf_op jit(solution)/shard_map/ppermute | solution.py:315
  53.6 17.4 %collective-permute-start.6 = (bf16[32,16,512]{2,1,0:T(8,128)(2,1)}, bf16[32,16,512]{2,1,0:T(8,128)(2,1)S(1)}, u32[]{:S(2)}, u32[]{:S(2)}) collective-permute-start(bf16[32,16,512]{2,1,0:T(8,128)(2,1)} %collective-permute-done.5.core_lat_ref), channel_id=1, source_target_pairs={{0,2},{2,0},{4,6},{6,4},{8,10},{10,8},{12,14},{14,12},{16,18},{18,... | collective-permute-start | bytes 1572872 | tf_op jit(solution)/shard_map/ppermute | solution.py:324
  60.0 14.8 %all-to-all-start.1 = ((bf16[32,16,512]{2,1,0:T(8,128)(2,1)}), bf16[32,16,512]{2,1,0:T(8,128)(2,1)S(1)}, u32[]{:S(2)}, u32[]{:S(2)}) async-start(bf16[32,16,512]{2,1,0:T(8,128)(2,1)} %shard_map.111), calls=%async_computation.1 | async-start | bytes 1048576 | tf_op jit(solution)/shard_map/all_to_all | solution.py:320
  64.0 1.4 %copy-start.17 = (f32[768,512]{1,0:T(8,128)S(1)}, f32[768,512]{1,0:T(8,128)}, u32[]{:S(2)}) copy-start(f32[768,512]{1,0:T(8,128)} %copy-done.16) | copy-start | bytes 4718596
  67.7 16.4 %collective-permute-start.7 = (bf16[384,512]{1,0:T(8,128)(2,1)}, bf16[384,512]{1,0:T(8,128)(2,1)}, u32[]{:S(2)}, u32[]{:S(2)}) collective-permute-start(bf16[384,512]{1,0:T(8,128)(2,1)} %get-tuple-element.42), channel_id=1, source_target_pairs={{0,1},{1,0},{2,3},{3,2},{4,5},{5,4},{6,7},{7,6},{8,9},{9,8},{10,11... | collective-permute-start | bytes 1179656 | tf_op jit(solution)/shard_map/ppermute | solution.py:331
  71.0 0.8 copy-start.1
  71.8 1.0 %copy-start.2 = (bf16[32,16,512]{2,1,0:T(8,128)(2,1)S(1)}, bf16[32,16,512]{2,1,0:T(8,128)(2,1)}, u32[]{:S(2)}) copy-start(bf16[32,16,512]{2,1,0:T(8,128)(2,1)} %copy-done.1) | copy-start | bytes 1572868
  84.1 0.8 copy-start.3

commit v4 on v2

--- a/solution.py
+++ b/solution.py
@@ -53,10 +53,12 @@
         ref.send()
 
 
-def first_kernel(shard_ref, send_ref, basis_ref, rest_ref, copies_ref, prev_ref, next_ref):
+def copies_kernel(shard_ref, copies_ref):
     for i in range(copies_ref.shape[0]):
         copies_ref[i] = shard_ref[...]
-    send(copies_ref)
+
+
+def rows_kernel(send_ref, basis_ref, rest_ref, prev_ref, next_ref):
     own, halo = basis_ref.shape[1], send_ref.shape[1]
     rest = rest_ref[...]
     parts = []
@@ -122,7 +124,7 @@
     frames, step,
     core_ref, mine_ref, sib_ref, own_ref, prv_ref, nxt_ref, d_ref, dt_ref, lap_ref, edge_ref,
     vert_ref, sq_ref, own_t_ref, halo_t_ref,
-    lat_ref, f_own_ref, f_prv_ref, f_nxt_ref, lg_ref, f_all_ref,
+    lat_ref, f_own_ref, f_prv_ref, f_nxt_ref, keep_ref, give_ref, f_all_ref,
 ):
     own_n = own_ref.shape[1]
     t = sq_ref.shape[0]
@@ -170,10 +172,21 @@
                 (3 * (own_n + halo) + c * halo, halo, own_n + halo),
             ):
                 f_all_ref[at_row : at_row + size, here] = short[first : first + size]
-    for at in range(0, lg_ref.shape[0], 256):
+    each = mine_ref.shape[1]
+    first = core_ref[0] == 0
+    for at in range(0, lat_ref.shape[0], 256):
         rows = slice(at, at + 256)
         both = jnp.concatenate([own_t_ref[rows, :], halo_t_ref[rows, :]], axis=1)
-        lg_ref[rows, :] = dot(both, f_all_ref[...]).astype(BF)
+        block = dot(both, f_all_ref[...])
+        for i in range(0, 256, 2 * each):
+            low, high = block[i : i + each], block[i + each : i + 2 * each]
+            chip = (at + i) // (2 * each)
+            keep_ref[chip] = jnp.where(first, low, high).astype(BF)
+            give_ref[chip] = jnp.where(first, high, low).astype(BF)
+
+
+def pair_kernel(a_ref, b_ref, out_ref):
+    out_ref[...] = (a_ref[...].astype(F32) + b_ref[...].astype(F32)).astype(BF)
 
 
 def share_kernel(shares_ref, out_ref):
@@ -201,14 +214,22 @@
         other_ref[c * half : (c + 1) * half, :] = jnp.where(first, high, low).astype(BF)
 
 
-def own_part_kernel(mine_ref, lat_ref, out_ref):
+def own_part_far_kernel(core_ref, mine_ref, lat_ref, core_lat_ref, sib_lat_ref, out_ref, far_lat_ref):
+    interleave(core_ref[0], core_lat_ref, sib_lat_ref, far_lat_ref)
     out_ref[...] = dot(mine_ref[...], lat_ref[...], NT).astype(BF)
 
 
-def basis_grad_kernel(core_ref, part_ref, far_ref, core_lat_ref, sib_lat_ref, out_ref, lat_ref):
-    interleave(core_ref[0], core_lat_ref, sib_lat_ref, lat_ref)
-    far = dot(far_ref[...], lat_ref[...], NT).astype(BF).astype(F32)
-    out_ref[...] = part_ref[...].astype(F32) + far
+def last_kernel(part_ref, far_ref, lat_ref, done_ref, out_ref, sum_ref, sem):
+    third = out_ref.shape[0] // 3
+    copies = []
+    for c in range(3):
+        rows = slice(c * third, (c + 1) * third)
+        far = dot(far_ref[rows, :], lat_ref[...], NT).astype(BF).astype(F32)
+        sum_ref[rows, :] = part_ref[rows, :].astype(F32) + far
+        copies.append(pltpu.make_async_copy(sum_ref.at[rows], out_ref.at[rows], sem.at[c]))
+        copies[-1].start()
+    for copy in copies:
+        copy.wait()
 
 
 class Loaded:
@@ -320,9 +341,9 @@
     half_index = lax.axis_index("frame").astype(jnp.int32).reshape(1)
 
     sent = ((3 * halo + 16, width), BF)
-    copies, rows_prev, rows_next = call(
-        first_kernel, [((chips, each, frames), BF), sent, sent],
-        latents.T, send_rows, basis, rest_pos, direct=False, room=60,
+    [copies] = call(copies_kernel, [((chips, each, frames), BF)], latents.T)
+    rows_prev, rows_next = call(
+        rows_kernel, [sent, sent], send_rows, basis, rest_pos, direct=False, room=60
     )
     lat_core = lax.all_to_all(
         copies, "patch", 0, 0, tiled=True, axis_index_groups=same_core
@@ -350,14 +371,15 @@
         macs=1 << 30,
     )
     lat_sib = lax.ppermute(lat_core, "patch", sibling)
-    lat_all, f_own, f_prv, f_nxt, lg = call(
+    lat_all, f_own, f_prv, f_nxt, keep, give = call(
         functools.partial(elastic_kernel, total_frames, min(frames, 256)),
         [
             ((width, frames), BF),
             ((3 * own, frames), F32),
             ((3 * halo, frames), BF),
             ((3 * halo, frames), BF),
-            ((width, frames), BF),
+            ((chips, each, frames), BF),
+            ((chips, each, frames), BF),
         ],
         core, lat_core, lat_sib, basis, halo_prv, halo_nxt, d, dt, lap, edge, vert, sq,
         own_t, halo_t,
@@ -367,7 +389,9 @@
     back_nxt = lax.ppermute(f_prv, "patch", backward)
     back_prv = lax.ppermute(f_nxt, "patch", onward)
 
-    shares = lax.all_to_all(lg.reshape(patches, each, frames), "patch", 0, 0, tiled=True)
+    got = lax.ppermute(give, "patch", sibling)
+    [pair] = call(pair_kernel, [((chips, each, frames), BF)], keep, got)
+    shares = lax.all_to_all(pair, "patch", 0, 0, tiled=True, axis_index_groups=same_core)
     [latent_grad] = call(share_kernel, [((each, frames), F32)], shares)
 
     far_core = lax.ppermute(lat_core, "frame", partner)
@@ -379,11 +403,18 @@
         scalars=1, macs=10 << 30,
     )
     received = lax.ppermute(other, "frame", partner)
-    [part] = call(own_part_kernel, [((3 * half, width), BF)], mine, lat_all, macs=3 * half * width * frames)
-    [basis_grad] = call(
-        basis_grad_kernel, [((3 * half, width), F32)], core, part, received, far_core, far_sib,
-        scalars=1, scratch=[pltpu.VMEM((width, frames), BF)],
-    )
+    part, lat_far = call(
+        own_part_far_kernel, [((3 * half, width), BF), ((width, frames), BF)],
+        core, mine, lat_all, far_core, far_sib, scalars=1, macs=3 * half * width * frames,
+    )
+    basis_grad = pl.pallas_call(
+        last_kernel,
+        in_specs=[VMEM, VMEM, VMEM, ANY],
+        out_specs=ANY,
+        out_shape=jax.ShapeDtypeStruct((3 * half, width), F32),
+        scratch_shapes=[pltpu.VMEM((3 * half, width), F32), pltpu.SemaphoreType.DMA((3,))],
+        compiler_params=pltpu.CompilerParams(vmem_limit_bytes=24 << 20),
+    )(part, received, lat_far, latent_grad)
     return basis_grad.reshape(3, half, width), latent_grad.T
 
 

time: 91.8 us -> 86.1 us (0.938)
  waiting for transfers between devices: 24.7 us -> 13.3 us
  local copies, waits for them, and re-layouts: 3.73 us -> 8.17 us
  Pallas kernels: 26.2 us -> 28.1 us
  starting transfers between devices: 35.9 us -> 34.8 us
    ppermute x1, waiting for transfers between devices: 17.3 us -> 8.6 us  [local(): received = lax.ppermute(other, 'frame', partner)]
    all_to_all x1, starting transfers between devices: 10 us -> 3.89 us  [local(): lax.all_to_all(pair, 'patch', 0, 0, tiled=True, axis_index_groups=same_core)]
    ppermute x1, starting transfers between devices: 0.65 us -> 5.46 us  [local(): far_sib = lax.ppermute(far_core, 'patch', sibling)]
    unnamed x24 -> x36, local copies, waits for them, and re-layouts: 3.73 us -> 8.17 us
    ppermute x0 -> x1, starting transfers between devices: none -> 3.99 us  [local(): got = lax.ppermute(give, 'patch', sibling)]
    all_to_all x1, waiting for transfers between devices: 7.38 us -> 4.38 us  [local(): lax.all_to_all(copies, 'patch', 0, 0, tiled=True, axis_index_groups=same_...]
    pallas_call x0 -> x1, Pallas kernels: none -> 2.97 us  [local(): pl.pallas_call(last_kernel, in_specs=[VMEM, VMEM, VMEM, ANY], out_specs=A...]
    ppermute x1, starting transfers between devices: 3.34 us -> 0.51 us  [local(): back_nxt = lax.ppermute(f_prv, 'patch', backward)]
  transfers between devices with their start and end apart: 10 -> 11, of which waited for: 2 -> 4; matrix products, arithmetic and copies ran while one was open for 0% -> 0% of each run, Pallas kernels for 24% -> 28%
where the time goes in v4:
time: 86.1 us; the launch traced here: 85.4 us
  starting transfers between devices  34.8 us (40%)
  Pallas kernels  28.1 us (33%)
  waiting for transfers between devices  13.3 us (15%)
  local copies, waits for them, and re-layouts  8.17 us (9%)
  between operations  0.97 us (1%)
    pallas_call x8, Pallas kernels, call(): pl.pallas_call(kernel, cost_estimate=pl.CostEstimate(flops=2 * macs, byte...  22.1 us
    all_to_all x1, starting transfers between devices, local(): lax.all_to_all(copies, 'patch', 0, 0, tiled=True, axis_index_groups=same_...  9.35 us
    ppermute x1, waiting for transfers between devices, local(): received = lax.ppermute(other, 'frame', partner)  8.6 us
    unnamed x36, local copies, waits for them, and re-layouts  8.17 us
    ppermute x1, starting transfers between devices, local(): far_sib = lax.ppermute(far_core, 'patch', sibling)  5.46 us
    all_to_all x1, waiting for transfers between devices, local(): lax.all_to_all(copies, 'patch', 0, 0, tiled=True, axis_index_groups=same_...  4.38 us
    ppermute x1, starting transfers between devices, local(): got = lax.ppermute(give, 'patch', sibling)  3.99 us
    all_to_all x1, starting transfers between devices, local(): lax.all_to_all(pair, 'patch', 0, 0, tiled=True, axis_index_groups=same_core)  3.89 us
  transfers between devices with their start and end apart: 11, of which 4 were waited for; matrix products, arithmetic and copies ran while one was open for 0% of the time, Pallas kernels for 28%

profile of v4, /device:TPU:1, one launch (start us, length us, event | category | flops | bytes accessed | tf_op | source)
XLA Modules:
  0.0 85.4 jit_solution(7855296281621146219)
XLA Ops:
  0.6 0.7 copy-done.4
  1.4 0.8 shard_map.104
  2.2 9.4 %all-to-all-start = ((bf16[32,16,512]{2,1,0:T(8,128)(2,1)}), bf16[32,16,512]{2,1,0:T(8,128)(2,1)}, u32[]{:S(2)}, u32[]{:S(2)}) async-start(bf16[32,16,512]{2,1,0:T(8,128)(2,1)} %shard_map.104), calls=%async_computation | async-start | bytes 1048576 | tf_op jit(solution)/shard_map/all_to_all | solution.py:348
  11.6 3.0 %shard_map.105 = (bf16[400,1024]{1,0:T(8,128)(2,1)}, bf16[400,1024]{1,0:T(8,128)(2,1)}) custom-call(s32[2,128]{1,0:T(2,128)} %send_ref.1, bf16[3,256,1024]{2,1,0:T(8,128)(2,1)} %own_ref.3, f32[3,256]{1,0:T(4,128)} %rest_ref.1), custom_call_target="tpu_custom_call" | custom-call | bytes 3215360 | tf_op jit(solution)/shard_map/pallas_call | solution.py:308
  14.6 2.3 %collective-permute-start.1 = (bf16[400,1024]{1,0:T(8,128)(2,1)}, bf16[400,1024]{1,0:T(8,128)(2,1)S(1)}, u32[]{:S(2)}, u32[]{:S(2)}) collective-permute-start(bf16[400,1024]{1,0:T(8,128)(2,1)} %get-tuple-element.24), channel_id=1, source_target_pairs={{0,2},{2,4},{4,6},{6,8},{8,10},{10,12},{12,14},{14,16},{16,18},{18... | collective-permute-start | bytes 2457608 | tf_op jit(solution)/shard_map/ppermute | solution.py:351
  17.0 4.4 %all-to-all-done.mine_ref = bf16[32,16,512]{2,1,0:T(8,128)(2,1)} async-done(((bf16[32,16,512]{2,1,0:T(8,128)(2,1)}), bf16[32,16,512]{2,1,0:T(8,128)(2,1)}, u32[]{:S(2)}, u32[]{:S(2)}) %all-to-all-start) | async-done | bytes 524320 | tf_op jit(solution)/shard_map/all_to_all | solution.py:348
  21.3 2.4 %collective-permute-start = (bf16[32,16,512]{2,1,0:T(8,128)(2,1)}, bf16[32,16,512]{2,1,0:T(8,128)(2,1)}, u32[]{:S(2)}, u32[]{:S(2)}) collective-permute-start(bf16[32,16,512]{2,1,0:T(8,128)(2,1)} %all-to-all-done.mine_ref), channel_id=1, source_target_pairs={{0,2},{2,0},{4,6},{6,4},{8,10},{10,8},{12,14},{14,12},{16,18},{18,... | collective-permute-start | bytes 1572872 | tf_op jit(solution)/shard_map/ppermute | solution.py:373
  23.8 0.0 copy-start.5
  23.8 1.8 %shard_map.106 = (bf16[1024,512]{1,0:T(8,128)(2,1)S(1)}, bf16[512,1024]{1,0:T(8,128)(2,1)S(1)}, bf16[384,512]{1,0:T(8,128)(2,1)S(1)}, bf16[512,384]{1,0:T(8,128)...) custom-call(s32[3,512]{1,0:T(4,128)S(1)} %copy-done.11, ...), custom_call_target="tpu_custom_call" | custom-call | flops 2147483648 | bytes 6834176 | tf_op jit(solution)/shard_map/pallas_call | solution.py:279
  25.6 3.6 %collective-permute-start.5 = (bf16[32,16,512]{2,1,0:T(8,128)(2,1)}, bf16[32,16,512]{2,1,0:T(8,128)(2,1)}, u32[]{:S(2)}, u32[]{:S(2)}) collective-permute-start(bf16[32,16,512]{2,1,0:T(8,128)(2,1)} %all-to-all-done.mine_ref), channel_id=1, source_target_pairs={{0,1},{1,0},{2,3},{3,2},{4,5},{5,4},{6,7},{7,6},{8,9},{9,8},{10,11... | collective-permute-start | bytes 1572872 | tf_op jit(solution)/shard_map/ppermute | solution.py:397
  29.1 0.1 collective-permute-done.2.nxt_ref
  29.2 1.9 %shard_map.107 = (f32[1024,128]{1,0:T(8,128)S(1)}, f32[512,128]{1,0:T(8,128)S(1)}, bf16[1024,768]{1,0:T(8,128)(2,1)S(1)}) custom-call(f32[3,256]{1,0:T(4,128)S(1)} %copy-done.5, f32[1,256]{1,0:T(1,128)S(1)} %bitcast.8, bf16[400,1024]{1,0:T(8,128)(2,1)S(1)} %collective-permute-done.1.prv_ref, bf16[400,1024]{1,0:T(8,128)(2,1)S(1)} %collective-permute-done.2.nxt_ref, ...), custom_call_target="tpu_custom_call" | custom-call | flops 2147483648 | bytes 5841408 | tf_op jit(solution)/shard_map/pallas_call | solution.py:279
  31.2 1.1 %copy-done.8 = bf16[400,1024]{1,0:T(8,128)(2,1)S(1)} copy-done((bf16[400,1024]{1,0:T(8,128)(2,1)S(1)}, bf16[400,1024]{1,0:T(8,128)(2,1)}, u32[]{:S(2)}) %copy-start.8) | copy-done | bytes 819224
  32.3 1.1 %copy-done.10 = bf16[400,1024]{1,0:T(8,128)(2,1)S(1)} copy-done((bf16[400,1024]{1,0:T(8,128)(2,1)S(1)}, bf16[400,1024]{1,0:T(8,128)(2,1)}, u32[]{:S(2)}) %copy-start.10) | copy-done | bytes 819224
  33.4 11.9 %shard_map.108 = (bf16[1024,512]{1,0:T(8,128)(2,1)S(1)}, f32[768,512]{1,0:T(8,128)S(1)}, bf16[384,512]{1,0:T(8,128)(2,1)S(1)}, bf16[384,512]{1,0:T(8,128)(2,1)},...) custom-call(s32[1]{0:T(128)} %bitcast.core_ref, bf16[32,16,512]{2,1,0:T(8,128)(2,1)} %all-to-all-done.mine_ref, ...), custom_call_target="tpu_custom_call" | custom-call | flops 10737418240 | bytes 15532036 | tf_op jit(solution)/shard_map/pallas_call | solution.py:279
  45.4 1.1 %copy-done.16 = f32[768,512]{1,0:T(8,128)} copy-done((f32[768,512]{1,0:T(8,128)}, f32[768,512]{1,0:T(8,128)S(1)}, u32[]{:S(2)}) %copy-start.16) | copy-done | bytes 1572888
  46.5 4.0 %collective-permute-start.8 = (bf16[32,16,512]{2,1,0:T(8,128)(2,1)}, bf16[32,16,512]{2,1,0:T(8,128)(2,1)S(1)}, u32[]{:S(2)}, u32[]{:S(2)}) collective-permute-start(bf16[32,16,512]{2,1,0:T(8,128)(2,1)} %get-tuple-element.45), channel_id=1, source_target_pairs={{0,2},{2,0},{4,6},{6,4},{8,10},{10,8},{12,14},{14,12},{16,18},{18,... | collective-permute-start | bytes 1572872 | tf_op jit(solution)/shard_map/ppermute | solution.py:392
  50.5 0.5 collective-permute-start.4
  51.0 5.5 %collective-permute-start.6 = (bf16[32,16,512]{2,1,0:T(8,128)(2,1)}, bf16[32,16,512]{2,1,0:T(8,128)(2,1)S(1)}, u32[]{:S(2)}, u32[]{:S(2)}) collective-permute-start(bf16[32,16,512]{2,1,0:T(8,128)(2,1)} %collective-permute-done.5.core_lat_ref), channel_id=1, source_target_pairs={{0,2},{2,0},{4,6},{6,4},{8,10},{10,8},{12,14},{14,12},{16,18},{18,... | collective-permute-start | bytes 1572872 | tf_op jit(solution)/shard_map/ppermute | solution.py:398
  56.5 0.9 %shard_map.111 = bf16[32,16,512]{2,1,0:T(8,128)(2,1)} custom-call(bf16[32,16,512]{2,1,0:T(8,128)(2,1)S(1)} %get-tuple-element.44.a_ref, bf16[32,16,512]{2,1,0:T(8,128)(2,1)S(1)} %collective-permute-done.8.b_ref), custom_call_target="tpu_custom_call" | custom-call | bytes 1572864 | tf_op jit(solution)/shard_map/pallas_call | solution.py:279
  57.4 3.9 %all-to-all-start.1 = ((bf16[32,16,512]{2,1,0:T(8,128)(2,1)}), bf16[32,16,512]{2,1,0:T(8,128)(2,1)S(1)}, u32[]{:S(2)}, u32[]{:S(2)}) async-start(bf16[32,16,512]{2,1,0:T(8,128)(2,1)} %shard_map.111), calls=%async_computation.1 | async-start | bytes 1048576 | tf_op jit(solution)/shard_map/all_to_all | solution.py:394
  61.3 1.4 %copy-done.17 = f32[768,512]{1,0:T(8,128)S(1)} copy-done((f32[768,512]{1,0:T(8,128)S(1)}, f32[768,512]{1,0:T(8,128)}, u32[]{:S(2)}) %copy-start.17) | copy-done | bytes 1572888
  62.7 2.4 %shard_map.109 = (bf16[384,512]{1,0:T(8,128)(2,1)S(1)}, bf16[384,512]{1,0:T(8,128)(2,1)}) custom-call(s32[1]{0:T(128)} %bitcast.1.half_ref, s32[2,128]{1,0:T(2,128)S(1)} %copy-done.6, f32[768,512]{1,0:T(8,128)S(1)} %copy-done.17, bf16[384,512]{1,0:T(8,128)(2,1)S(1)} %collective-permute-done.3.back_prv_ref, bf16[384,512]{1,0:T(8,128)(2,1)} %collective-permute-done.4.back_nxt_ref), custom_call_target="tpu_custom_call" | custom-call | flops 21474836480 | bytes 3146756 | tf_op jit(solution)/shard_map/pallas_call | solution.py:279
  65.1 3.3 %collective-permute-start.7 = (bf16[384,512]{1,0:T(8,128)(2,1)}, bf16[384,512]{1,0:T(8,128)(2,1)}, u32[]{:S(2)}, u32[]{:S(2)}) collective-permute-start(bf16[384,512]{1,0:T(8,128)(2,1)} %get-tuple-element.42), channel_id=1, source_target_pairs={{0,1},{1,0},{2,3},{3,2},{4,5},{5,4},{6,7},{7,6},{8,9},{9,8},{10,11... | collective-permute-start | bytes 1179656 | tf_op jit(solution)/shard_map/ppermute | solution.py:405
  68.4 0.8 copy-done.1
  69.2 1.0 %copy-done.2 = bf16[32,16,512]{2,1,0:T(8,128)(2,1)S(1)} copy-done((bf16[32,16,512]{2,1,0:T(8,128)(2,1)S(1)}, bf16[32,16,512]{2,1,0:T(8,128)(2,1)}, u32[]{:S(2)}) %copy-start.2) | copy-done | bytes 524312
  70.2 1.7 %shard_map.110 = (bf16[384,1024]{1,0:T(8,128)(2,1)S(1)}, bf16[1024,512]{1,0:T(8,128)(2,1)S(1)}) custom-call(s32[1]{0:T(128)} %bitcast.core_ref, bf16[384,512]{1,0:T(8,128)(2,1)S(1)} %get-tuple-element.39.mine_ref, bf16[1024,512]{1,0:T(8,128)(2,1)S(1)} %get-tuple-element.40.lat_ref, bf16[32,16,512]{2,1,0:T(8,128)(2,1)} %collective-permute-done.5.core_lat_ref, ...), custom_call_target="tpu_custom_call" | custom-call | flops 402653184 | bytes 4325380 | tf_op jit(solution)/shard_map/pallas_call | solution.py:279
  71.9 0.2 all-to-all-done.1.shares_ref
  72.2 0.7 shard_map.112.done_ref
  72.9 8.6 %collective-permute-done.7.far_ref = bf16[384,512]{1,0:T(8,128)(2,1)} collective-permute-done((bf16[384,512]{1,0:T(8,128)(2,1)}, bf16[384,512]{1,0:T(8,128)(2,1)}, u32[]{:S(2)}, u32[]{:S(2)}) %collective-permute-start.7) | collective-permute-done | bytes 393248 | tf_op jit(solution)/shard_map/ppermute | solution.py:405
  81.5 0.8 copy-done.3
  82.2 3.0 %shard_map.113 = f32[384,1024]{1,0:T(8,128)} custom-call(bf16[384,1024]{1,0:T(8,128)(2,1)S(1)} %get-tuple-element.41.part_ref, bf16[384,512]{1,0:T(8,128)(2,1)} %collective-permute-done.7.far_ref, bf16[1024,512]{1,0:T(8,128)(2,1)S(1)} %get-tuple-element.43.lat_ref, f32[16,512]{1,0:T(8,128)S(1)} %copy-done.3), custom_call_target="tpu_custom_call" | custom-call | tf_op jit(solution)/shard_map/pallas_call | solution.py:410
  (36 shorter events, 0.1 us)
Async XLA Ops:
  0.6 0.7 copy-start.4
  1.3 22.4 %copy-start = (bf16[3,256,1024]{2,1,0:T(8,128)(2,1)S(1)}, bf16[3,256,1024]{2,1,0:T(8,128)(2,1)}, u32[]{:S(2)}) copy-start(bf16[3,256,1024]{2,1,0:T(8,128)(2,1)} %own_ref.3) | copy-start | bytes 4718596
  1.4 22.4 %copy-start.11 = (s32[3,512]{1,0:T(4,128)S(1)}, s32[3,512]{1,0:T(4,128)}, u32[]{:S(2)}) copy-start(s32[3,512]{1,0:T(4,128)} %tri_ref.1) | copy-start | bytes 18436
  1.4 22.4 %copy-start.12 = (f32[3,512]{1,0:T(4,128)S(1)}, f32[3,512]{1,0:T(4,128)}, u32[]{:S(2)}) copy-start(f32[3,512]{1,0:T(4,128)} %sq_ref.1) | copy-start | bytes 18436
  1.4 22.4 %copy-start.13 = (s32[4,384]{1,0:T(4,128)S(1)}, s32[4,384]{1,0:T(4,128)}, u32[]{:S(2)}) copy-start(s32[4,384]{1,0:T(4,128)} %hin_ref.1) | copy-start | bytes 18436
  2.2 19.1 %all-to-all-start = ((bf16[32,16,512]{2,1,0:T(8,128)(2,1)}), bf16[32,16,512]{2,1,0:T(8,128)(2,1)}, u32[]{:S(2)}, u32[]{:S(2)}) async-start(bf16[32,16,512]{2,1,0:T(8,128)(2,1)} %shard_map.104), calls=%async_computation | async-start | bytes 1048576 | tf_op jit(solution)/shard_map/all_to_all | solution.py:348
  14.6 14.5 %collective-permute-start.1 = (bf16[400,1024]{1,0:T(8,128)(2,1)}, bf16[400,1024]{1,0:T(8,128)(2,1)S(1)}, u32[]{:S(2)}, u32[]{:S(2)}) collective-permute-start(bf16[400,1024]{1,0:T(8,128)(2,1)} %get-tuple-element.24), channel_id=1, source_target_pairs={{0,2},{2,4},{4,6},{6,8},{8,10},{10,12},{12,14},{14,16},{16,18},{18... | collective-permute-start | bytes 2457608 | tf_op jit(solution)/shard_map/ppermute | solution.py:351
  17.0 12.3 %collective-permute-start.2 = (bf16[400,1024]{1,0:T(8,128)(2,1)}, bf16[400,1024]{1,0:T(8,128)(2,1)S(1)}, u32[]{:S(2)}, u32[]{:S(2)}) collective-permute-start(bf16[400,1024]{1,0:T(8,128)(2,1)} %get-tuple-element.25), channel_id=1, source_target_pairs={{2,0},{4,2},{6,4},{8,6},{10,8},{12,10},{14,12},{16,14},{18,16},{20... | collective-permute-start | bytes 2457608 | tf_op jit(solution)/shard_map/ppermute | solution.py:352
  21.3 9.8 %collective-permute-start = (bf16[32,16,512]{2,1,0:T(8,128)(2,1)}, bf16[32,16,512]{2,1,0:T(8,128)(2,1)}, u32[]{:S(2)}, u32[]{:S(2)}) collective-permute-start(bf16[32,16,512]{2,1,0:T(8,128)(2,1)} %all-to-all-done.mine_ref), channel_id=1, source_target_pairs={{0,2},{2,0},{4,6},{6,4},{8,10},{10,8},{12,14},{14,12},{16,18},{18,... | collective-permute-start | bytes 1572872 | tf_op jit(solution)/shard_map/ppermute | solution.py:373
  23.8 5.4 %copy-start.5 = (f32[3,256]{1,0:T(4,128)S(1)}, f32[3,256]{1,0:T(4,128)}, u32[]{:S(2)}) copy-start(f32[3,256]{1,0:T(4,128)} %rest_ref.1) | copy-start | bytes 9220
  23.8 5.4 %copy-start.14 = (f32[3,384]{1,0:T(4,128)S(1)}, f32[3,384]{1,0:T(4,128)}, u32[]{:S(2)}) copy-start(f32[3,384]{1,0:T(4,128)} %bend_ref.1) | copy-start | bytes 13828
  23.8 5.4 %copy-start.15 = (f32[256]{0:T(256)S(1)}, f32[256]{0:T(256)}, u32[]{:S(2)}) copy-start(f32[256]{0:T(256)} %param.16) | copy-start | bytes 3076
  25.6 25.4 %collective-permute-start.5 = (bf16[32,16,512]{2,1,0:T(8,128)(2,1)}, bf16[32,16,512]{2,1,0:T(8,128)(2,1)}, u32[]{:S(2)}, u32[]{:S(2)}) collective-permute-start(bf16[32,16,512]{2,1,0:T(8,128)(2,1)} %all-to-all-done.mine_ref), channel_id=1, source_target_pairs={{0,1},{1,0},{2,3},{3,2},{4,5},{5,4},{6,7},{7,6},{8,9},{9,8},{10,11... | collective-permute-start | bytes 1572872 | tf_op jit(solution)/shard_map/ppermute | solution.py:397
  29.1 2.0 %copy-start.7 = (bf16[400,1024]{1,0:T(8,128)(2,1)}, bf16[400,1024]{1,0:T(8,128)(2,1)S(1)}, u32[]{:S(2)}) copy-start(bf16[400,1024]{1,0:T(8,128)(2,1)S(1)} %collective-permute-done.1.prv_ref) | copy-start | bytes 2457604
  29.2 1.9 %copy-start.9 = (bf16[400,1024]{1,0:T(8,128)(2,1)}, bf16[400,1024]{1,0:T(8,128)(2,1)S(1)}, u32[]{:S(2)}) copy-start(bf16[400,1024]{1,0:T(8,128)(2,1)S(1)} %collective-permute-done.2.nxt_ref) | copy-start | bytes 2457604
  31.1 1.1 %copy-start.8 = (bf16[400,1024]{1,0:T(8,128)(2,1)S(1)}, bf16[400,1024]{1,0:T(8,128)(2,1)}, u32[]{:S(2)}) copy-start(bf16[400,1024]{1,0:T(8,128)(2,1)} %copy-done.7) | copy-start | bytes 2457604
  32.3 1.1 %copy-start.10 = (bf16[400,1024]{1,0:T(8,128)(2,1)S(1)}, bf16[400,1024]{1,0:T(8,128)(2,1)}, u32[]{:S(2)}) copy-start(bf16[400,1024]{1,0:T(8,128)(2,1)} %copy-done.9) | copy-start | bytes 2457604
  45.4 1.1 %copy-start.16 = (f32[768,512]{1,0:T(8,128)}, f32[768,512]{1,0:T(8,128)S(1)}, u32[]{:S(2)}) copy-start(f32[768,512]{1,0:T(8,128)S(1)} %get-tuple-element.36.f_own_ref) | copy-start | bytes 4718596
  46.5 14.8 %copy-start.6 = (s32[2,128]{1,0:T(2,128)S(1)}, s32[2,128]{1,0:T(2,128)}, u32[]{:S(2)}) copy-start(s32[2,128]{1,0:T(2,128)} %send_ref.1) | copy-start | bytes 3076
  46.5 10.0 %collective-permute-start.8 = (bf16[32,16,512]{2,1,0:T(8,128)(2,1)}, bf16[32,16,512]{2,1,0:T(8,128)(2,1)S(1)}, u32[]{:S(2)}, u32[]{:S(2)}) collective-permute-start(bf16[32,16,512]{2,1,0:T(8,128)(2,1)} %get-tuple-element.45), channel_id=1, source_target_pairs={{0,2},{2,0},{4,6},{6,4},{8,10},{10,8},{12,14},{14,12},{16,18},{18,... | collective-permute-start | bytes 1572872 | tf_op jit(solution)/shard_map/ppermute | solution.py:392
  50.5 10.8 %collective-permute-start.3 = (bf16[384,512]{1,0:T(8,128)(2,1)}, bf16[384,512]{1,0:T(8,128)(2,1)S(1)}, u32[]{:S(2)}, u32[]{:S(2)}) collective-permute-start(bf16[384,512]{1,0:T(8,128)(2,1)} %get-tuple-element.37), channel_id=1, source_target_pairs={{0,2},{2,4},{4,6},{6,8},{8,10},{10,12},{12,14},{14,16},{16,18},{18... | collective-permute-start | bytes 1179656 | tf_op jit(solution)/shard_map/ppermute | solution.py:390
  50.5 10.8 %collective-permute-start.4 = (bf16[384,512]{1,0:T(8,128)(2,1)S(1)}, bf16[384,512]{1,0:T(8,128)(2,1)}, u32[]{:S(2)}, u32[]{:S(2)}) collective-permute-start(bf16[384,512]{1,0:T(8,128)(2,1)S(1)} %get-tuple-element.38), channel_id=1, source_target_pairs={{2,0},{4,2},{6,4},{8,6},{10,8},{12,10},{14,12},{16,14},{18,16},{20... | collective-permute-start | bytes 1179656 | tf_op jit(solution)/shard_map/ppermute | solution.py:389
  51.0 17.4 %collective-permute-start.6 = (bf16[32,16,512]{2,1,0:T(8,128)(2,1)}, bf16[32,16,512]{2,1,0:T(8,128)(2,1)S(1)}, u32[]{:S(2)}, u32[]{:S(2)}) collective-permute-start(bf16[32,16,512]{2,1,0:T(8,128)(2,1)} %collective-permute-done.5.core_lat_ref), channel_id=1, source_target_pairs={{0,2},{2,0},{4,6},{6,4},{8,10},{10,8},{12,14},{14,12},{16,18},{18,... | collective-permute-start | bytes 1572872 | tf_op jit(solution)/shard_map/ppermute | solution.py:398
  57.4 14.8 %all-to-all-start.1 = ((bf16[32,16,512]{2,1,0:T(8,128)(2,1)}), bf16[32,16,512]{2,1,0:T(8,128)(2,1)S(1)}, u32[]{:S(2)}, u32[]{:S(2)}) async-start(bf16[32,16,512]{2,1,0:T(8,128)(2,1)} %shard_map.111), calls=%async_computation.1 | async-start | bytes 1048576 | tf_op jit(solution)/shard_map/all_to_all | solution.py:394
  61.3 1.4 %copy-start.17 = (f32[768,512]{1,0:T(8,128)S(1)}, f32[768,512]{1,0:T(8,128)}, u32[]{:S(2)}) copy-start(f32[768,512]{1,0:T(8,128)} %copy-done.16) | copy-start | bytes 4718596
  65.1 16.4 %collective-permute-start.7 = (bf16[384,512]{1,0:T(8,128)(2,1)}, bf16[384,512]{1,0:T(8,128)(2,1)}, u32[]{:S(2)}, u32[]{:S(2)}) collective-permute-start(bf16[384,512]{1,0:T(8,128)(2,1)} %get-tuple-element.42), channel_id=1, source_target_pairs={{0,1},{1,0},{2,3},{3,2},{4,5},{5,4},{6,7},{7,6},{8,9},{9,8},{10,11... | collective-permute-start | bytes 1179656 | tf_op jit(solution)/shard_map/ppermute | solution.py:405
  68.4 0.8 copy-start.1
  69.2 1.0 %copy-start.2 = (bf16[32,16,512]{2,1,0:T(8,128)(2,1)S(1)}, bf16[32,16,512]{2,1,0:T(8,128)(2,1)}, u32[]{:S(2)}) copy-start(bf16[32,16,512]{2,1,0:T(8,128)(2,1)} %copy-done.1) | copy-start | bytes 1572868
  81.5 0.8 copy-start.3

commit v5 on v4

--- a/solution.py
+++ b/solution.py
@@ -400,7 +400,7 @@
     piece = ((3 * half, frames), BF)
     mine, other = call(
         adjoint_kernel, [piece, piece], half_index, send_rows, f_own, back_prv, back_nxt,
-        scalars=1, macs=10 << 30,
+        scalars=1, direct=False, near=(3, 4), room=60, macs=10 << 30,
     )
     received = lax.ppermute(other, "frame", partner)
     part, lat_far = call(

time: 86.1 us -> 86.8 us (level)
  Pallas kernels: 28.1 us -> 29.8 us
  waiting for transfers between devices: 13.3 us -> 11.9 us
    pallas_call x1 -> x2, Pallas kernels: 3.04 us -> 7.09 us  [call(): pl.pallas_call(body, cost_estimate=pl.CostEstimate(flops=2 * macs, bytes_...]
    pallas_call x8 -> x7, Pallas kernels: 22.1 us -> 19.7 us  [call(): pl.pallas_call(kernel, cost_estimate=pl.CostEstimate(flops=2 * macs, byte...]
    ppermute x1, waiting for transfers between devices: 8.6 us -> 7.37 us  [local(): received = lax.ppermute(other, 'frame', partner)]
  transfers between devices with their start and end apart: 11 -> 11, of which waited for: 4 -> 3; matrix products, arithmetic and copies ran while one was open for 0% -> 0% of each run, Pallas kernels for 28% -> 30%
where the time goes in v5:
time: 86.8 us; the launch traced here: 86 us
  starting transfers between devices  34.9 us (40%)
  Pallas kernels  29.8 us (34%)
  waiting for transfers between devices  11.9 us (14%)
  local copies, waits for them, and re-layouts  8.51 us (10%)
  between operations  0.97 us (1%)
    pallas_call x7, Pallas kernels, call(): pl.pallas_call(kernel, cost_estimate=pl.CostEstimate(flops=2 * macs, byte...  19.7 us
    all_to_all x1, starting transfers between devices, local(): lax.all_to_all(copies, 'patch', 0, 0, tiled=True, axis_index_groups=same_...  9.35 us
    unnamed x36, local copies, waits for them, and re-layouts  8.51 us
    ppermute x1, waiting for transfers between devices, local(): received = lax.ppermute(other, 'frame', partner)  7.37 us
    pallas_call x2, Pallas kernels, call(): pl.pallas_call(body, cost_estimate=pl.CostEstimate(flops=2 * macs, bytes_...  7.09 us
    ppermute x1, starting transfers between devices, local(): far_sib = lax.ppermute(far_core, 'patch', sibling)  5.46 us
    all_to_all x1, waiting for transfers between devices, local(): lax.all_to_all(copies, 'patch', 0, 0, tiled=True, axis_index_groups=same_...  4.38 us
    ppermute x1, starting transfers between devices, local(): got = lax.ppermute(give, 'patch', sibling)  3.99 us
  transfers between devices with their start and end apart: 11, of which 3 were waited for; matrix products, arithmetic and copies ran while one was open for 0% of the time, Pallas kernels for 30%

profile of v5, /device:TPU:1, one launch (start us, length us, event | category | flops | bytes accessed | tf_op | source)
XLA Modules:
  0.0 86.0 jit_solution(8147227748966242653)
XLA Ops:
  0.6 0.7 copy-done.5
  1.4 0.8 shard_map.104
  2.2 9.4 %all-to-all-start = ((bf16[32,16,512]{2,1,0:T(8,128)(2,1)}), bf16[32,16,512]{2,1,0:T(8,128)(2,1)}, u32[]{:S(2)}, u32[]{:S(2)}) async-start(bf16[32,16,512]{2,1,0:T(8,128)(2,1)} %shard_map.104), calls=%async_computation | async-start | bytes 1048576 | tf_op jit(solution)/shard_map/all_to_all | solution.py:348
  11.6 3.0 %shard_map.105 = (bf16[400,1024]{1,0:T(8,128)(2,1)}, bf16[400,1024]{1,0:T(8,128)(2,1)}) custom-call(s32[2,128]{1,0:T(2,128)} %refs_1_.3, bf16[3,256,1024]{2,1,0:T(8,128)(2,1)} %own_ref.3, f32[3,256]{1,0:T(4,128)} %rest_ref.1), custom_call_target="tpu_custom_call" | custom-call | bytes 3215360 | tf_op jit(solution)/shard_map/pallas_call | solution.py:308
  14.6 2.3 %collective-permute-start.1 = (bf16[400,1024]{1,0:T(8,128)(2,1)}, bf16[400,1024]{1,0:T(8,128)(2,1)S(1)}, u32[]{:S(2)}, u32[]{:S(2)}) collective-permute-start(bf16[400,1024]{1,0:T(8,128)(2,1)} %get-tuple-element.24), channel_id=1, source_target_pairs={{0,2},{2,4},{4,6},{6,8},{8,10},{10,12},{12,14},{14,16},{16,18},{18... | collective-permute-start | bytes 2457608 | tf_op jit(solution)/shard_map/ppermute | solution.py:351
  17.0 4.4 %all-to-all-done.mine_ref = bf16[32,16,512]{2,1,0:T(8,128)(2,1)} async-done(((bf16[32,16,512]{2,1,0:T(8,128)(2,1)}), bf16[32,16,512]{2,1,0:T(8,128)(2,1)}, u32[]{:S(2)}, u32[]{:S(2)}) %all-to-all-start) | async-done | bytes 524320 | tf_op jit(solution)/shard_map/all_to_all | solution.py:348
  21.3 2.4 %collective-permute-start = (bf16[32,16,512]{2,1,0:T(8,128)(2,1)}, bf16[32,16,512]{2,1,0:T(8,128)(2,1)}, u32[]{:S(2)}, u32[]{:S(2)}) collective-permute-start(bf16[32,16,512]{2,1,0:T(8,128)(2,1)} %all-to-all-done.mine_ref), channel_id=1, source_target_pairs={{0,2},{2,0},{4,6},{6,4},{8,10},{10,8},{12,14},{14,12},{16,18},{18,... | collective-permute-start | bytes 1572872 | tf_op jit(solution)/shard_map/ppermute | solution.py:373
  23.8 0.0 copy-start.14
  23.8 1.8 %shard_map.106 = (bf16[1024,512]{1,0:T(8,128)(2,1)S(1)}, bf16[512,1024]{1,0:T(8,128)(2,1)S(1)}, bf16[384,512]{1,0:T(8,128)(2,1)S(1)}, bf16[512,384]{1,0:T(8,128)...) custom-call(s32[3,512]{1,0:T(4,128)S(1)} %copy-done.11, ...), custom_call_target="tpu_custom_call" | custom-call | flops 2147483648 | bytes 6834176 | tf_op jit(solution)/shard_map/pallas_call | solution.py:279
  25.6 3.6 %collective-permute-start.5 = (bf16[32,16,512]{2,1,0:T(8,128)(2,1)}, bf16[32,16,512]{2,1,0:T(8,128)(2,1)}, u32[]{:S(2)}, u32[]{:S(2)}) collective-permute-start(bf16[32,16,512]{2,1,0:T(8,128)(2,1)} %all-to-all-done.mine_ref), channel_id=1, source_target_pairs={{0,1},{1,0},{2,3},{3,2},{4,5},{5,4},{6,7},{7,6},{8,9},{9,8},{10,11... | collective-permute-start | bytes 1572872 | tf_op jit(solution)/shard_map/ppermute | solution.py:397
  29.1 0.1 collective-permute-done.2.nxt_ref
  29.2 1.9 %shard_map.107 = (f32[1024,128]{1,0:T(8,128)S(1)}, f32[512,128]{1,0:T(8,128)S(1)}, bf16[1024,768]{1,0:T(8,128)(2,1)S(1)}) custom-call(f32[3,256]{1,0:T(4,128)S(1)} %copy-done.6, f32[1,256]{1,0:T(1,128)S(1)} %bitcast.8, bf16[400,1024]{1,0:T(8,128)(2,1)S(1)} %collective-permute-done.1.prv_ref, bf16[400,1024]{1,0:T(8,128)(2,1)S(1)} %collective-permute-done.2.nxt_ref, ...), custom_call_target="tpu_custom_call" | custom-call | flops 2147483648 | bytes 5841408 | tf_op jit(solution)/shard_map/pallas_call | solution.py:279
  31.2 1.1 %copy-done.8 = bf16[400,1024]{1,0:T(8,128)(2,1)S(1)} copy-done((bf16[400,1024]{1,0:T(8,128)(2,1)S(1)}, bf16[400,1024]{1,0:T(8,128)(2,1)}, u32[]{:S(2)}) %copy-start.8) | copy-done | bytes 819224
  32.3 1.1 %copy-done.10 = bf16[400,1024]{1,0:T(8,128)(2,1)S(1)} copy-done((bf16[400,1024]{1,0:T(8,128)(2,1)S(1)}, bf16[400,1024]{1,0:T(8,128)(2,1)}, u32[]{:S(2)}) %copy-start.10) | copy-done | bytes 819224
  33.4 11.9 %shard_map.108 = (bf16[1024,512]{1,0:T(8,128)(2,1)S(1)}, f32[768,512]{1,0:T(8,128)S(1)}, bf16[384,512]{1,0:T(8,128)(2,1)S(1)}, bf16[384,512]{1,0:T(8,128)(2,1)},...) custom-call(s32[1]{0:T(128)} %bitcast.core_ref, bf16[32,16,512]{2,1,0:T(8,128)(2,1)} %all-to-all-done.mine_ref, ...), custom_call_target="tpu_custom_call" | custom-call | flops 10737418240 | bytes 15532036 | tf_op jit(solution)/shard_map/pallas_call | solution.py:279
  45.4 1.1 %copy-done.16 = f32[768,512]{1,0:T(8,128)} copy-done((f32[768,512]{1,0:T(8,128)}, f32[768,512]{1,0:T(8,128)S(1)}, u32[]{:S(2)}) %copy-start.16) | copy-done | bytes 1572888
  46.5 4.0 %collective-permute-start.8 = (bf16[32,16,512]{2,1,0:T(8,128)(2,1)}, bf16[32,16,512]{2,1,0:T(8,128)(2,1)S(1)}, u32[]{:S(2)}, u32[]{:S(2)}) collective-permute-start(bf16[32,16,512]{2,1,0:T(8,128)(2,1)} %get-tuple-element.45), channel_id=1, source_target_pairs={{0,2},{2,0},{4,6},{6,4},{8,10},{10,8},{12,14},{14,12},{16,18},{18,... | collective-permute-start | bytes 1572872 | tf_op jit(solution)/shard_map/ppermute | solution.py:392
  50.5 0.5 collective-permute-start.4
  51.0 5.5 %collective-permute-start.6 = (bf16[32,16,512]{2,1,0:T(8,128)(2,1)}, bf16[32,16,512]{2,1,0:T(8,128)(2,1)S(1)}, u32[]{:S(2)}, u32[]{:S(2)}) collective-permute-start(bf16[32,16,512]{2,1,0:T(8,128)(2,1)} %collective-permute-done.5.core_lat_ref), channel_id=1, source_target_pairs={{0,2},{2,0},{4,6},{6,4},{8,10},{10,8},{12,14},{14,12},{16,18},{18,... | collective-permute-start | bytes 1572872 | tf_op jit(solution)/shard_map/ppermute | solution.py:398
  56.5 0.9 %shard_map.111 = bf16[32,16,512]{2,1,0:T(8,128)(2,1)} custom-call(bf16[32,16,512]{2,1,0:T(8,128)(2,1)S(1)} %get-tuple-element.44.a_ref, bf16[32,16,512]{2,1,0:T(8,128)(2,1)S(1)} %collective-permute-done.8.b_ref), custom_call_target="tpu_custom_call" | custom-call | bytes 1572864 | tf_op jit(solution)/shard_map/pallas_call | solution.py:279
  57.4 3.9 %all-to-all-start.1 = ((bf16[32,16,512]{2,1,0:T(8,128)(2,1)}), bf16[32,16,512]{2,1,0:T(8,128)(2,1)S(1)}, u32[]{:S(2)}, u32[]{:S(2)}) async-start(bf16[32,16,512]{2,1,0:T(8,128)(2,1)} %shard_map.111), calls=%async_computation.1 | async-start | bytes 1048576 | tf_op jit(solution)/shard_map/all_to_all | solution.py:394
  61.3 0.7 copy-done.17
  62.1 4.0 %shard_map.109 = (bf16[384,512]{1,0:T(8,128)(2,1)}, bf16[384,512]{1,0:T(8,128)(2,1)}) custom-call(s32[1]{0:T(128)} %bitcast.1.refs_0_, s32[2,128]{1,0:T(2,128)} %refs_1_.3, f32[768,512]{1,0:T(8,128)} %copy-done.16, bf16[384,512]{1,0:T(8,128)(2,1)} %copy-done.17, bf16[384,512]{1,0:T(8,128)(2,1)} %collective-permute-done.4.refs_4_), custom_call_target="tpu_custom_call" | custom-call | flops 21474836480 | bytes 3146756 | tf_op jit(solution)/shard_map/pallas_call | solution.py:308
  66.1 3.4 %collective-permute-start.7 = (bf16[384,512]{1,0:T(8,128)(2,1)}, bf16[384,512]{1,0:T(8,128)(2,1)}, u32[]{:S(2)}, u32[]{:S(2)}) collective-permute-start(bf16[384,512]{1,0:T(8,128)(2,1)} %get-tuple-element.42), channel_id=1, source_target_pairs={{0,1},{1,0},{2,3},{3,2},{4,5},{5,4},{6,7},{7,6},{8,9},{9,8},{10,11... | collective-permute-start | bytes 1179656 | tf_op jit(solution)/shard_map/ppermute | solution.py:405
  69.5 0.8 copy-done.1
  70.3 1.0 %copy-done.2 = bf16[32,16,512]{2,1,0:T(8,128)(2,1)S(1)} copy-done((bf16[32,16,512]{2,1,0:T(8,128)(2,1)S(1)}, bf16[32,16,512]{2,1,0:T(8,128)(2,1)}, u32[]{:S(2)}) %copy-start.2) | copy-done | bytes 524312
  71.3 1.0 %copy-done.3 = bf16[384,512]{1,0:T(8,128)(2,1)S(1)} copy-done((bf16[384,512]{1,0:T(8,128)(2,1)S(1)}, bf16[384,512]{1,0:T(8,128)(2,1)}, u32[]{:S(2)}) %copy-start.3) | copy-done | bytes 393240
  72.3 1.7 %shard_map.110 = (bf16[384,1024]{1,0:T(8,128)(2,1)S(1)}, bf16[1024,512]{1,0:T(8,128)(2,1)S(1)}) custom-call(s32[1]{0:T(128)} %bitcast.core_ref, bf16[384,512]{1,0:T(8,128)(2,1)S(1)} %copy-done.3, bf16[1024,512]{1,0:T(8,128)(2,1)S(1)} %get-tuple-element.40.lat_ref, bf16[32,16,512]{2,1,0:T(8,128)(2,1)} %collective-permute-done.5.core_lat_ref, ...), custom_call_target="tpu_custom_call" | custom-call | flops 402653184 | bytes 4325380 | tf_op jit(solution)/shard_map/pallas_call | solution.py:279
  74.1 0.7 shard_map.112.done_ref
  74.8 7.4 %collective-permute-done.7.far_ref = bf16[384,512]{1,0:T(8,128)(2,1)} collective-permute-done((bf16[384,512]{1,0:T(8,128)(2,1)}, bf16[384,512]{1,0:T(8,128)(2,1)}, u32[]{:S(2)}, u32[]{:S(2)}) %collective-permute-start.7) | collective-permute-done | bytes 393248 | tf_op jit(solution)/shard_map/ppermute | solution.py:405
  82.1 0.8 copy-done.4
  82.9 3.0 %shard_map.113 = f32[384,1024]{1,0:T(8,128)} custom-call(bf16[384,1024]{1,0:T(8,128)(2,1)S(1)} %get-tuple-element.41.part_ref, bf16[384,512]{1,0:T(8,128)(2,1)} %collective-permute-done.7.far_ref, bf16[1024,512]{1,0:T(8,128)(2,1)S(1)} %get-tuple-element.43.lat_ref, f32[16,512]{1,0:T(8,128)S(1)} %copy-done.4), custom_call_target="tpu_custom_call" | custom-call | tf_op jit(solution)/shard_map/pallas_call | solution.py:410
  (36 shorter events, 0.1 us)
Async XLA Ops:
  0.6 0.7 copy-start.5
  1.3 22.4 %copy-start = (bf16[3,256,1024]{2,1,0:T(8,128)(2,1)S(1)}, bf16[3,256,1024]{2,1,0:T(8,128)(2,1)}, u32[]{:S(2)}) copy-start(bf16[3,256,1024]{2,1,0:T(8,128)(2,1)} %own_ref.3) | copy-start | bytes 4718596
  1.4 22.4 %copy-start.11 = (s32[3,512]{1,0:T(4,128)S(1)}, s32[3,512]{1,0:T(4,128)}, u32[]{:S(2)}) copy-start(s32[3,512]{1,0:T(4,128)} %tri_ref.1) | copy-start | bytes 18436
  1.4 22.4 %copy-start.12 = (f32[3,512]{1,0:T(4,128)S(1)}, f32[3,512]{1,0:T(4,128)}, u32[]{:S(2)}) copy-start(f32[3,512]{1,0:T(4,128)} %sq_ref.1) | copy-start | bytes 18436
  1.4 22.4 %copy-start.13 = (s32[4,384]{1,0:T(4,128)S(1)}, s32[4,384]{1,0:T(4,128)}, u32[]{:S(2)}) copy-start(s32[4,384]{1,0:T(4,128)} %hin_ref.1) | copy-start | bytes 18436
  2.2 19.1 %all-to-all-start = ((bf16[32,16,512]{2,1,0:T(8,128)(2,1)}), bf16[32,16,512]{2,1,0:T(8,128)(2,1)}, u32[]{:S(2)}, u32[]{:S(2)}) async-start(bf16[32,16,512]{2,1,0:T(8,128)(2,1)} %shard_map.104), calls=%async_computation | async-start | bytes 1048576 | tf_op jit(solution)/shard_map/all_to_all | solution.py:348
  14.6 14.5 %collective-permute-start.1 = (bf16[400,1024]{1,0:T(8,128)(2,1)}, bf16[400,1024]{1,0:T(8,128)(2,1)S(1)}, u32[]{:S(2)}, u32[]{:S(2)}) collective-permute-start(bf16[400,1024]{1,0:T(8,128)(2,1)} %get-tuple-element.24), channel_id=1, source_target_pairs={{0,2},{2,4},{4,6},{6,8},{8,10},{10,12},{12,14},{14,16},{16,18},{18... | collective-permute-start | bytes 2457608 | tf_op jit(solution)/shard_map/ppermute | solution.py:351
  17.0 12.3 %collective-permute-start.2 = (bf16[400,1024]{1,0:T(8,128)(2,1)}, bf16[400,1024]{1,0:T(8,128)(2,1)S(1)}, u32[]{:S(2)}, u32[]{:S(2)}) collective-permute-start(bf16[400,1024]{1,0:T(8,128)(2,1)} %get-tuple-element.25), channel_id=1, source_target_pairs={{2,0},{4,2},{6,4},{8,6},{10,8},{12,10},{14,12},{16,14},{18,16},{20... | collective-permute-start | bytes 2457608 | tf_op jit(solution)/shard_map/ppermute | solution.py:352
  21.3 9.8 %collective-permute-start = (bf16[32,16,512]{2,1,0:T(8,128)(2,1)}, bf16[32,16,512]{2,1,0:T(8,128)(2,1)}, u32[]{:S(2)}, u32[]{:S(2)}) collective-permute-start(bf16[32,16,512]{2,1,0:T(8,128)(2,1)} %all-to-all-done.mine_ref), channel_id=1, source_target_pairs={{0,2},{2,0},{4,6},{6,4},{8,10},{10,8},{12,14},{14,12},{16,18},{18,... | collective-permute-start | bytes 1572872 | tf_op jit(solution)/shard_map/ppermute | solution.py:373
  23.8 5.4 %copy-start.6 = (f32[3,256]{1,0:T(4,128)S(1)}, f32[3,256]{1,0:T(4,128)}, u32[]{:S(2)}) copy-start(f32[3,256]{1,0:T(4,128)} %rest_ref.1) | copy-start | bytes 9220
  23.8 5.4 %copy-start.14 = (f32[3,384]{1,0:T(4,128)S(1)}, f32[3,384]{1,0:T(4,128)}, u32[]{:S(2)}) copy-start(f32[3,384]{1,0:T(4,128)} %bend_ref.1) | copy-start | bytes 13828
  23.8 5.4 %copy-start.15 = (f32[256]{0:T(256)S(1)}, f32[256]{0:T(256)}, u32[]{:S(2)}) copy-start(f32[256]{0:T(256)} %param.16) | copy-start | bytes 3076
  25.6 25.4 %collective-permute-start.5 = (bf16[32,16,512]{2,1,0:T(8,128)(2,1)}, bf16[32,16,512]{2,1,0:T(8,128)(2,1)}, u32[]{:S(2)}, u32[]{:S(2)}) collective-permute-start(bf16[32,16,512]{2,1,0:T(8,128)(2,1)} %all-to-all-done.mine_ref), channel_id=1, source_target_pairs={{0,1},{1,0},{2,3},{3,2},{4,5},{5,4},{6,7},{7,6},{8,9},{9,8},{10,11... | collective-permute-start | bytes 1572872 | tf_op jit(solution)/shard_map/ppermute | solution.py:397
  29.1 2.0 %copy-start.7 = (bf16[400,1024]{1,0:T(8,128)(2,1)}, bf16[400,1024]{1,0:T(8,128)(2,1)S(1)}, u32[]{:S(2)}) copy-start(bf16[400,1024]{1,0:T(8,128)(2,1)S(1)} %collective-permute-done.1.prv_ref) | copy-start | bytes 2457604
  29.2 1.9 %copy-start.9 = (bf16[400,1024]{1,0:T(8,128)(2,1)}, bf16[400,1024]{1,0:T(8,128)(2,1)S(1)}, u32[]{:S(2)}) copy-start(bf16[400,1024]{1,0:T(8,128)(2,1)S(1)} %collective-permute-done.2.nxt_ref) | copy-start | bytes 2457604
  31.1 1.1 %copy-start.8 = (bf16[400,1024]{1,0:T(8,128)(2,1)S(1)}, bf16[400,1024]{1,0:T(8,128)(2,1)}, u32[]{:S(2)}) copy-start(bf16[400,1024]{1,0:T(8,128)(2,1)} %copy-done.7) | copy-start | bytes 2457604
  32.3 1.1 %copy-start.10 = (bf16[400,1024]{1,0:T(8,128)(2,1)S(1)}, bf16[400,1024]{1,0:T(8,128)(2,1)}, u32[]{:S(2)}) copy-start(bf16[400,1024]{1,0:T(8,128)(2,1)} %copy-done.9) | copy-start | bytes 2457604
  45.4 1.1 %copy-start.16 = (f32[768,512]{1,0:T(8,128)}, f32[768,512]{1,0:T(8,128)S(1)}, u32[]{:S(2)}) copy-start(f32[768,512]{1,0:T(8,128)S(1)} %get-tuple-element.36.refs_2_) | copy-start | bytes 4718596
  46.5 10.0 %collective-permute-start.8 = (bf16[32,16,512]{2,1,0:T(8,128)(2,1)}, bf16[32,16,512]{2,1,0:T(8,128)(2,1)S(1)}, u32[]{:S(2)}, u32[]{:S(2)}) collective-permute-start(bf16[32,16,512]{2,1,0:T(8,128)(2,1)} %get-tuple-element.45), channel_id=1, source_target_pairs={{0,2},{2,0},{4,6},{6,4},{8,10},{10,8},{12,14},{14,12},{16,18},{18,... | collective-permute-start | bytes 1572872 | tf_op jit(solution)/shard_map/ppermute | solution.py:392
  50.5 10.8 %collective-permute-start.3 = (bf16[384,512]{1,0:T(8,128)(2,1)}, bf16[384,512]{1,0:T(8,128)(2,1)S(1)}, u32[]{:S(2)}, u32[]{:S(2)}) collective-permute-start(bf16[384,512]{1,0:T(8,128)(2,1)} %get-tuple-element.37), channel_id=1, source_target_pairs={{0,2},{2,4},{4,6},{6,8},{8,10},{10,12},{12,14},{14,16},{16,18},{18... | collective-permute-start | bytes 1179656 | tf_op jit(solution)/shard_map/ppermute | solution.py:390
  50.5 10.8 %collective-permute-start.4 = (bf16[384,512]{1,0:T(8,128)(2,1)S(1)}, bf16[384,512]{1,0:T(8,128)(2,1)}, u32[]{:S(2)}, u32[]{:S(2)}) collective-permute-start(bf16[384,512]{1,0:T(8,128)(2,1)S(1)} %get-tuple-element.38), channel_id=1, source_target_pairs={{2,0},{4,2},{6,4},{8,6},{10,8},{12,10},{14,12},{16,14},{18,16},{20... | collective-permute-start | bytes 1179656 | tf_op jit(solution)/shard_map/ppermute | solution.py:389
  51.0 18.5 %collective-permute-start.6 = (bf16[32,16,512]{2,1,0:T(8,128)(2,1)}, bf16[32,16,512]{2,1,0:T(8,128)(2,1)S(1)}, u32[]{:S(2)}, u32[]{:S(2)}) collective-permute-start(bf16[32,16,512]{2,1,0:T(8,128)(2,1)} %collective-permute-done.5.core_lat_ref), channel_id=1, source_target_pairs={{0,2},{2,0},{4,6},{6,4},{8,10},{10,8},{12,14},{14,12},{16,18},{18,... | collective-permute-start | bytes 1572872 | tf_op jit(solution)/shard_map/ppermute | solution.py:398
  57.4 16.7 %all-to-all-start.1 = ((bf16[32,16,512]{2,1,0:T(8,128)(2,1)}), bf16[32,16,512]{2,1,0:T(8,128)(2,1)S(1)}, u32[]{:S(2)}, u32[]{:S(2)}) async-start(bf16[32,16,512]{2,1,0:T(8,128)(2,1)} %shard_map.111), calls=%async_computation.1 | async-start | bytes 1048576 | tf_op jit(solution)/shard_map/all_to_all | solution.py:394
  61.3 0.8 copy-start.17
  66.1 16.0 %collective-permute-start.7 = (bf16[384,512]{1,0:T(8,128)(2,1)}, bf16[384,512]{1,0:T(8,128)(2,1)}, u32[]{:S(2)}, u32[]{:S(2)}) collective-permute-start(bf16[384,512]{1,0:T(8,128)(2,1)} %get-tuple-element.42), channel_id=1, source_target_pairs={{0,1},{1,0},{2,3},{3,2},{4,5},{5,4},{6,7},{7,6},{8,9},{9,8},{10,11... | collective-permute-start | bytes 1179656 | tf_op jit(solution)/shard_map/ppermute | solution.py:405
  69.5 0.8 copy-start.1
  70.3 1.0 %copy-start.2 = (bf16[32,16,512]{2,1,0:T(8,128)(2,1)S(1)}, bf16[32,16,512]{2,1,0:T(8,128)(2,1)}, u32[]{:S(2)}) copy-start(bf16[32,16,512]{2,1,0:T(8,128)(2,1)} %copy-done.1) | copy-start | bytes 1572868
  71.3 1.0 %copy-start.3 = (bf16[384,512]{1,0:T(8,128)(2,1)S(1)}, bf16[384,512]{1,0:T(8,128)(2,1)}, u32[]{:S(2)}) copy-start(bf16[384,512]{1,0:T(8,128)(2,1)} %get-tuple-element.39.mine_ref) | copy-start | bytes 1179652
  82.1 0.8 copy-start.4
